TPU v7x, 256 devices: a whole 4x4x8 slice. The times are simulated.
256 devices in a mesh: branch: 4 (over y_lo, core), seq: 64 (over x, y_hi, z).
Axes of the slice: x: 4, y: 4 (y_hi: 2, y_lo: 2; y = y_hi * 2 + y_lo), z: 8, core: 2. Of those that a mesh axis runs over, the one named last changes fastest.
Arguments:
- ctrl_q: bfloat16 [4, 4096, 2048], P('branch', 'seq'), may hold values from -128 to 128
- ctrl_k: bfloat16 [4, 4096, 2048], P('branch', 'seq'), may hold values from -128 to 128
- ctrl_v: bfloat16 [4, 4096, 2048], P('branch', 'seq'), may hold values from -96 to 96
- joining_codes: int32 [4, 4096], P('branch', 'seq'), may hold values from 0 to 32
- base_q: bfloat16 [4096, 2048], P('seq', 'branch'), may hold values from -128 to 128
- base_k: bfloat16 [4096, 2048], P('seq', 'branch'), may hold values from -128 to 128
- base_v: bfloat16 [4096, 2048], P('seq', 'branch'), may hold values from -48 to 48
Outputs:
- joined: float32 [4096, 2048], P('seq', 'branch')
- base_out: bfloat16 [4096, 2048], P('seq', 'branch')
All inputs are finite; a program needn't handle non-finite values.
Results may differ from a plain program's by a relative error of at most 0.013.
Values may be sent and summed in bfloat16 or wider, within the bound.
No kernel may reach another device: no remote copies, remote signals or barrier semaphores. Data moves between devices by JAX's collectives and lax.ppermute only.
A program may use at most 128 MiB of HBM per device.

v0:
```python
import jax
import jax.numpy as jnp
from jax import lax
from jax.sharding import PartitionSpec as P

HEADS = 16
HEAD_DIM = 128


def split_heads(matrix, heads):
    return matrix.reshape(matrix.shape[0], heads, matrix.shape[1] // heads)


def merge_heads(attended):
    heads, rows, depth = attended.shape
    return jnp.transpose(attended, (1, 0, 2)).reshape(rows, heads * depth)


def empty_carry(heads, rows, depth):
    return (
        jnp.full((heads, rows), -1e30, jnp.float32),
        jnp.zeros((heads, rows), jnp.float32),
        jnp.zeros((heads, rows, depth), jnp.float32),
    )


def fold_pairs(carry, query_heads, key_part, value_part):
    best, total, accum = carry
    heads = query_heads.shape[1]
    scale = query_heads.shape[2] ** (-0.5)
    scores = (
        jnp.einsum(
            "qhd,khd->hqk",
            query_heads,
            split_heads(key_part, heads),
            preferred_element_type=jnp.float32,
        )
        * scale
    )
    new_best = jnp.maximum(best, jnp.max(scores, axis=-1))
    expo = jnp.exp(scores - new_best[..., None])
    total = jnp.sum(expo, axis=-1)
    accum = jnp.einsum(
        "hqk,khd->hqd",
        expo.astype(jnp.bfloat16),
        split_heads(value_part, heads),
        preferred_element_type=jnp.float32,
    )
    return (new_best, total, accum)


def shards(ctrl_q, ctrl_k, ctrl_v, joining_codes, base_q, base_k, base_v):
    rows = ctrl_q.shape[1]
    local_heads = HEADS // lax.axis_size("branch")
    control_queries = split_heads(ctrl_q[0], HEADS)
    piece = (
        lax.all_gather(ctrl_k[0], "seq", axis=0, tiled=True),
        lax.all_gather(ctrl_v[0], "seq", axis=0, tiled=True),
    )
    control_best, control_total, control_accum = fold_pairs(
        empty_carry(HEADS, rows, HEAD_DIM), control_queries, piece[0], piece[1]
    )
    residual = merge_heads(control_accum / control_total[..., None])
    factors = joining_codes[0].astype(jnp.float32) / 16.0
    joined = lax.psum_scatter(
        (residual * factors[:, None]).astype(jnp.bfloat16),
        "branch",
        scatter_dimension=1,
        tiled=True,
    ).astype(jnp.float32)
    base_values = (base_v.astype(jnp.float32) + joined).astype(jnp.bfloat16)
    base_queries = split_heads(base_q, local_heads)
    piece = (
        lax.all_gather(base_k, "seq", axis=0, tiled=True),
        lax.all_gather(base_values, "seq", axis=0, tiled=True),
    )
    base_best, base_total, base_accum = fold_pairs(
        empty_carry(local_heads, rows, HEAD_DIM), base_queries, piece[0], piece[1]
    )
    base_out = merge_heads(base_accum / base_total[..., None]).astype(jnp.bfloat16)
    return (joined, base_out)


def solution(mesh):
    placed = (
        P("branch", "seq", None),
        P("branch", "seq", None),
        P("branch", "seq", None),
        P("branch", "seq"),
        P("seq", "branch"),
        P("seq", "branch"),
        P("seq", "branch"),
    )
    return jax.shard_map(
        shards,
        mesh=mesh,
        in_specs=placed,
        out_specs=(P("seq", "branch"), P("seq", "branch")),
        check_vma=False,
    )
```

profile of v0, /device:TPU:8, one launch (start us, length us, event | category | flops | bytes accessed | tf_op | source)
XLA Modules:
  0.0 746.2 jit_solution(8411828762147623653)
XLA Ops:
  7.2 0.0 copy-start
  7.2 0.0 all-gather.11.cloned.1.call-start
  7.2 0.7 all-gather.11.cloned.1.call-update
  7.9 0.0 all-gather.13.cloned.1.call-start
  8.0 0.7 all-gather.13.cloned.1.call-update
  8.7 0.0 reduce-scatter.2.cloned.1.call-start
  8.7 1.0 copy.42
  9.7 0.7 multiply_bitcast_fusion
  10.4 202.8 %all-gather.11.cloned.1.call-done = bf16[1,4096,2048]{2,1,0:T(8,128)(2,1)} async-done(((bf16[1,64,2048]{2,1,0:T(8,128)(2,1)}), bf16[1,4096,2048]{2,1,0:T(8,128)(2,1)}) %all-gather.11.cloned.1.call-update) | async-done | bytes 16777232 | tf_op jit(solution)/shard_map/all_gather | solution.py:57
  213.2 21.0 %copy.23 = bf16[1,4096,2048]{1,2,0:T(8,128)(2,1)} copy(bf16[1,4096,2048]{2,1,0:T(8,128)(2,1)} %all-gather.11.cloned.1.call-done) | data formatting | bytes 33554432 | tf_op jit(solution)/shard_map/all_gather | solution.py:57
  234.2 14.6 %multiply_reduce_fusion = (f32[16,64]{1,0:T(8,128)S(1)}, f32[16,64,4096]{2,1,0:T(8,128)}) fusion(bf16[4096,16,128]{0,2,1:T(8,128)(2,1)} %bitcast.50, bf16[64,16,128]{2,1,0:T(8,128)(2,1)S(1)} %bitcast.53), kind=kOutput, calls=%fused_computation.1 | convolution fusion | flops 1082129408 | bytes 33820672 | tf_op jit(solution)/shard_map/qhd,khd->hqk/dot_general | solution.py:32
  248.8 8.7 %fusion = f32[16,64]{1,0:T(8,128)S(1)} fusion(f32[16,64,4096]{2,1,0:T(8,128)} %get-tuple-element.5, f32[16,64]{1,0:T(8,128)S(1)} %broadcast_maximum_fusion), kind=kLoop, calls=%fused_computation.2 | loop fusion | flops 12581888 | bytes 16785408 | tf_op jit(solution)/shard_map/reduce_sum | solution.py:42
  257.4 155.7 %all-gather.13.cloned.1.call-done = bf16[1,4096,2048]{2,1,0:T(8,128)(2,1)} async-done(((bf16[1,64,2048]{2,1,0:T(8,128)(2,1)}), bf16[1,4096,2048]{2,1,0:T(8,128)(2,1)}) %all-gather.13.cloned.1.call-update) | async-done | bytes 16777232 | tf_op jit(solution)/shard_map/all_gather | solution.py:58
  413.1 20.9 %copy.26 = bf16[1,4096,2048]{1,2,0:T(8,128)(2,1)} copy(bf16[1,4096,2048]{2,1,0:T(8,128)(2,1)} %all-gather.13.cloned.1.call-done) | data formatting | bytes 33554432 | tf_op jit(solution)/shard_map/all_gather | solution.py:58
  434.1 0.0 copy-start.2
  434.1 13.7 %fusion.29 = f32[16,8,8,128]{3,2,1,0:T(8,128)S(1)} fusion(bf16[4096,16,128]{0,2,1:T(8,128)(2,1)} %bitcast.49, f32[16,64,4096]{2,1,0:T(8,128)} %get-tuple-element.5, f32[16,64]{1,0:T(8,128)S(1)} %broadcast_maximum_fusion, f32[64,16]{0,1:T(8,128)S(1)} %bitcast.55), kind=kOutput, calls=%fused_computation.19 | convolution fusion | flops 1086455808 | bytes 34086912 | tf_op jit(solution)/shard_map/hqk,khd->hqd/dot_general | solution.py:43
  447.7 0.8 fusion.32
  448.5 0.0 reduce-scatter.2.cloned.1.call-update
  448.6 0.0 all-gather.7.cloned.1.call-start
  448.6 0.5 all-gather.7.cloned.1.call-update
  449.1 0.2 all-gather.9.cloned.1.call-start
  449.4 15.4 %reduce-scatter.2.cloned.1.call-done = bf16[64,512]{1,0:T(8,128)(2,1)} async-done(((bf16[64,2048]{1,0:T(8,128)(2,1)}), bf16[64,512]{1,0:T(8,128)(2,1)}) %reduce-scatter.2.cloned.1.call-update) | async-done | bytes 65552 | tf_op jit(solution)/shard_map/reduce_scatter | solution.py:65
  464.8 0.0 copy-done.2
  464.8 1.5 add_convert_fusion
  466.3 0.0 all-gather.9.cloned.1.call-update
  466.3 132.1 %all-gather.7.cloned.1.call-done = bf16[4096,512]{1,0:T(8,128)(2,1)} async-done(((bf16[64,512]{1,0:T(8,128)(2,1)}), bf16[4096,512]{1,0:T(8,128)(2,1)}) %all-gather.7.cloned.1.call-update) | async-done | bytes 4194320 | tf_op jit(solution)/shard_map/all_gather | solution.py:74
  598.4 6.4 copy.29
  604.8 0.0 copy-done
  604.8 3.1 fusion.38
  607.9 0.0 copy-start.1
  607.9 2.0 copy-done.1
  609.9 0.7 fusion.6
  610.6 116.9 %all-gather.9.cloned.1.call-done = bf16[4096,512]{1,0:T(8,128)(2,1)} async-done(((bf16[64,512]{1,0:T(8,128)(2,1)}), bf16[4096,512]{1,0:T(8,128)(2,1)}) %all-gather.9.cloned.1.call-update) | async-done | bytes 4194320 | tf_op jit(solution)/shard_map/all_gather | solution.py:75
  727.4 6.5 copy.32
  733.9 5.1 fusion.23
  739.0 0.6 copy.55
  (2 shorter events, 0.0 us)
Async XLA Ops:
  7.2 597.6 %copy-start = (bf16[64,512]{1,0:T(8,128)(2,1)S(1)}, bf16[64,512]{1,0:T(8,128)(2,1)}, u32[]{:S(2)}) copy-start(bf16[64,512]{1,0:T(8,128)(2,1)} %param.11) | copy-start | bytes 196612
  7.2 206.0 %all-gather.11.cloned.1.call-start = ((), (), s32[]{:S(2)}) async-start(), calls=%async_computation.4 | async-start | bytes 17039360 | tf_op jit(solution)/shard_map/all_gather | solution.py:57
  7.9 405.2 %all-gather.13.cloned.1.call-start = ((), (), s32[]{:S(2)}) async-start(), calls=%async_computation.5 | async-start | bytes 17039360 | tf_op jit(solution)/shard_map/all_gather | solution.py:58
  8.7 456.1 %reduce-scatter.2.cloned.1.call-start = ((), (), s32[]{:S(2)}) async-start(), calls=%async_computation.1 | async-start | bytes 327680 | tf_op jit(solution)/shard_map/reduce_scatter | solution.py:65
  434.1 30.7 %copy-start.2 = (bf16[64,512]{1,0:T(8,128)(2,1)S(1)}, bf16[64,512]{1,0:T(8,128)(2,1)}, u32[]{:S(2)}) copy-start(bf16[64,512]{1,0:T(8,128)(2,1)} %param.13) | copy-start | bytes 196612
  448.6 149.8 %all-gather.7.cloned.1.call-start = ((), (), s32[]{:S(2)}) async-start(), calls=%async_computation.2 | async-start | bytes 4259840 | tf_op jit(solution)/shard_map/all_gather | solution.py:74
  449.1 278.3 %all-gather.9.cloned.1.call-start = ((), (), s32[]{:S(2)}) async-start(), calls=%async_computation.3 | async-start | bytes 4259840 | tf_op jit(solution)/shard_map/all_gather | solution.py:75
  607.9 2.0 copy-start.1
Sparse Core Ops, SparseCore 0:
  11.7 201.4 all-gather.10
  216.8 196.2 all-gather.12
  448.7 16.0 reduce-scatter.1
  468.8 129.4 all-gather.6
  603.0 124.3 all-gather.8
where the time goes:
time: 749 us; the launch traced here: 746 us
  waiting for transfers between devices  625 us (83%)
  local copies, waits for them, and re-layouts  58.4 us (8%)
  matrix products  36.5 us (5%)
  between operations  13.8 us (2%)
  other arithmetic  12.4 us (2%)
    all_gather x1, waiting for transfers between devices, shards(): lax.all_gather(ctrl_k[0], 'seq', axis=0, tiled=True)  203 us
    all_gather x1, waiting for transfers between devices, shards(): lax.all_gather(ctrl_v[0], 'seq', axis=0, tiled=True)  156 us
    all_gather x1, waiting for transfers between devices, shards(): lax.all_gather(base_k, 'seq', axis=0, tiled=True)  132 us
    all_gather x1, waiting for transfers between devices, shards(): lax.all_gather(base_values, 'seq', axis=0, tiled=True)  117 us
    all_gather x1, local copies, waits for them, and re-layouts, shards(): lax.all_gather(ctrl_k[0], 'seq', axis=0, tiled=True)  21 us
    all_gather x1, local copies, waits for them, and re-layouts, shards(): lax.all_gather(ctrl_v[0], 'seq', axis=0, tiled=True)  20.9 us
    dot_general x2, matrix products, fold_pairs(): jnp.einsum('hqk,khd->hqd', expo.astype(jnp.bfloat16), split_heads(value_p...  18.8 us
    dot_general x2, matrix products, fold_pairs(): jnp.einsum('qhd,khd->hqk', query_heads, split_heads(key_part, heads), pre...  17.7 us
  transfers between devices with their start and end apart: 5, of which 5 were waited for; matrix products, arithmetic and copies ran while one was open for 8% of the time, Pallas kernels for 0%

commit v1 on v0

v1 whole, which is shorter than its diff:
```python
import functools

import jax
import jax.numpy as jnp
from jax import lax
from jax.experimental import pallas as pl
from jax.experimental.pallas import tpu as pltpu
from jax.sharding import Mesh, PartitionSpec as P

HEADS = 16
DIM = 128
SCALE2 = DIM ** -0.5 * 1.4426950408889634
BF, F32 = jnp.bfloat16, jnp.float32
MIB = 1 << 20
VM = pl.BlockSpec(memory_space=pltpu.VMEM)
SM = pl.BlockSpec(memory_space=pltpu.SMEM)


def call(body, outs, operands, specs=None, vmem=16, flops=0, scratch=()):
    moved = sum(o.size * o.dtype.itemsize for o in [*operands, *outs])
    return pl.pallas_call(
        body,
        out_shape=outs,
        in_specs=specs or [VM] * len(operands),
        out_specs=[VM] * len(outs),
        scratch_shapes=list(scratch),
        compiler_params=pltpu.CompilerParams(vmem_limit_bytes=vmem * MIB),
        cost_estimate=pl.CostEstimate(flops=flops, bytes_accessed=moved, transcendentals=0),
    )(*operands)


def sds(shape, dtype=BF):
    return jax.ShapeDtypeStruct(shape, dtype)


def dot_nt(a, b):
    return lax.dot_general(a, b, (((1,), (1,)), ((), ())), preferred_element_type=F32)


def dot_nn(a, b):
    return lax.dot_general(a, b, (((1,), (0,)), ((), ())), preferred_element_type=F32)


def pack_kernel(k_ref, v_ref, q_ref, code_ref, out_ref):
    row = code_ref[...].astype(F32)
    row = jnp.concatenate([row, jnp.zeros((1, 64), F32)], axis=1)
    rows = jnp.broadcast_to(row, (16, 128)).astype(BF)
    for h in range(HEADS):
        cols = slice(h * DIM, (h + 1) * DIM)
        out_ref[h, 0:64] = k_ref[:, cols]
        out_ref[h, 64:128] = v_ref[:, cols]
        out_ref[h, 128:192] = q_ref[:, cols]
        out_ref[h, 192:208] = rows


def unpack_kernel(in_ref, k_ref, v_ref, q_ref, factor_ref):
    lane = lax.broadcasted_iota(jnp.int32, (64, 128), 1)
    sub = lax.broadcasted_iota(jnp.int32, (64, 128), 0)
    for t in range(16):
        rows = slice(t * 64, (t + 1) * 64)
        k_ref[rows] = in_ref[t, 0:64]
        v_ref[rows] = in_ref[t, 64:128]
        q_ref[rows] = in_ref[t, 128:192]
        code = in_ref[t, 192:208].astype(F32)[0:1]
        code = jnp.broadcast_to(code, (64, 128))
        col = jnp.sum(jnp.where(lane == sub, code, 0.0), axis=1, keepdims=True)
        factor_ref[rows] = col / 16.0


def score_kernel(q_ref, k_ref, p_ref, m_ref, l_ref):
    for i in range(4):
        rows = slice(i * 256, (i + 1) * 256)
        s = dot_nt(q_ref[rows], k_ref[...])
        m = jnp.max(s, axis=1, keepdims=True)
        p = jnp.exp2((s - m) * SCALE2)
        m_ref[rows] = m
        l_ref[rows] = jnp.sum(p, axis=1, keepdims=True)
        p_ref[rows] = p.astype(BF)


def value_kernel(p_ref, v_ref, acc_ref):
    for i in range(4):
        rows = slice(i * 256, (i + 1) * 256)
        acc_ref[rows] = dot_nn(p_ref[rows], v_ref[...])


def finish_kernel(b_ref, factor_ref, *refs):
    ms, ls, (acc0, p1, v1, p2, v2, p3, v3), outs = refs[0:4], refs[4:8], refs[8:15], refs[15:]
    b = b_ref[0]
    for i in (3, 2, 1, 0):
        rows = pl.ds(pl.multiple_of((b ^ i) * 256, 256), 256)
        m = [r[rows] for r in ms]
        best = jnp.maximum(jnp.maximum(m[0], m[1]), jnp.maximum(m[2], m[3]))
        w = [jnp.exp2((x - best) * SCALE2) for x in m]
        total = sum(w[c] * ls[c][rows] for c in range(4))
        acc = acc0[rows] * w[0]
        for c, (p, v) in ((1, (p1, v1)), (3, (p3, v3)), (2, (p2, v2))):
            acc = acc + dot_nn(p[rows], v[...]) * w[c]
        acc = acc / total * factor_ref[rows]
        outs[i][...] = acc.astype(outs[i].dtype)


def base_score_kernel(at_ref, q_ref, k_ref, p_ref, l_ref):
    yl, co, x = at_ref[0], at_ref[1], at_ref[2]
    blocks = []
    for cr in range(2):
        for xr in range(4):
            for yr in range(2):
                first = ((yl ^ yr) * 2 + (co ^ cr)) * 4 + ((x + 4 - xr) & 3)
                keys = k_ref[pl.ds(pl.multiple_of(first * 256, 256), 256)]
                blocks.append(dot_nt(q_ref[...], keys))
    best = functools.reduce(jnp.maximum, blocks)
    best = jnp.max(best, axis=1, keepdims=True)
    total = None
    for n, s in enumerate(blocks):
        p = jnp.exp2((s - best) * SCALE2)
        p_ref[n // 2, :, (n % 2) * 256 : (n % 2 + 1) * 256] = p.astype(BF)
        total = p if total is None else total + p
    l_ref[...] = jnp.sum(total, axis=1, keepdims=True)


def base_value_kernel(p_ref, l_ref, joined_ref, *refs):
    acc = None
    for n, v in enumerate(refs[:-1]):
        part = dot_nn(p_ref[n], v[...])
        acc = part if acc is None else acc + part
    out = (acc / l_ref[...]).astype(BF)
    joined = joined_ref[...].astype(BF)
    for t in range(4):
        rows = slice(t * 64, (t + 1) * 64)
        refs[-1][t, 0:64] = joined[rows]
        refs[-1][t, 64:128] = out[rows]


def home_kernel(in_ref, joined_ref, out_ref):
    for i in range(4):
        cols = slice(i * DIM, (i + 1) * DIM)
        joined_ref[:, cols] = in_ref[i, 0:64].astype(F32)
        out_ref[:, cols] = in_ref[i, 64:128]


def base_pack_kernel(k_ref, v_ref, q_ref, out_ref):
    for i in range(4):
        cols = slice(i * DIM, (i + 1) * DIM)
        out_ref[i, 0:64] = k_ref[:, cols]
        out_ref[i, 64:128] = v_ref[:, cols]
        out_ref[i, 128:192] = q_ref[:, cols]


def swap(values):
    perm = [(b * 16 + c * 4 + z, c * 16 + b * 4 + z) for b in range(4) for c in range(4) for z in range(4)]
    return lax.ppermute(values, ("yl", "co", "yh", "zh", "zl"), perm)


def along_x(values, step):
    return lax.ppermute(values, "x", [(j, (j + step) % 4) for j in range(4)])


def other(values, axis):
    return lax.ppermute(values, axis, [(0, 1), (1, 0)])


def shards(ctrl_q, ctrl_k, ctrl_v, codes, base_q, base_k, base_v):
    at = jnp.stack([lax.axis_index("yl"), lax.axis_index("co"), lax.axis_index("x")]).astype(jnp.int32)
    branch = (at[0] * 2 + at[1]).reshape(1)

    (base,) = call(base_pack_kernel, [sds((4, 192, DIM))], [base_k, base_v, base_q])
    base = swap(lax.all_to_all(base, "zl", 0, 0, tiled=True))
    base_keys, base_vals, base_quer = (base[:, 64 * i : 64 * i + 64].reshape(256, DIM) for i in range(3))
    base_keys = lax.all_gather(base_keys, ("yl", "co", "x"), axis=0, tiled=True)

    (packed,) = call(pack_kernel, [sds((HEADS, 208, DIM))], [ctrl_k[0], ctrl_v[0], ctrl_q[0], codes])
    packed = lax.all_to_all(packed, ("yh", "zh", "zl"), 0, 0, tiled=True)
    own_k, own_v, quer, factor = call(
        unpack_kernel, [sds((1024, DIM))] * 3 + [sds((1024, 1), F32)], [packed]
    )
    keys, vals = [own_k] + [None] * 3, [own_v] + [None] * 3
    for step in (1, 3, 2):
        keys[step] = along_x(own_k, step)
    for step in (1, 3, 2):
        vals[step] = along_x(own_v, step)
    scored = [
        call(
            score_kernel,
            [sds((1024, 1024)), sds((1024, 1), F32), sds((1024, 1), F32)],
            [quer, k],
            vmem=24,
            flops=2 * 1024 * 1024 * 128,
        )
        for k in keys
    ]
    ps, ms, ls = zip(*scored)
    (acc0,) = call(value_kernel, [sds((1024, DIM), F32)], [ps[0], vals[0]], flops=2 * 1024 * 1024 * 128)
    operands = [branch, factor, *ms, *ls, acc0, ps[1], vals[1], ps[2], vals[2], ps[3], vals[3]]
    outs = call(
        finish_kernel,
        [sds((256, DIM), F32)] + [sds((256, DIM))] * 3,
        operands,
        specs=[SM] + [VM] * (len(operands) - 1),
        vmem=28,
        flops=3 * 2 * 1024 * 1024 * 128,
    )

    joined = outs[0]
    for k in (3, 2, 1):
        joined = joined + lax.ppermute(outs[k], ("yl", "co"), [(j, j ^ k) for j in range(4)]).astype(F32)
    base_values = (base_vals.astype(F32) + joined).astype(BF)

    base_p, base_l = call(
        base_score_kernel,
        [sds((8, 256, 512)), sds((256, 1), F32)],
        [at, base_quer, base_keys],
        specs=[SM, VM, VM],
        vmem=24,
        flops=2 * 256 * 4096 * 128,
    )
    pair = jnp.concatenate([base_values, other(base_values, "yl")], axis=0)
    mine = [pair] + [None] * 3
    for step in (1, 3, 2):
        mine[step] = along_x(pair, step)
    theirs = [other(v, "co") for v in mine]
    (result,) = call(
        base_value_kernel, [sds((4, 128, DIM))], [base_p, base_l, joined, *mine, *theirs], flops=2 * 256 * 4096 * 128
    )
    result = lax.all_to_all(swap(result), "zl", 0, 0, tiled=True)
    return call(home_kernel, [sds((64, 512), F32), sds((64, 512))], [result])


def solution(mesh):
    fine = Mesh(mesh.devices.reshape(2, 2, 4, 2, 2, 4), ("yl", "co", "x", "yh", "zh", "zl"))
    branch, seq = ("yl", "co"), ("x", "yh", "zh", "zl")
    return jax.shard_map(
        shards,
        mesh=fine,
        in_specs=(P(branch, seq, None),) * 3 + (P(branch, seq),) + (P(seq, branch),) * 3,
        out_specs=(P(seq, branch), P(seq, branch)),
        check_vma=False,
    )
```

time: 749 us -> 144 us (0.19)
  the two profiles are of different devices: /device:TPU:8 before, /device:TPU:19 now
where the time goes in v1:
time: 144 us
  starting transfers between devices  49.7 us (35%)
  waiting for transfers between devices  48.9 us (34%)
  between operations  14.1 us (10%)
  Pallas kernels  12.8 us (9%)
  blocking collectives  10.1 us (7%)
  local copies, waits for them, and re-layouts  7.88 us (5%)
    ppermute x2, waiting for transfers between devices, swap(): return lax.ppermute(values, ('yl', 'co', 'yh', 'zh', 'zl'), perm)  26.5 us
    ppermute x9, waiting for transfers between devices, along_x(): return lax.ppermute(values, 'x', [(j, (j + step) % 4) for j in range(4)])  14.1 us
    ppermute x2, starting transfers between devices, swap(): return lax.ppermute(values, ('yl', 'co', 'yh', 'zh', 'zl'), perm)  14 us
    pallas_call x12, Pallas kernels, call(): pl.pallas_call(body, out_shape=outs, in_specs=specs or [VM] * len(operand...  12.8 us
    all_to_all x1, blocking collectives, shards(): result = lax.all_to_all(swap(result), 'zl', 0, 0, tiled=True)  10.1 us
    ppermute x5, starting transfers between devices, other(): return lax.ppermute(values, axis, [(0, 1), (1, 0)])  9.54 us
    ppermute x9, starting transfers between devices, along_x(): return lax.ppermute(values, 'x', [(j, (j + step) % 4) for j in range(4)])  9.31 us
    all_to_all x1, starting transfers between devices, shards(): packed = lax.all_to_all(packed, ('yh', 'zh', 'zl'), 0, 0, tiled=True)  8.99 us
  transfers between devices with their start and end apart: 22, of which 12 were waited for; matrix products, arithmetic and copies ran while one was open for 1% of the time, Pallas kernels for 7%

profile of v1, /device:TPU:19, one launch (start us, length us, event | category | flops | bytes accessed | tf_op | source)
XLA Modules:
  0.0 143.5 jit_solution(16526149294497186268)
XLA Ops:
  7.2 0.8 copy-done.4
  8.0 0.8 copy-done.5
  8.8 0.8 copy-done.6
  9.7 0.7 shard_map.86
  10.4 5.6 %all-to-all-start = ((bf16[4,192,128]{2,1,0:T(8,128)(2,1)}), bf16[4,192,128]{2,1,0:T(8,128)(2,1)S(1)}, u32[]{:S(2)}, u32[]{:S(2)}) async-start(bf16[4,192,128]{2,1,0:T(8,128)(2,1)} %shard_map.86), calls=%async_computation | async-start | bytes 393216 | tf_op jit(solution)/shard_map/all_to_all | solution.py:168
  16.0 0.9 copy-done.1
  17.0 0.9 copy-done.2
  17.9 0.9 copy-done.3
  18.9 0.7 copy-done.7
  19.5 1.0 shard_map.88
  20.6 0.7 all-to-all-done
  21.2 9.0 %all-to-all-start.1 = ((bf16[16,208,128]{2,1,0:T(8,128)(2,1)}), bf16[16,208,128]{2,1,0:T(8,128)(2,1)S(1)}, u32[]{:S(2)}, u32[]{:S(2)}) async-start(bf16[16,208,128]{2,1,0:T(8,128)(2,1)} %shard_map.88), calls=%async_computation.1 | async-start | bytes 1703936 | tf_op jit(solution)/shard_map/all_to_all | solution.py:173
  30.2 9.5 %collective-permute-start = (bf16[4,192,128]{2,1,0:T(8,128)(2,1)S(1)}, bf16[4,192,128]{2,1,0:T(8,128)(2,1)S(1)}, u32[]{:S(2)}, u32[]{:S(2)}) collective-permute-start(bf16[4,192,128]{2,1,0:T(8,128)(2,1)S(1)} %all-to-all-done), channel_id=1, source_target_pairs={{0,0},{1,1},{2,2},{3,3},{4,64},{5,65},{6,66},{7,67},{8,128},{9,129... | collective-permute-start | bytes 589832 | tf_op jit(solution)/shard_map/ppermute | solution.py:152
  39.8 18.3 %collective-permute-done = bf16[4,192,128]{2,1,0:T(8,128)(2,1)S(1)} collective-permute-done((bf16[4,192,128]{2,1,0:T(8,128)(2,1)S(1)}, bf16[4,192,128]{2,1,0:T(8,128)(2,1)S(1)}, u32[]{:S(2)}, u32[]{:S(2)}) %collective-permute-start) | collective-permute-done | bytes 196640 | tf_op jit(solution)/shard_map/ppermute | solution.py:152
  59.1 1.3 collective-permute-start.1
  60.4 0.8 collective-permute-start.2
  61.2 1.9 %collective-permute-start.3 = (bf16[1024,128]{1,0:T(8,128)(2,1)S(1)}, bf16[1024,128]{1,0:T(8,128)(2,1)S(1)}, u32[]{:S(2)}, u32[]{:S(2)}) collective-permute-start(bf16[1024,128]{1,0:T(8,128)(2,1)S(1)} %get-tuple-element.28.k_ref), channel_id=1, source_target_pairs={{0,48},{16,0},{32,16},{48,32},{1,49},{17,1},{33,17},{49,33},{2,50}... | collective-permute-start | bytes 786440 | tf_op jit(solution)/shard_map/ppermute | solution.py:156
  63.1 2.9 %collective-permute-start.5 = (bf16[1024,128]{1,0:T(8,128)(2,1)S(1)}, bf16[1024,128]{1,0:T(8,128)(2,1)S(1)}, u32[]{:S(2)}, u32[]{:S(2)}) collective-permute-start(bf16[1024,128]{1,0:T(8,128)(2,1)S(1)} %get-tuple-element.38.v_ref), channel_id=1, source_target_pairs={{0,32},{16,48},{32,0},{48,16},{1,33},{17,49},{33,1},{49,17},{2,34}... | collective-permute-start | bytes 786440 | tf_op jit(solution)/shard_map/ppermute | solution.py:156
  66.0 5.1 %collective-permute-done.1.k_ref = bf16[1024,128]{1,0:T(8,128)(2,1)S(1)} collective-permute-done((bf16[1024,128]{1,0:T(8,128)(2,1)S(1)}, bf16[1024,128]{1,0:T(8,128)(2,1)S(1)}, u32[]{:S(2)}, u32[]{:S(2)}) %collective-permute-start.1) | collective-permute-done | bytes 262176 | tf_op jit(solution)/shard_map/ppermute | solution.py:156
  71.1 1.2 shard_map.90
  72.3 0.7 shard_map.94.refs_8_
  73.0 1.2 shard_map.91
  74.1 1.2 shard_map.92
  75.3 1.3 collective-permute-done.3.k_ref
  76.6 1.2 shard_map.93
  77.7 2.0 %collective-permute-done.4.refs_10_ = bf16[1024,128]{1,0:T(8,128)(2,1)S(1)} collective-permute-done((bf16[1024,128]{1,0:T(8,128)(2,1)S(1)}, bf16[1024,128]{1,0:T(8,128)(2,1)S(1)}, u32[]{:S(2)}, u32[]{:S(2)}) %collective-permute-start.4) | collective-permute-done | bytes 262176 | tf_op jit(solution)/shard_map/ppermute | solution.py:156
  79.7 3.1 %collective-permute-done.5.refs_12_ = bf16[1024,128]{1,0:T(8,128)(2,1)S(1)} collective-permute-done((bf16[1024,128]{1,0:T(8,128)(2,1)S(1)}, bf16[1024,128]{1,0:T(8,128)(2,1)S(1)}, u32[]{:S(2)}, u32[]{:S(2)}) %collective-permute-start.5) | collective-permute-done | bytes 262176 | tf_op jit(solution)/shard_map/ppermute | solution.py:156
  82.8 2.6 %collective-permute-done.6.refs_14_ = bf16[1024,128]{1,0:T(8,128)(2,1)S(1)} collective-permute-done((bf16[1024,128]{1,0:T(8,128)(2,1)S(1)}, bf16[1024,128]{1,0:T(8,128)(2,1)S(1)}, u32[]{:S(2)}, u32[]{:S(2)}) %collective-permute-start.6) | collective-permute-done | bytes 262176 | tf_op jit(solution)/shard_map/ppermute | solution.py:156
  85.5 2.0 %shard_map.95 = (f32[256,128]{1,0:T(8,128)S(1)}, bf16[256,128]{1,0:T(8,128)(2,1)S(1)}, bf16[256,128]{1,0:T(8,128)(2,1)S(1)}, bf16[256,128]{1,0:T(8,128)(2,1)S(1)}) custom-call(s32[1]{0:T(128)} %bitcast.5.b_ref, f32[1024,1]{1,0:T(8,128)S(1)} %get-tuple-element.26.factor_ref, f32[1024,1]{1,0:T(8,128)S(1)} %get-tuple-element.29.refs_0_, ...), custom_call_target="tpu_custom_call" | custom-call | flops 805306368 | bytes 7966724 | tf_op jit(solution)/shard_map/pallas_call | solution.py:21
  87.5 0.8 collective-permute-start.7
  88.8 0.9 collective-permute-start.9
  89.7 2.1 %collective-permute-done.7 = bf16[256,128]{1,0:T(8,128)(2,1)S(1)} collective-permute-done((bf16[256,128]{1,0:T(8,128)(2,1)S(1)}, bf16[256,128]{1,0:T(8,128)(2,1)S(1)}, u32[]{:S(2)}, u32[]{:S(2)}) %collective-permute-start.7) | collective-permute-done | bytes 65568 | tf_op jit(solution)/shard_map/ppermute | solution.py:206
  92.5 1.0 collective-permute-start.10
  93.5 2.5 %collective-permute-done.10 = bf16[256,128]{1,0:T(8,128)(2,1)S(1)} collective-permute-done((bf16[256,128]{1,0:T(8,128)(2,1)S(1)}, bf16[256,128]{1,0:T(8,128)(2,1)S(1)}, u32[]{:S(2)}, u32[]{:S(2)}) %collective-permute-start.10) | collective-permute-done | bytes 65568 | tf_op jit(solution)/shard_map/ppermute | solution.py:160
  96.5 0.8 collective-permute-start.12
  97.3 1.1 collective-permute-start.13
  98.4 3.0 %collective-permute-start.14 = (bf16[512,128]{1,0:T(8,128)(2,1)S(1)}, bf16[512,128]{1,0:T(8,128)(2,1)S(1)}, u32[]{:S(2)}, u32[]{:S(2)}) collective-permute-start(bf16[512,128]{1,0:T(8,128)(2,1)S(1)} %pad_maximum_fusion.refs_0_), channel_id=1, source_target_pairs={{0,64},{64,0},{1,65},{65,1},{2,66},{66,2},{3,67},{67,3},{4,68},{68... | collective-permute-start | bytes 393224 | tf_op jit(solution)/shard_map/ppermute | solution.py:160
  101.4 2.7 %collective-permute-start.15 = (bf16[512,128]{1,0:T(8,128)(2,1)S(1)}, bf16[512,128]{1,0:T(8,128)(2,1)S(1)}, u32[]{:S(2)}, u32[]{:S(2)}) collective-permute-start(bf16[512,128]{1,0:T(8,128)(2,1)S(1)} %collective-permute-done.11.refs_1_), channel_id=1, source_target_pairs={{0,64},{64,0},{1,65},{65,1},{2,66},{66,2},{3,67},{67,3},{4,68},{68... | collective-permute-start | bytes 393224 | tf_op jit(solution)/shard_map/ppermute | solution.py:160
  104.1 2.0 %collective-permute-start.16 = (bf16[512,128]{1,0:T(8,128)(2,1)S(1)}, bf16[512,128]{1,0:T(8,128)(2,1)S(1)}, u32[]{:S(2)}, u32[]{:S(2)}) collective-permute-start(bf16[512,128]{1,0:T(8,128)(2,1)S(1)} %collective-permute-done.12.refs_2_), channel_id=1, source_target_pairs={{0,64},{64,0},{1,65},{65,1},{2,66},{66,2},{3,67},{67,3},{4,68},{68... | collective-permute-start | bytes 393224 | tf_op jit(solution)/shard_map/ppermute | solution.py:160
  106.1 0.8 collective-permute-start.17
  107.0 2.4 %all-gather.2.cloned.1.call-done.k_ref = bf16[4096,128]{1,0:T(8,128)(2,1)} async-done(((bf16[256,128]{1,0:T(8,128)(2,1)}), bf16[4096,128]{1,0:T(8,128)(2,1)}) %all-gather.2.cloned.1.call-update) | async-done | bytes 1048592 | tf_op jit(solution)/shard_map/all_gather | solution.py:170
  109.4 1.2 copy-done
  110.6 1.9 %shard_map.87 = (bf16[8,256,512]{2,1,0:T(8,128)(2,1)S(1)}, f32[256,1]{1,0:T(8,128)S(1)}) custom-call(s32[3]{0:T(128)S(1)} %pad_add_fusion.at_ref, bf16[256,128]{1,0:T(8,128)(2,1)S(1)} %bitcast.12, bf16[4096,128]{1,0:T(8,128)(2,1)S(1)} %copy-done), custom_call_target="tpu_custom_call" | custom-call | flops 268435456 | bytes 3212300 | tf_op jit(solution)/shard_map/pallas_call | solution.py:21
  112.6 0.7 shard_map.96
  113.3 4.4 %collective-permute-start.18 = (bf16[4,128,128]{2,1,0:T(8,128)(2,1)S(1)}, bf16[4,128,128]{2,1,0:T(8,128)(2,1)S(1)}, u32[]{:S(2)}, u32[]{:S(2)}) collective-permute-start(bf16[4,128,128]{2,1,0:T(8,128)(2,1)S(1)} %shard_map.96), channel_id=1, source_target_pairs={{0,0},{1,1},{2,2},{3,3},{4,64},{5,65},{6,66},{7,67},{8,128},{9,129... | collective-permute-start | bytes 393224 | tf_op jit(solution)/shard_map/ppermute | solution.py:152
  117.7 8.2 %collective-permute-done.18 = bf16[4,128,128]{2,1,0:T(8,128)(2,1)S(1)} collective-permute-done((bf16[4,128,128]{2,1,0:T(8,128)(2,1)S(1)}, bf16[4,128,128]{2,1,0:T(8,128)(2,1)S(1)}, u32[]{:S(2)}, u32[]{:S(2)}) %collective-permute-start.18) | collective-permute-done | bytes 131104 | tf_op jit(solution)/shard_map/ppermute | solution.py:152
  125.9 10.1 %all_to_all.15.in_ref = bf16[4,128,128]{2,1,0:T(8,128)(2,1)S(1)} all-to-all(bf16[4,128,128]{2,1,0:T(8,128)(2,1)S(1)} %collective-permute-done.18), channel_id=1, replica_groups=mesh['yl'=2,'co'=2,'x'=4,'yh'=2,'zh'=2,'zl'=4] {'zl'}, dimensions={0} | all-to-all | bytes 262144 | tf_op jit(solution)/shard_map/all_to_all | solution.py:225
  136.0 0.7 shard_map.97
  (30 shorter events, 2.7 us)
Async XLA Ops:
  7.2 0.8 copy-start.4
  8.0 0.8 copy-start.5
  8.8 0.8 copy-start.6
  10.4 10.8 %all-to-all-start = ((bf16[4,192,128]{2,1,0:T(8,128)(2,1)}), bf16[4,192,128]{2,1,0:T(8,128)(2,1)S(1)}, u32[]{:S(2)}, u32[]{:S(2)}) async-start(bf16[4,192,128]{2,1,0:T(8,128)(2,1)} %shard_map.86), calls=%async_computation | async-start | bytes 393216 | tf_op jit(solution)/shard_map/all_to_all | solution.py:168
  16.0 0.9 copy-start.1
  17.0 0.9 copy-start.2
  17.9 0.9 copy-start.3
  18.9 0.7 copy-start.7
  21.2 37.6 %all-to-all-start.1 = ((bf16[16,208,128]{2,1,0:T(8,128)(2,1)}), bf16[16,208,128]{2,1,0:T(8,128)(2,1)S(1)}, u32[]{:S(2)}, u32[]{:S(2)}) async-start(bf16[16,208,128]{2,1,0:T(8,128)(2,1)} %shard_map.88), calls=%async_computation.1 | async-start | bytes 1703936 | tf_op jit(solution)/shard_map/all_to_all | solution.py:173
  30.2 79.2 %all-gather.2.cloned.1.call-start = ((), (), s32[]{:S(2)}) async-start(), calls=%async_computation.3 | async-start | bytes 1114112 | tf_op jit(solution)/shard_map/all_gather | solution.py:170
  30.2 27.9 %collective-permute-start = (bf16[4,192,128]{2,1,0:T(8,128)(2,1)S(1)}, bf16[4,192,128]{2,1,0:T(8,128)(2,1)S(1)}, u32[]{:S(2)}, u32[]{:S(2)}) collective-permute-start(bf16[4,192,128]{2,1,0:T(8,128)(2,1)S(1)} %all-to-all-done), channel_id=1, source_target_pairs={{0,0},{1,1},{2,2},{3,3},{4,64},{5,65},{6,66},{7,67},{8,128},{9,129... | collective-permute-start | bytes 589832 | tf_op jit(solution)/shard_map/ppermute | solution.py:152
  59.1 12.0 %collective-permute-start.1 = (bf16[1024,128]{1,0:T(8,128)(2,1)S(1)}, bf16[1024,128]{1,0:T(8,128)(2,1)S(1)}, u32[]{:S(2)}, u32[]{:S(2)}) collective-permute-start(bf16[1024,128]{1,0:T(8,128)(2,1)S(1)} %get-tuple-element.28.k_ref), channel_id=1, source_target_pairs={{0,16},{16,32},{32,48},{48,0},{1,17},{17,33},{33,49},{49,1},{2,18}... | collective-permute-start | bytes 786440 | tf_op jit(solution)/shard_map/ppermute | solution.py:156
  60.4 13.8 %collective-permute-start.2 = (bf16[1024,128]{1,0:T(8,128)(2,1)S(1)}, bf16[1024,128]{1,0:T(8,128)(2,1)S(1)}, u32[]{:S(2)}, u32[]{:S(2)}) collective-permute-start(bf16[1024,128]{1,0:T(8,128)(2,1)S(1)} %get-tuple-element.28.k_ref), channel_id=1, source_target_pairs={{0,32},{16,48},{32,0},{48,16},{1,33},{17,49},{33,1},{49,17},{2,34}... | collective-permute-start | bytes 786440 | tf_op jit(solution)/shard_map/ppermute | solution.py:156
  61.2 15.4 %collective-permute-start.3 = (bf16[1024,128]{1,0:T(8,128)(2,1)S(1)}, bf16[1024,128]{1,0:T(8,128)(2,1)S(1)}, u32[]{:S(2)}, u32[]{:S(2)}) collective-permute-start(bf16[1024,128]{1,0:T(8,128)(2,1)S(1)} %get-tuple-element.28.k_ref), channel_id=1, source_target_pairs={{0,48},{16,0},{32,16},{48,32},{1,49},{17,1},{33,17},{49,33},{2,50}... | collective-permute-start | bytes 786440 | tf_op jit(solution)/shard_map/ppermute | solution.py:156
  63.1 16.7 %collective-permute-start.4 = (bf16[1024,128]{1,0:T(8,128)(2,1)S(1)}, bf16[1024,128]{1,0:T(8,128)(2,1)S(1)}, u32[]{:S(2)}, u32[]{:S(2)}) collective-permute-start(bf16[1024,128]{1,0:T(8,128)(2,1)S(1)} %get-tuple-element.38.v_ref), channel_id=1, source_target_pairs={{0,16},{16,32},{32,48},{48,0},{1,17},{17,33},{33,49},{49,1},{2,18}... | collective-permute-start | bytes 786440 | tf_op jit(solution)/shard_map/ppermute | solution.py:156
  63.1 19.8 %collective-permute-start.5 = (bf16[1024,128]{1,0:T(8,128)(2,1)S(1)}, bf16[1024,128]{1,0:T(8,128)(2,1)S(1)}, u32[]{:S(2)}, u32[]{:S(2)}) collective-permute-start(bf16[1024,128]{1,0:T(8,128)(2,1)S(1)} %get-tuple-element.38.v_ref), channel_id=1, source_target_pairs={{0,32},{16,48},{32,0},{48,16},{1,33},{17,49},{33,1},{49,17},{2,34}... | collective-permute-start | bytes 786440 | tf_op jit(solution)/shard_map/ppermute | solution.py:156
  71.1 14.4 %collective-permute-start.6 = (bf16[1024,128]{1,0:T(8,128)(2,1)S(1)}, bf16[1024,128]{1,0:T(8,128)(2,1)S(1)}, u32[]{:S(2)}, u32[]{:S(2)}) collective-permute-start(bf16[1024,128]{1,0:T(8,128)(2,1)S(1)} %get-tuple-element.38.v_ref), channel_id=1, source_target_pairs={{0,48},{16,0},{32,16},{48,32},{1,49},{17,1},{33,17},{49,33},{2,50}... | collective-permute-start | bytes 786440 | tf_op jit(solution)/shard_map/ppermute | solution.py:156
  87.5 4.3 %collective-permute-start.7 = (bf16[256,128]{1,0:T(8,128)(2,1)S(1)}, bf16[256,128]{1,0:T(8,128)(2,1)S(1)}, u32[]{:S(2)}, u32[]{:S(2)}) collective-permute-start(bf16[256,128]{1,0:T(8,128)(2,1)S(1)} %get-tuple-element.43), channel_id=1, source_target_pairs={{0,192},{64,128},{128,64},{192,0},{1,193},{65,129},{129,65},{193,1... | collective-permute-start | bytes 196616 | tf_op jit(solution)/shard_map/ppermute | solution.py:206
  88.3 4.1 %collective-permute-start.8 = (bf16[256,128]{1,0:T(8,128)(2,1)S(1)}, bf16[256,128]{1,0:T(8,128)(2,1)S(1)}, u32[]{:S(2)}, u32[]{:S(2)}) collective-permute-start(bf16[256,128]{1,0:T(8,128)(2,1)S(1)} %get-tuple-element.44), channel_id=1, source_target_pairs={{0,128},{64,192},{128,0},{192,64},{1,129},{65,193},{129,1},{193,65... | collective-permute-start | bytes 196616 | tf_op jit(solution)/shard_map/ppermute | solution.py:206
  88.8 3.7 %collective-permute-start.9 = (bf16[256,128]{1,0:T(8,128)(2,1)S(1)}, bf16[256,128]{1,0:T(8,128)(2,1)S(1)}, u32[]{:S(2)}, u32[]{:S(2)}) collective-permute-start(bf16[256,128]{1,0:T(8,128)(2,1)S(1)} %get-tuple-element.45), channel_id=1, source_target_pairs={{0,64},{64,0},{128,192},{192,128},{1,65},{65,1},{129,193},{193,129... | collective-permute-start | bytes 196616 | tf_op jit(solution)/shard_map/ppermute | solution.py:206
  92.5 3.5 %collective-permute-start.10 = (bf16[256,128]{1,0:T(8,128)(2,1)S(1)}, bf16[256,128]{1,0:T(8,128)(2,1)S(1)}, u32[]{:S(2)}, u32[]{:S(2)}) collective-permute-start(bf16[256,128]{1,0:T(8,128)(2,1)S(1)} %get-tuple-element.46), channel_id=1, source_target_pairs={{0,128},{128,0},{1,129},{129,1},{2,130},{130,2},{3,131},{131,3},{4... | collective-permute-start | bytes 196616 | tf_op jit(solution)/shard_map/ppermute | solution.py:160
  96.1 5.4 %collective-permute-start.11 = (bf16[512,128]{1,0:T(8,128)(2,1)S(1)}, bf16[512,128]{1,0:T(8,128)(2,1)S(1)}, u32[]{:S(2)}, u32[]{:S(2)}) collective-permute-start(bf16[512,128]{1,0:T(8,128)(2,1)S(1)} %pad_maximum_fusion.refs_0_), channel_id=1, source_target_pairs={{0,16},{16,32},{32,48},{48,0},{1,17},{17,33},{33,49},{49,1},{2,18}... | collective-permute-start | bytes 393224 | tf_op jit(solution)/shard_map/ppermute | solution.py:156
  96.5 7.6 %collective-permute-start.12 = (bf16[512,128]{1,0:T(8,128)(2,1)S(1)}, bf16[512,128]{1,0:T(8,128)(2,1)S(1)}, u32[]{:S(2)}, u32[]{:S(2)}) collective-permute-start(bf16[512,128]{1,0:T(8,128)(2,1)S(1)} %pad_maximum_fusion.refs_0_), channel_id=1, source_target_pairs={{0,32},{16,48},{32,0},{48,16},{1,33},{17,49},{33,1},{49,17},{2,34}... | collective-permute-start | bytes 393224 | tf_op jit(solution)/shard_map/ppermute | solution.py:156
  97.3 8.8 %collective-permute-start.13 = (bf16[512,128]{1,0:T(8,128)(2,1)S(1)}, bf16[512,128]{1,0:T(8,128)(2,1)S(1)}, u32[]{:S(2)}, u32[]{:S(2)}) collective-permute-start(bf16[512,128]{1,0:T(8,128)(2,1)S(1)} %pad_maximum_fusion.refs_0_), channel_id=1, source_target_pairs={{0,48},{16,0},{32,16},{48,32},{1,49},{17,1},{33,17},{49,33},{2,50}... | collective-permute-start | bytes 393224 | tf_op jit(solution)/shard_map/ppermute | solution.py:156
  98.4 14.2 %collective-permute-start.14 = (bf16[512,128]{1,0:T(8,128)(2,1)S(1)}, bf16[512,128]{1,0:T(8,128)(2,1)S(1)}, u32[]{:S(2)}, u32[]{:S(2)}) collective-permute-start(bf16[512,128]{1,0:T(8,128)(2,1)S(1)} %pad_maximum_fusion.refs_0_), channel_id=1, source_target_pairs={{0,64},{64,0},{1,65},{65,1},{2,66},{66,2},{3,67},{67,3},{4,68},{68... | collective-permute-start | bytes 393224 | tf_op jit(solution)/shard_map/ppermute | solution.py:160
  101.4 11.1 %collective-permute-start.15 = (bf16[512,128]{1,0:T(8,128)(2,1)S(1)}, bf16[512,128]{1,0:T(8,128)(2,1)S(1)}, u32[]{:S(2)}, u32[]{:S(2)}) collective-permute-start(bf16[512,128]{1,0:T(8,128)(2,1)S(1)} %collective-permute-done.11.refs_1_), channel_id=1, source_target_pairs={{0,64},{64,0},{1,65},{65,1},{2,66},{66,2},{3,67},{67,3},{4,68},{68... | collective-permute-start | bytes 393224 | tf_op jit(solution)/shard_map/ppermute | solution.py:160
  104.1 8.5 %collective-permute-start.16 = (bf16[512,128]{1,0:T(8,128)(2,1)S(1)}, bf16[512,128]{1,0:T(8,128)(2,1)S(1)}, u32[]{:S(2)}, u32[]{:S(2)}) collective-permute-start(bf16[512,128]{1,0:T(8,128)(2,1)S(1)} %collective-permute-done.12.refs_2_), channel_id=1, source_target_pairs={{0,64},{64,0},{1,65},{65,1},{2,66},{66,2},{3,67},{67,3},{4,68},{68... | collective-permute-start | bytes 393224 | tf_op jit(solution)/shard_map/ppermute | solution.py:160
  106.1 6.5 %collective-permute-start.17 = (bf16[512,128]{1,0:T(8,128)(2,1)S(1)}, bf16[512,128]{1,0:T(8,128)(2,1)S(1)}, u32[]{:S(2)}, u32[]{:S(2)}) collective-permute-start(bf16[512,128]{1,0:T(8,128)(2,1)S(1)} %collective-permute-done.13.refs_3_), channel_id=1, source_target_pairs={{0,64},{64,0},{1,65},{65,1},{2,66},{66,2},{3,67},{67,3},{4,68},{68... | collective-permute-start | bytes 393224 | tf_op jit(solution)/shard_map/ppermute | solution.py:160
  109.4 1.2 copy-start
  113.3 12.6 %collective-permute-start.18 = (bf16[4,128,128]{2,1,0:T(8,128)(2,1)S(1)}, bf16[4,128,128]{2,1,0:T(8,128)(2,1)S(1)}, u32[]{:S(2)}, u32[]{:S(2)}) collective-permute-start(bf16[4,128,128]{2,1,0:T(8,128)(2,1)S(1)} %shard_map.96), channel_id=1, source_target_pairs={{0,0},{1,1},{2,2},{3,3},{4,64},{5,65},{6,66},{7,67},{8,128},{9,129... | collective-permute-start | bytes 393224 | tf_op jit(solution)/shard_map/ppermute | solution.py:152
Sparse Core Ops, SparseCore 0:
  58.9 50.4 all-gather.1

commit v2 on v1

v2 whole, which is shorter than its diff:
```python
import functools

import jax
import jax.numpy as jnp
from jax import lax
from jax.experimental import pallas as pl
from jax.experimental.pallas import tpu as pltpu
from jax.sharding import Mesh, PartitionSpec as P

HEADS = 16
DIM = 128
SCALE2 = DIM ** -0.5 * 1.4426950408889634
BF, F32 = jnp.bfloat16, jnp.float32
MIB = 1 << 20
VM = pl.BlockSpec(memory_space=pltpu.VMEM)
SM = pl.BlockSpec(memory_space=pltpu.SMEM)
ANY = pl.BlockSpec(memory_space=pltpu.HBM)


def call(body, outs, operands, specs=None, out_specs=None, vmem=16, flops=0, scratch=()):
    moved = sum(o.size * o.dtype.itemsize for o in [*operands, *outs])
    return pl.pallas_call(
        body,
        out_shape=outs,
        in_specs=specs or [VM] * len(operands),
        out_specs=out_specs or [VM] * len(outs),
        scratch_shapes=list(scratch),
        compiler_params=pltpu.CompilerParams(vmem_limit_bytes=vmem * MIB),
        cost_estimate=pl.CostEstimate(flops=flops, bytes_accessed=moved, transcendentals=0),
    )(*operands)


def sds(shape, dtype=BF):
    return jax.ShapeDtypeStruct(shape, dtype)


def dot_nt(a, b):
    return lax.dot_general(a, b, (((1,), (1,)), ((), ())), preferred_element_type=F32)


def dot_nn(a, b):
    return lax.dot_general(a, b, (((1,), (0,)), ((), ())), preferred_element_type=F32)


def pack_kernel(k_ref, v_ref, q_ref, code_ref, out_ref, code_row, held, sem):
    code = pltpu.make_async_copy(code_ref, code_row, sem.at[48])
    code.start()
    copies = []
    for place in range(HEADS):
        yh, zt, zp = place // 8, place // 2 % 4, place % 2
        head = (yh * 2 + zp) * 4 + zt
        for n, ref in enumerate((k_ref, v_ref, q_ref)):
            source = ref.at[0, :, pl.ds(head * DIM, DIM)]
            target = held.at[place, pl.ds(n * 64, 64)]
            copies.append(pltpu.make_async_copy(source, target, sem.at[place * 3 + n]))
    for copy in copies:
        copy.start()
    code.wait()
    row = jnp.concatenate([code_row[...].astype(F32), jnp.zeros((1, 64), F32)], axis=1)
    held[:, 192:208] = jnp.broadcast_to(row.reshape(1, 1, 128), (HEADS, 16, DIM)).astype(BF)
    for copy in copies:
        copy.wait()
    last = pltpu.make_async_copy(held, out_ref, sem.at[49])
    last.start()
    last.wait()


def base_pack_kernel(at_ref, k_ref, v_ref, q_ref, *refs):
    outs, sem = refs[:4], refs[4]
    copies = []
    for step, out in enumerate(outs):
        head = (at_ref[3] + step) & 3
        for n, ref in enumerate((k_ref, v_ref, q_ref)):
            source = ref.at[:, pl.ds(pl.multiple_of(head * DIM, DIM), DIM)]
            target = out.at[pl.ds(n * 64, 64)]
            copies.append(pltpu.make_async_copy(source, target, sem.at[step * 3 + n]))
    for copy in copies:
        copy.start()
    for copy in copies:
        copy.wait()


def base_unpack_kernel(at_ref, *refs):
    ins, (kv_ref, q_ref) = refs[:4], refs[4:]
    for step, ref in enumerate(ins):
        first = ((at_ref[3] + 4 - step) & 3) * 64
        kv_ref[pl.ds(pl.multiple_of(first, 64), 64)] = ref[0:64]
        kv_ref[pl.ds(pl.multiple_of(256 + first, 64), 64)] = ref[64:128]
        q_ref[pl.ds(pl.multiple_of(first, 64), 64)] = ref[128:192]


def unpack_kernel(in_ref, after_ref, kv_ref, q_ref, factor_ref):
    del after_ref
    lane = lax.broadcasted_iota(jnp.int32, (64, 128), 1)
    sub = lax.broadcasted_iota(jnp.int32, (64, 128), 0)
    for place in range(16):
        yh, zt, zp = place // 8, place // 2 % 4, place % 2
        t = (yh * 2 + zp) * 4 + zt
        rows = slice(t * 64, (t + 1) * 64)
        first = t // 8 * 1024 + t % 8 * 64
        kv_ref[first : first + 64] = in_ref[place, 0:64]
        kv_ref[first + 512 : first + 576] = in_ref[place, 64:128]
        q_ref[rows] = in_ref[place, 128:192]
        code = in_ref[place, 192:208].astype(F32)[0:1]
        code = jnp.broadcast_to(code, (64, 128))
        col = jnp.sum(jnp.where(lane == sub, code, 0.0), axis=1, keepdims=True)
        factor_ref[rows] = col / 16.0


def score_kernel(q_ref, *refs):
    halves, (p_ref, m_ref, l_ref) = refs[:-3], refs[-3:]
    keys = [halves[0], halves[-1]]
    starts = (0, 0 if len(halves) == 2 else 1024)
    for i in range(4):
        rows = slice(i * 256, (i + 1) * 256)
        s = jnp.concatenate([dot_nt(q_ref[rows], k[a : a + 512]) for k, a in zip(keys, starts)], axis=1)
        m = jnp.max(s, axis=1, keepdims=True)
        p = jnp.exp2((s - m) * SCALE2)
        m_ref[rows] = m
        l_ref[rows] = jnp.sum(p, axis=1, keepdims=True)
        p_ref[rows] = p.astype(BF)


def merge(rows, ms, ls):
    m = [r[rows] for r in ms]
    best = functools.reduce(jnp.maximum, m)
    weights = [jnp.exp2((x - best) * SCALE2) for x in m]
    return best, weights, sum(w * l[rows] for w, l in zip(weights, ls))


def middle_kernel(*refs):
    ms, ls, ps, vs, (m_ref, l_ref, acc_ref) = refs[0:3], refs[3:6], refs[6:9], refs[9:12], refs[12:]
    for i in range(4):
        rows = slice(i * 256, (i + 1) * 256)
        best, weights, total = merge(rows, ms, ls)
        m_ref[rows] = best
        l_ref[rows] = total
        acc_ref[rows] = sum(
            (dot_nn(p[rows, 0:512], v[512:1024]) + dot_nn(p[rows, 512:1024], v[1536:2048])) * w
            for p, v, w in zip(ps, vs, weights)
        )


def finish_kernel(at_ref, factor_ref, *refs):
    ms, ls, acc_ref, p_ref, va_ref, vb_ref, keep_ref, give_ref = refs[0:2], refs[2:4], *refs[4:]
    b = at_ref[0] * 2 + at_ref[1]
    for chunk, out, place in ((1, give_ref, 0), (3, give_ref, 1), (0, keep_ref, 0), (2, keep_ref, 1)):
        rows = pl.ds(pl.multiple_of((b ^ chunk) * 256, 256), 256)
        _, weights, total = merge(rows, ms, ls)
        far = dot_nn(p_ref[rows, 0:512], va_ref[512:1024]) + dot_nn(p_ref[rows, 512:1024], vb_ref[512:1024])
        acc = acc_ref[rows] * weights[0] + far * weights[1]
        acc = acc / total * factor_ref[rows]
        out[place * 256 : place * 256 + 256] = acc.astype(out.dtype)


def pair_kernel(keep_ref, got_ref, pair_ref, send_ref):
    pair = keep_ref[...] + got_ref[...].astype(F32)
    pair_ref[...] = pair
    send_ref[...] = pair.astype(BF)


def join_kernel(pair_ref, got_ref, bv_ref, more_ref, after_ref, joined_ref, values_ref):
    del after_ref
    for n, base in enumerate((bv_ref, more_ref)):
        rows = slice(n * 256, n * 256 + 256)
        joined = pair_ref[rows] + got_ref[256 - n * 256 : 512 - n * 256].astype(F32)
        if n == 0:
            joined_ref[...] = joined.astype(BF)
        values_ref[rows] = (base[256:512].astype(F32) + joined).astype(BF)


def base_pair_kernel(kv_ref, more_ref, out_ref):
    out_ref[0:256] = kv_ref[0:256]
    out_ref[256:512] = more_ref[0:256]


def base_score_kernel(q_ref, *refs):
    keys, (p_ref, l_ref) = refs[:8], refs[8:]
    blocks = [dot_nt(q_ref[...], k[...]) for k in keys]
    best = jnp.max(functools.reduce(jnp.maximum, blocks), axis=1, keepdims=True)
    total = None
    for n, s in enumerate(blocks):
        p = jnp.exp2((s - best) * SCALE2)
        p_ref[n] = p.astype(BF)
        total = p if total is None else total + p
    l_ref[...] = jnp.sum(total, axis=1, keepdims=True)


def base_value_kernel(at_ref, p_ref, l_ref, joined_ref, *refs):
    values, outs, held = refs[:8], refs[8:12], refs[12]
    acc = None
    for n, v in enumerate(values):
        part = dot_nn(p_ref[n], v[...])
        acc = part if acc is None else acc + part
    held[...] = (acc / l_ref[...]).astype(BF)
    for step, out in enumerate(outs):
        rows = pl.ds(pl.multiple_of(((at_ref[3] + step) & 3) * 64, 64), 64)
        out[0:64] = joined_ref[rows]
        out[64:128] = held[rows]


def home_kernel(at_ref, in_ref, joined_ref, out_ref):
    for step in range(4):
        head = (at_ref[3] + 4 - step) & 3
        cols = pl.ds(pl.multiple_of(head * DIM, DIM), DIM)
        joined_ref[:, cols] = in_ref[step, 0:64].astype(F32)
        out_ref[:, cols] = in_ref[step, 64:128]


def swap(values, step=0):
    def place(b, c, z):
        return ((b * 2 + c // 2) * 4 + z) * 2 + c % 2

    perm = [
        (place(b, c, z), place(c, b, (z + step) % 4)) for b in range(4) for c in range(4) for z in range(4)
    ]
    return lax.ppermute(values, ("yl", "co", "yh", "zt", "zp"), perm)


def along(axis, values, step):
    return lax.ppermute(values, axis, [(j, (j + step) % 4) for j in range(4)])


def other(values, axis):
    return lax.ppermute(values, axis, [(0, 1), (1, 0)])


def gather_pair(pair):
    mine = [pair] + [None] * 3
    for step in (1, 3, 2):
        mine[step] = along("x", pair, step)
    return mine + [other(v, "co") for v in mine]


def shards(ctrl_q, ctrl_k, ctrl_v, codes, base_q, base_k, base_v):
    at = jnp.stack([lax.axis_index(a) for a in ("yl", "co", "x", "zt")]).astype(jnp.int32)

    (packed,) = call(
        pack_kernel,
        [sds((HEADS, 208, DIM))],
        [ctrl_k, ctrl_v, ctrl_q, codes],
        specs=[ANY] * 4,
        out_specs=[ANY],
        vmem=60,
        scratch=[pltpu.VMEM((1, 64), jnp.int32), pltpu.VMEM((HEADS, 208, DIM), BF), pltpu.SemaphoreType.DMA((50,))],
    )
    sent = lax.all_to_all(packed, ("yh", "zt", "zp"), 0, 0, tiled=True)

    parts = call(
        base_pack_kernel,
        [sds((192, DIM))] * 4,
        [at, base_k, base_v, base_q],
        specs=[SM] + [ANY] * 3,
        out_specs=[ANY] * 4,
        scratch=[pltpu.SemaphoreType.DMA((12,))],
    )
    parts = [swap(part, step) for step, part in enumerate(parts)]
    base_kv, base_quer = call(
        base_unpack_kernel, [sds((512, DIM)), sds((256, DIM))], [at, *parts], specs=[SM] + [VM] * 4
    )
    own, quer, factor = call(
        unpack_kernel, [sds((2048, DIM)), sds((1024, DIM)), sds((1024, 1), F32)], [sent, base_quer], specs=[VM, pl.BlockSpec(memory_space=pl.ANY)]
    )
    after, before = along("x", own, 1), along("x", own, 3)
    far = [along("x", after[:1024], 1), along("x", before[1024:], 3)]

    more_kv = other(base_kv, "yl")
    (base_pair,) = call(
        base_pair_kernel,
        [sds((512, DIM))],
        [base_kv, more_kv],
    )
    base_keys = gather_pair(base_pair)
    base_p, base_l = call(
        base_score_kernel,
        [sds((8, 256, 512)), sds((256, 1), F32)],
        [base_quer, *base_keys],
        vmem=24,
        flops=2 * 256 * 4096 * 128,
    )

    outs = [sds((1024, 1024)), sds((1024, 1), F32), sds((1024, 1), F32)]
    scored = [
        call(score_kernel, outs, [quer, kv], vmem=24, flops=2 * 1024 * 1024 * 128) for kv in (own, after, before)
    ]
    ps, ms, ls = zip(*scored)
    m, l, acc = call(
        middle_kernel,
        [sds((1024, 1), F32), sds((1024, 1), F32), sds((1024, DIM), F32)],
        [*ms, *ls, *ps, own, after, before],
        vmem=24,
        flops=3 * 2 * 1024 * 1024 * 128,
    )
    far_p, far_m, far_l = call(score_kernel, outs, [quer, *far], vmem=24, flops=2 * 1024 * 1024 * 128)
    keep, give = call(
        finish_kernel,
        [sds((512, DIM), F32), sds((512, DIM))],
        [at, factor, m, far_m, l, far_l, acc, far_p, *far],
        specs=[SM] + [VM] * 9,
        vmem=24,
        flops=2 * 1024 * 1024 * 128,
    )

    pair, send = call(pair_kernel, [sds((512, DIM), F32), sds((512, DIM))], [keep, other(give, "co")])
    joined, base_values = call(
        join_kernel, [sds((256, DIM)), sds((512, DIM))], [pair, other(send, "yl"), base_kv, more_kv, base_l], specs=[VM] * 4 + [pl.BlockSpec(memory_space=pl.ANY)]
    )

    outs = call(
        base_value_kernel,
        [sds((128, DIM))] * 4,
        [at, base_p, base_l, joined, *gather_pair(base_values)],
        specs=[SM] + [VM] * 11,
        flops=2 * 256 * 4096 * 128,
        scratch=[pltpu.VMEM((256, DIM), BF)],
    )
    result = [outs[0]] + [None] * 3
    for step in (1, 3, 2):
        result[step] = along("zt", outs[step], step)
    result = swap(jnp.stack(result))
    return call(home_kernel, [sds((64, 512), F32), sds((64, 512))], [at, result], specs=[SM, VM])


def solution(mesh):
    fine = Mesh(mesh.devices.reshape(2, 2, 4, 2, 4, 2), ("yl", "co", "x", "yh", "zt", "zp"))
    branch, seq = ("yl", "co"), ("x", "yh", "zt", "zp")
    return jax.shard_map(
        shards,
        mesh=fine,
        in_specs=(P(branch, seq, None),) * 3 + (P(branch, seq),) + (P(seq, branch),) * 3,
        out_specs=(P(seq, branch), P(seq, branch)),
        check_vma=False,
    )
```

time: 144 us -> 112 us (0.78)
  the two profiles are of different devices: /device:TPU:19 before, /device:TPU:8 now
where the time goes in v2:
time: 112 us
  starting transfers between devices  52.7 us (47%)
  waiting for transfers between devices  42.3 us (38%)
  Pallas kernels  15.8 us (14%)
    ppermute x13, starting transfers between devices, along(): return lax.ppermute(values, axis, [(j, (j + step) % 4) for j in range(4)])  23.5 us
    ppermute x5, waiting for transfers between devices, swap(): return lax.ppermute(values, ('yl', 'co', 'yh', 'zt', 'zp'), perm)  19.8 us
    ppermute x13, waiting for transfers between devices, along(): return lax.ppermute(values, axis, [(j, (j + step) % 4) for j in range(4)])  17.3 us
    ppermute x5, starting transfers between devices, swap(): return lax.ppermute(values, ('yl', 'co', 'yh', 'zt', 'zp'), perm)  16.8 us
    pallas_call x16, Pallas kernels, call(): pl.pallas_call(body, out_shape=outs, in_specs=specs or [VM] * len(operand...  15.8 us
    all_to_all x1, starting transfers between devices, shards(): sent = lax.all_to_all(packed, ('yh', 'zt', 'zp'), 0, 0, tiled=True)  10.3 us
    ppermute x11, waiting for transfers between devices, other(): return lax.ppermute(values, axis, [(0, 1), (1, 0)])  5.25 us
  transfers between devices with their start and end apart: 30, of which 15 were waited for; matrix products, arithmetic and copies ran while one was open for 0% of the time, Pallas kernels for 9%

profile of v2, /device:TPU:8, one launch (start us, length us, event | category | flops | bytes accessed | tf_op | source)
XLA Modules:
  0.0 111.8 jit_solution(9627587785281542787)
XLA Ops:
  0.7 2.5 %shard_map.90 = bf16[16,208,128]{2,1,0:T(8,128)(2,1)} custom-call(bf16[1,64,2048]{2,1,0:T(8,128)(2,1)} %k_ref.3, bf16[1,64,2048]{2,1,0:T(8,128)(2,1)} %v_ref.3, bf16[1,64,2048]{2,1,0:T(8,128)(2,1)} %q_ref.3, s32[1,64]{1,0:T(1,128)} %code_ref.1), custom_call_target="tpu_custom_call" | custom-call | bytes 1638656 | tf_op jit(solution)/shard_map/pallas_call | solution.py:22
  3.2 10.3 %all-to-all-start = ((bf16[16,208,128]{2,1,0:T(8,128)(2,1)}), bf16[16,208,128]{2,1,0:T(8,128)(2,1)S(1)}, u32[]{:S(2)}, u32[]{:S(2)}) async-start(bf16[16,208,128]{2,1,0:T(8,128)(2,1)} %shard_map.90), calls=%async_computation | async-start | bytes 1703936 | tf_op jit(solution)/shard_map/all_to_all | solution.py:247
  13.6 0.7 shard_map.86
  14.3 4.6 %collective-permute-start = (bf16[192,128]{1,0:T(8,128)(2,1)S(1)}, bf16[192,128]{1,0:T(8,128)(2,1)S(1)}, u32[]{:S(2)}, u32[]{:S(2)}) collective-permute-start(bf16[192,128]{1,0:T(8,128)(2,1)S(1)} %get-tuple-element.38), channel_id=1, source_target_pairs={{0,0},{2,2},{4,4},{6,6},{1,64},{3,66},{5,68},{7,70},{8,128},{10,13... | collective-permute-start | bytes 147464 | tf_op jit(solution)/shard_map/ppermute | solution.py:217
  18.9 1.9 %collective-permute-start.1 = (bf16[192,128]{1,0:T(8,128)(2,1)S(1)}, bf16[192,128]{1,0:T(8,128)(2,1)S(1)}, u32[]{:S(2)}, u32[]{:S(2)}) collective-permute-start(bf16[192,128]{1,0:T(8,128)(2,1)S(1)} %get-tuple-element.39), channel_id=1, source_target_pairs={{0,2},{2,4},{4,6},{6,0},{1,66},{3,68},{5,70},{7,64},{8,130},{10,13... | collective-permute-start | bytes 147464 | tf_op jit(solution)/shard_map/ppermute | solution.py:217
  20.8 5.0 %collective-permute-start.2 = (bf16[192,128]{1,0:T(8,128)(2,1)S(1)}, bf16[192,128]{1,0:T(8,128)(2,1)S(1)}, u32[]{:S(2)}, u32[]{:S(2)}) collective-permute-start(bf16[192,128]{1,0:T(8,128)(2,1)S(1)} %get-tuple-element.40), channel_id=1, source_target_pairs={{0,4},{2,6},{4,0},{6,2},{1,68},{3,70},{5,64},{7,66},{8,132},{10,13... | collective-permute-start | bytes 147464 | tf_op jit(solution)/shard_map/ppermute | solution.py:217
  25.9 3.0 %collective-permute-start.3 = (bf16[192,128]{1,0:T(8,128)(2,1)S(1)}, bf16[192,128]{1,0:T(8,128)(2,1)S(1)}, u32[]{:S(2)}, u32[]{:S(2)}) collective-permute-start(bf16[192,128]{1,0:T(8,128)(2,1)S(1)} %get-tuple-element.41), channel_id=1, source_target_pairs={{0,6},{2,0},{4,2},{6,4},{1,70},{3,64},{5,66},{7,68},{8,134},{10,12... | collective-permute-start | bytes 147464 | tf_op jit(solution)/shard_map/ppermute | solution.py:217
  28.9 12.4 %collective-permute-done.1.refs_1_ = bf16[192,128]{1,0:T(8,128)(2,1)S(1)} collective-permute-done((bf16[192,128]{1,0:T(8,128)(2,1)S(1)}, bf16[192,128]{1,0:T(8,128)(2,1)S(1)}, u32[]{:S(2)}, u32[]{:S(2)}) %collective-permute-start.1) | collective-permute-done | bytes 49184 | tf_op jit(solution)/shard_map/ppermute | solution.py:217
  41.3 2.0 %collective-permute-done.2.refs_2_ = bf16[192,128]{1,0:T(8,128)(2,1)S(1)} collective-permute-done((bf16[192,128]{1,0:T(8,128)(2,1)S(1)}, bf16[192,128]{1,0:T(8,128)(2,1)S(1)}, u32[]{:S(2)}, u32[]{:S(2)}) %collective-permute-start.2) | collective-permute-done | bytes 49184 | tf_op jit(solution)/shard_map/ppermute | solution.py:217
  43.3 0.6 shard_map.87
  43.9 0.2 shard_map.91
  44.1 1.6 %collective-permute-start.12 = (bf16[2048,128]{1,0:T(8,128)(2,1)S(1)}, bf16[2048,128]{1,0:T(8,128)(2,1)S(1)}, u32[]{:S(2)}, u32[]{:S(2)}) collective-permute-start(bf16[2048,128]{1,0:T(8,128)(2,1)S(1)} %get-tuple-element.48.refs_0_.refs_9_), channel_id=1, source_target_pairs={{0,16},{16,32},{32,48},{48,0},{1,17},{17,33},{33,49},{49,1},{2,18}... | collective-permute-start | bytes 1572872 | tf_op jit(solution)/shard_map/ppermute | solution.py:221
  45.7 1.7 %collective-permute-start.13 = (bf16[2048,128]{1,0:T(8,128)(2,1)S(1)}, bf16[2048,128]{1,0:T(8,128)(2,1)S(1)}, u32[]{:S(2)}, u32[]{:S(2)}) collective-permute-start(bf16[2048,128]{1,0:T(8,128)(2,1)S(1)} %get-tuple-element.48.refs_0_.refs_9_), channel_id=1, source_target_pairs={{0,48},{16,0},{32,16},{48,32},{1,49},{17,1},{33,17},{49,33},{2,50}... | collective-permute-start | bytes 1572872 | tf_op jit(solution)/shard_map/ppermute | solution.py:221
  47.6 9.7 %collective-permute-done.12.refs_0_.refs_10_ = bf16[2048,128]{1,0:T(8,128)(2,1)S(1)} collective-permute-done((bf16[2048,128]{1,0:T(8,128)(2,1)S(1)}, bf16[2048,128]{1,0:T(8,128)(2,1)S(1)}, u32[]{:S(2)}, u32[]{:S(2)}) %collective-permute-start.12) | collective-permute-done | bytes 524320 | tf_op jit(solution)/shard_map/ppermute | solution.py:221
  57.3 0.4 collective-permute-start.14
  57.8 3.0 %collective-permute-start.15 = (bf16[1024,128]{1,0:T(8,128)(2,1)S(1)}, bf16[1024,128]{1,0:T(8,128)(2,1)S(1)}, u32[]{:S(2)}, u32[]{:S(2)}) collective-permute-start(bf16[1024,128]{1,0:T(8,128)(2,1)S(1)} %slice.9), channel_id=1, source_target_pairs={{0,48},{16,0},{32,16},{48,32},{1,49},{17,1},{33,17},{49,33},{2,50}... | collective-permute-start | bytes 786440 | tf_op jit(solution)/shard_map/ppermute | solution.py:221
  60.8 0.8 collective-permute-start.6
  61.6 1.1 %collective-permute-start.7 = (bf16[512,128]{1,0:T(8,128)(2,1)S(1)}, bf16[512,128]{1,0:T(8,128)(2,1)S(1)}, u32[]{:S(2)}, u32[]{:S(2)}) collective-permute-start(bf16[512,128]{1,0:T(8,128)(2,1)S(1)} %shard_map.88.refs_0_), channel_id=1, source_target_pairs={{0,48},{16,0},{32,16},{48,32},{1,49},{17,1},{33,17},{49,33},{2,50}... | collective-permute-start | bytes 393224 | tf_op jit(solution)/shard_map/ppermute | solution.py:221
  62.7 0.9 collective-permute-start.5
  63.6 1.2 %shard_map.92 = (bf16[1024,1024]{1,0:T(8,128)(2,1)S(1)}, f32[1024,1]{1,0:T(8,128)S(1)}, f32[1024,1]{1,0:T(8,128)S(1)}) custom-call(bf16[1024,128]{1,0:T(8,128)(2,1)S(1)} %get-tuple-element.47.q_ref, bf16[2048,128]{1,0:T(8,128)(2,1)S(1)} %get-tuple-element.48.refs_0_.refs_9_), custom_call_target="tpu_custom_call" | custom-call | flops 268435456 | bytes 2891776 | tf_op jit(solution)/shard_map/pallas_call | solution.py:22
  64.8 1.2 %shard_map.93 = (bf16[1024,1024]{1,0:T(8,128)(2,1)S(1)}, f32[1024,1]{1,0:T(8,128)S(1)}, f32[1024,1]{1,0:T(8,128)S(1)}) custom-call(bf16[1024,128]{1,0:T(8,128)(2,1)S(1)} %get-tuple-element.47.q_ref, bf16[2048,128]{1,0:T(8,128)(2,1)S(1)} %collective-permute-done.12.refs_0_.refs_10_), custom_call_target="tpu_custom_call" | custom-call | flops 268435456 | bytes 2891776 | tf_op jit(solution)/shard_map/pallas_call | solution.py:22
  65.9 1.2 %shard_map.94 = (bf16[1024,1024]{1,0:T(8,128)(2,1)S(1)}, f32[1024,1]{1,0:T(8,128)S(1)}, f32[1024,1]{1,0:T(8,128)S(1)}) custom-call(bf16[1024,128]{1,0:T(8,128)(2,1)S(1)} %get-tuple-element.47.q_ref, bf16[2048,128]{1,0:T(8,128)(2,1)S(1)} %collective-permute-done.13.refs_0_.refs_11_), custom_call_target="tpu_custom_call" | custom-call | flops 268435456 | bytes 2891776 | tf_op jit(solution)/shard_map/pallas_call | solution.py:22
  67.1 1.8 %shard_map.95 = (f32[1024,1]{1,0:T(8,128)S(1)}, f32[1024,1]{1,0:T(8,128)S(1)}, f32[1024,128]{1,0:T(8,128)S(1)}) custom-call(f32[1024,1]{1,0:T(8,128)S(1)} %get-tuple-element.49.refs_0_, f32[1024,1]{1,0:T(8,128)S(1)} %get-tuple-element.50.refs_1_, f32[1024,1]{1,0:T(8,128)S(1)} %get-tuple-element.51.refs_2_, f32[1024,1]{1,0:T(8,128)S(1)} %get-tuple-element.52.refs_3_, ...), custom_call_target="tpu_custom_call" | custom-call | flops 805306368 | bytes 8421376 | tf_op jit(solution)/shard_map/pallas_call | solution.py:22
  69.0 1.2 %shard_map.96 = (bf16[1024,1024]{1,0:T(8,128)(2,1)S(1)}, f32[1024,1]{1,0:T(8,128)S(1)}, f32[1024,1]{1,0:T(8,128)S(1)}) custom-call(bf16[1024,128]{1,0:T(8,128)(2,1)S(1)} %get-tuple-element.47.q_ref, bf16[1024,128]{1,0:T(8,128)(2,1)S(1)} %collective-permute-done.14.refs_0_.refs_6_, bf16[1024,128]{1,0:T(8,128)(2,1)S(1)} %collective-permute-done.15.refs_1_.refs_7_), custom_call_target="tpu_custom_call" | custom-call | flops 268435456 | bytes 2891776 | tf_op jit(solution)/shard_map/pallas_call | solution.py:22
  70.1 1.3 %shard_map.97 = (f32[512,128]{1,0:T(8,128)S(1)}, bf16[512,128]{1,0:T(8,128)(2,1)S(1)}) custom-call(s32[4]{0:T(128)S(1)} %pad_add_fusion.at_ref, f32[1024,1]{1,0:T(8,128)S(1)} %get-tuple-element.46.factor_ref, f32[1024,1]{1,0:T(8,128)S(1)} %get-tuple-element.58.refs_0_, f32[1024,1]{1,0:T(8,128)S(1)} %get-tuple-element.59.refs_1_, ...), custom_call_target="tpu_custom_call" | custom-call | flops 268435456 | bytes 3559440 | tf_op jit(solution)/shard_map/pallas_call | solution.py:22
  71.5 0.5 collective-permute-start.8
  72.1 0.4 collective-permute-start.11
  72.7 0.2 collective-permute-done.16.got_ref
  72.9 0.3 collective-permute-start.17
  73.2 0.2 collective-permute-done.10.refs_6_
  73.6 0.3 collective-permute-done.9.refs_5_
  73.9 1.4 %shard_map.89 = (bf16[8,256,512]{2,1,0:T(8,128)(2,1)S(1)}, f32[256,1]{1,0:T(8,128)S(1)}) custom-call(bf16[256,128]{1,0:T(8,128)(2,1)S(1)} %get-tuple-element.42.q_ref.after_ref, bf16[512,128]{1,0:T(8,128)(2,1)S(1)} %shard_map.88.refs_0_, bf16[512,128]{1,0:T(8,128)(2,1)S(1)} %collective-permute-done.5.refs_1_, ...), custom_call_target="tpu_custom_call" | custom-call | flops 268435456 | bytes 3212288 | tf_op jit(solution)/shard_map/pallas_call | solution.py:22
  75.3 3.3 %collective-permute-done.17.got_ref = bf16[512,128]{1,0:T(8,128)(2,1)S(1)} collective-permute-done((bf16[512,128]{1,0:T(8,128)(2,1)S(1)}, bf16[512,128]{1,0:T(8,128)(2,1)S(1)}, u32[]{:S(2)}, u32[]{:S(2)}) %collective-permute-start.17) | collective-permute-done | bytes 131104 | tf_op jit(solution)/shard_map/ppermute | solution.py:225
  78.7 1.1 collective-permute-start.18
  79.7 3.0 %collective-permute-start.19 = (bf16[512,128]{1,0:T(8,128)(2,1)S(1)}, bf16[512,128]{1,0:T(8,128)(2,1)S(1)}, u32[]{:S(2)}, u32[]{:S(2)}) collective-permute-start(bf16[512,128]{1,0:T(8,128)(2,1)S(1)} %get-tuple-element.69.refs_0_), channel_id=1, source_target_pairs={{0,32},{16,48},{32,0},{48,16},{1,33},{17,49},{33,1},{49,17},{2,34}... | collective-permute-start | bytes 393224 | tf_op jit(solution)/shard_map/ppermute | solution.py:221
  82.8 1.7 %collective-permute-start.20 = (bf16[512,128]{1,0:T(8,128)(2,1)S(1)}, bf16[512,128]{1,0:T(8,128)(2,1)S(1)}, u32[]{:S(2)}, u32[]{:S(2)}) collective-permute-start(bf16[512,128]{1,0:T(8,128)(2,1)S(1)} %get-tuple-element.69.refs_0_), channel_id=1, source_target_pairs={{0,48},{16,0},{32,16},{48,32},{1,49},{17,1},{33,17},{49,33},{2,50}... | collective-permute-start | bytes 393224 | tf_op jit(solution)/shard_map/ppermute | solution.py:221
  84.4 2.0 %collective-permute-done.18.refs_1_ = bf16[512,128]{1,0:T(8,128)(2,1)S(1)} collective-permute-done((bf16[512,128]{1,0:T(8,128)(2,1)S(1)}, bf16[512,128]{1,0:T(8,128)(2,1)S(1)}, u32[]{:S(2)}, u32[]{:S(2)}) %collective-permute-start.18) | collective-permute-done | bytes 131104 | tf_op jit(solution)/shard_map/ppermute | solution.py:221
  86.4 1.9 %collective-permute-done.19.refs_2_ = bf16[512,128]{1,0:T(8,128)(2,1)S(1)} collective-permute-done((bf16[512,128]{1,0:T(8,128)(2,1)S(1)}, bf16[512,128]{1,0:T(8,128)(2,1)S(1)}, u32[]{:S(2)}, u32[]{:S(2)}) %collective-permute-start.19) | collective-permute-done | bytes 131104 | tf_op jit(solution)/shard_map/ppermute | solution.py:221
  88.4 0.5 collective-permute-start.24
  88.8 0.8 collective-permute-done.23.refs_6_
  89.9 1.2 %shard_map.100 = (bf16[128,128]{1,0:T(8,128)(2,1)S(1)}, bf16[128,128]{1,0:T(8,128)(2,1)S(1)}, bf16[128,128]{1,0:T(8,128)(2,1)S(1)}, bf16[128,128]{1,0:T(8,128)(2,1)S(1)}) custom-call(s32[4]{0:T(128)S(1)} %pad_add_fusion.at_ref, bf16[8,256,512]{2,1,0:T(8,128)(2,1)S(1)} %get-tuple-element.44.p_ref, f32[256,1]{1,0:T(8,128)S(1)} %get-tuple-element.45.after_ref.l_ref, ...), custom_call_target="tpu_custom_call" | custom-call | flops 268435456 | bytes 3343376 | tf_op jit(solution)/shard_map/pallas_call | solution.py:22
  91.1 3.6 %collective-permute-start.25 = (bf16[128,128]{1,0:T(8,128)(2,1)S(1)}, bf16[128,128]{1,0:T(8,128)(2,1)S(1)}, u32[]{:S(2)}, u32[]{:S(2)}) collective-permute-start(bf16[128,128]{1,0:T(8,128)(2,1)S(1)} %get-tuple-element.71), channel_id=1, source_target_pairs={{0,2},{2,4},{4,6},{6,0},{1,3},{3,5},{5,7},{7,1},{8,10},{10,12},{12... | collective-permute-start | bytes 98312 | tf_op jit(solution)/shard_map/ppermute | solution.py:221
  94.7 0.5 collective-permute-start.26
  95.2 4.0 %collective-permute-start.27 = (bf16[128,128]{1,0:T(8,128)(2,1)S(1)}, bf16[128,128]{1,0:T(8,128)(2,1)S(1)}, u32[]{:S(2)}, u32[]{:S(2)}) collective-permute-start(bf16[128,128]{1,0:T(8,128)(2,1)S(1)} %get-tuple-element.73), channel_id=1, source_target_pairs={{0,6},{2,0},{4,2},{6,4},{1,7},{3,1},{5,3},{7,5},{8,14},{10,8},{12,... | collective-permute-start | bytes 98312 | tf_op jit(solution)/shard_map/ppermute | solution.py:221
  99.3 3.6 %collective-permute-done.26 = bf16[128,128]{1,0:T(8,128)(2,1)S(1)} collective-permute-done((bf16[128,128]{1,0:T(8,128)(2,1)S(1)}, bf16[128,128]{1,0:T(8,128)(2,1)S(1)}, u32[]{:S(2)}, u32[]{:S(2)}) %collective-permute-start.26) | collective-permute-done | bytes 32800 | tf_op jit(solution)/shard_map/ppermute | solution.py:221
  102.9 2.2 %collective-permute-start.28 = (bf16[4,128,128]{2,1,0:T(8,128)(2,1)S(1)}, bf16[4,128,128]{2,1,0:T(8,128)(2,1)S(1)}, u32[]{:S(2)}, u32[]{:S(2)}) collective-permute-start(bf16[4,128,128]{2,1,0:T(8,128)(2,1)S(1)} %pad_maximum_fusion), channel_id=1, source_target_pairs={{0,0},{2,2},{4,4},{6,6},{1,64},{3,66},{5,68},{7,70},{8,128},{10,13... | collective-permute-start | bytes 393224 | tf_op jit(solution)/shard_map/ppermute | solution.py:217
  105.2 5.4 %collective-permute-done.28.in_ref = bf16[4,128,128]{2,1,0:T(8,128)(2,1)S(1)} collective-permute-done((bf16[4,128,128]{2,1,0:T(8,128)(2,1)S(1)}, bf16[4,128,128]{2,1,0:T(8,128)(2,1)S(1)}, u32[]{:S(2)}, u32[]{:S(2)}) %collective-permute-start.28) | collective-permute-done | bytes 131104 | tf_op jit(solution)/shard_map/ppermute | solution.py:217
  110.6 1.2 %shard_map.101 = (f32[64,512]{1,0:T(8,128)}, bf16[64,512]{1,0:T(8,128)(2,1)}) custom-call(s32[4]{0:T(128)S(1)} %pad_add_fusion.at_ref, bf16[4,128,128]{2,1,0:T(8,128)(2,1)S(1)} %collective-permute-done.28.in_ref), custom_call_target="tpu_custom_call" | custom-call | bytes 327696 | tf_op jit(solution)/shard_map/pallas_call | solution.py:22
  (38 shorter events, 1.2 us)
Async XLA Ops:
  0.6 13.0 %copy-start.2 = (bf16[64,512]{1,0:T(8,128)(2,1)S(1)}, bf16[64,512]{1,0:T(8,128)(2,1)}, u32[]{:S(2)}) copy-start(bf16[64,512]{1,0:T(8,128)(2,1)} %q_ref.2) | copy-start | bytes 196612
  0.6 12.9 %copy-start = (bf16[64,512]{1,0:T(8,128)(2,1)S(1)}, bf16[64,512]{1,0:T(8,128)(2,1)}, u32[]{:S(2)}) copy-start(bf16[64,512]{1,0:T(8,128)(2,1)} %k_ref.2) | copy-start | bytes 196612
  0.7 12.9 %copy-start.1 = (bf16[64,512]{1,0:T(8,128)(2,1)S(1)}, bf16[64,512]{1,0:T(8,128)(2,1)}, u32[]{:S(2)}) copy-start(bf16[64,512]{1,0:T(8,128)(2,1)} %v_ref.2) | copy-start | bytes 196612
  3.2 40.7 %all-to-all-start = ((bf16[16,208,128]{2,1,0:T(8,128)(2,1)}), bf16[16,208,128]{2,1,0:T(8,128)(2,1)S(1)}, u32[]{:S(2)}, u32[]{:S(2)}) async-start(bf16[16,208,128]{2,1,0:T(8,128)(2,1)} %shard_map.90), calls=%async_computation | async-start | bytes 1703936 | tf_op jit(solution)/shard_map/all_to_all | solution.py:247
  14.3 14.6 %collective-permute-start = (bf16[192,128]{1,0:T(8,128)(2,1)S(1)}, bf16[192,128]{1,0:T(8,128)(2,1)S(1)}, u32[]{:S(2)}, u32[]{:S(2)}) collective-permute-start(bf16[192,128]{1,0:T(8,128)(2,1)S(1)} %get-tuple-element.38), channel_id=1, source_target_pairs={{0,0},{2,2},{4,4},{6,6},{1,64},{3,66},{5,68},{7,70},{8,128},{10,13... | collective-permute-start | bytes 147464 | tf_op jit(solution)/shard_map/ppermute | solution.py:217
  18.9 22.4 %collective-permute-start.1 = (bf16[192,128]{1,0:T(8,128)(2,1)S(1)}, bf16[192,128]{1,0:T(8,128)(2,1)S(1)}, u32[]{:S(2)}, u32[]{:S(2)}) collective-permute-start(bf16[192,128]{1,0:T(8,128)(2,1)S(1)} %get-tuple-element.39), channel_id=1, source_target_pairs={{0,2},{2,4},{4,6},{6,0},{1,66},{3,68},{5,70},{7,64},{8,130},{10,13... | collective-permute-start | bytes 147464 | tf_op jit(solution)/shard_map/ppermute | solution.py:217
  20.8 22.5 %collective-permute-start.2 = (bf16[192,128]{1,0:T(8,128)(2,1)S(1)}, bf16[192,128]{1,0:T(8,128)(2,1)S(1)}, u32[]{:S(2)}, u32[]{:S(2)}) collective-permute-start(bf16[192,128]{1,0:T(8,128)(2,1)S(1)} %get-tuple-element.40), channel_id=1, source_target_pairs={{0,4},{2,6},{4,0},{6,2},{1,68},{3,70},{5,64},{7,66},{8,132},{10,13... | collective-permute-start | bytes 147464 | tf_op jit(solution)/shard_map/ppermute | solution.py:217
  25.9 17.4 %collective-permute-start.3 = (bf16[192,128]{1,0:T(8,128)(2,1)S(1)}, bf16[192,128]{1,0:T(8,128)(2,1)S(1)}, u32[]{:S(2)}, u32[]{:S(2)}) collective-permute-start(bf16[192,128]{1,0:T(8,128)(2,1)S(1)} %get-tuple-element.41), channel_id=1, source_target_pairs={{0,6},{2,0},{4,2},{6,4},{1,70},{3,64},{5,66},{7,68},{8,134},{10,12... | collective-permute-start | bytes 147464 | tf_op jit(solution)/shard_map/ppermute | solution.py:217
  44.1 13.2 %collective-permute-start.12 = (bf16[2048,128]{1,0:T(8,128)(2,1)S(1)}, bf16[2048,128]{1,0:T(8,128)(2,1)S(1)}, u32[]{:S(2)}, u32[]{:S(2)}) collective-permute-start(bf16[2048,128]{1,0:T(8,128)(2,1)S(1)} %get-tuple-element.48.refs_0_.refs_9_), channel_id=1, source_target_pairs={{0,16},{16,32},{32,48},{48,0},{1,17},{17,33},{33,49},{49,1},{2,18}... | collective-permute-start | bytes 1572872 | tf_op jit(solution)/shard_map/ppermute | solution.py:221
  45.7 12.1 %collective-permute-start.13 = (bf16[2048,128]{1,0:T(8,128)(2,1)S(1)}, bf16[2048,128]{1,0:T(8,128)(2,1)S(1)}, u32[]{:S(2)}, u32[]{:S(2)}) collective-permute-start(bf16[2048,128]{1,0:T(8,128)(2,1)S(1)} %get-tuple-element.48.refs_0_.refs_9_), channel_id=1, source_target_pairs={{0,48},{16,0},{32,16},{48,32},{1,49},{17,1},{33,17},{49,33},{2,50}... | collective-permute-start | bytes 1572872 | tf_op jit(solution)/shard_map/ppermute | solution.py:221
  47.4 13.3 %collective-permute-start.4 = (bf16[512,128]{1,0:T(8,128)(2,1)S(1)}, bf16[512,128]{1,0:T(8,128)(2,1)S(1)}, u32[]{:S(2)}, u32[]{:S(2)}) collective-permute-start(bf16[512,128]{1,0:T(8,128)(2,1)S(1)} %get-tuple-element.43.kv_ref.bv_ref), channel_id=1, source_target_pairs={{0,128},{128,0},{1,129},{129,1},{2,130},{130,2},{3,131},{131,3},{4... | collective-permute-start | bytes 393224 | tf_op jit(solution)/shard_map/ppermute | solution.py:225
  57.3 11.6 %collective-permute-start.14 = (bf16[1024,128]{1,0:T(8,128)(2,1)S(1)}, bf16[1024,128]{1,0:T(8,128)(2,1)S(1)}, u32[]{:S(2)}, u32[]{:S(2)}) collective-permute-start(bf16[1024,128]{1,0:T(8,128)(2,1)S(1)} %slice.8), channel_id=1, source_target_pairs={{0,16},{16,32},{32,48},{48,0},{1,17},{17,33},{33,49},{49,1},{2,18}... | collective-permute-start | bytes 786440 | tf_op jit(solution)/shard_map/ppermute | solution.py:221
  57.8 11.1 %collective-permute-start.15 = (bf16[1024,128]{1,0:T(8,128)(2,1)S(1)}, bf16[1024,128]{1,0:T(8,128)(2,1)S(1)}, u32[]{:S(2)}, u32[]{:S(2)}) collective-permute-start(bf16[1024,128]{1,0:T(8,128)(2,1)S(1)} %slice.9), channel_id=1, source_target_pairs={{0,48},{16,0},{32,16},{48,32},{1,49},{17,1},{33,17},{49,33},{2,50}... | collective-permute-start | bytes 786440 | tf_op jit(solution)/shard_map/ppermute | solution.py:221
  60.8 11.3 %collective-permute-start.6 = (bf16[512,128]{1,0:T(8,128)(2,1)S(1)}, bf16[512,128]{1,0:T(8,128)(2,1)S(1)}, u32[]{:S(2)}, u32[]{:S(2)}) collective-permute-start(bf16[512,128]{1,0:T(8,128)(2,1)S(1)} %shard_map.88.refs_0_), channel_id=1, source_target_pairs={{0,32},{16,48},{32,0},{48,16},{1,33},{17,49},{33,1},{49,17},{2,34}... | collective-permute-start | bytes 393224 | tf_op jit(solution)/shard_map/ppermute | solution.py:221
  61.6 10.6 %collective-permute-start.7 = (bf16[512,128]{1,0:T(8,128)(2,1)S(1)}, bf16[512,128]{1,0:T(8,128)(2,1)S(1)}, u32[]{:S(2)}, u32[]{:S(2)}) collective-permute-start(bf16[512,128]{1,0:T(8,128)(2,1)S(1)} %shard_map.88.refs_0_), channel_id=1, source_target_pairs={{0,48},{16,0},{32,16},{48,32},{1,49},{17,1},{33,17},{49,33},{2,50}... | collective-permute-start | bytes 393224 | tf_op jit(solution)/shard_map/ppermute | solution.py:221
  62.7 9.9 %collective-permute-start.5 = (bf16[512,128]{1,0:T(8,128)(2,1)S(1)}, bf16[512,128]{1,0:T(8,128)(2,1)S(1)}, u32[]{:S(2)}, u32[]{:S(2)}) collective-permute-start(bf16[512,128]{1,0:T(8,128)(2,1)S(1)} %shard_map.88.refs_0_), channel_id=1, source_target_pairs={{0,16},{16,32},{32,48},{48,0},{1,17},{17,33},{33,49},{49,1},{2,18}... | collective-permute-start | bytes 393224 | tf_op jit(solution)/shard_map/ppermute | solution.py:221
  71.4 1.4 %collective-permute-start.16 = (bf16[512,128]{1,0:T(8,128)(2,1)S(1)}, bf16[512,128]{1,0:T(8,128)(2,1)S(1)}, u32[]{:S(2)}, u32[]{:S(2)}) collective-permute-start(bf16[512,128]{1,0:T(8,128)(2,1)S(1)} %get-tuple-element.65), channel_id=1, source_target_pairs={{0,64},{64,0},{1,65},{65,1},{2,66},{66,2},{3,67},{67,3},{4,68},{68... | collective-permute-start | bytes 393224 | tf_op jit(solution)/shard_map/ppermute | solution.py:225
  71.5 1.7 %collective-permute-start.8 = (bf16[512,128]{1,0:T(8,128)(2,1)S(1)}, bf16[512,128]{1,0:T(8,128)(2,1)S(1)}, u32[]{:S(2)}, u32[]{:S(2)}) collective-permute-start(bf16[512,128]{1,0:T(8,128)(2,1)S(1)} %shard_map.88.refs_0_), channel_id=1, source_target_pairs={{0,64},{64,0},{1,65},{65,1},{2,66},{66,2},{3,67},{67,3},{4,68},{68... | collective-permute-start | bytes 393224 | tf_op jit(solution)/shard_map/ppermute | solution.py:225
  72.0 1.3 %collective-permute-start.10 = (bf16[512,128]{1,0:T(8,128)(2,1)S(1)}, bf16[512,128]{1,0:T(8,128)(2,1)S(1)}, u32[]{:S(2)}, u32[]{:S(2)}) collective-permute-start(bf16[512,128]{1,0:T(8,128)(2,1)S(1)} %collective-permute-done.6.refs_2_), channel_id=1, source_target_pairs={{0,64},{64,0},{1,65},{65,1},{2,66},{66,2},{3,67},{67,3},{4,68},{68... | collective-permute-start | bytes 393224 | tf_op jit(solution)/shard_map/ppermute | solution.py:225
  72.1 1.4 %collective-permute-start.11 = (bf16[512,128]{1,0:T(8,128)(2,1)S(1)}, bf16[512,128]{1,0:T(8,128)(2,1)S(1)}, u32[]{:S(2)}, u32[]{:S(2)}) collective-permute-start(bf16[512,128]{1,0:T(8,128)(2,1)S(1)} %collective-permute-done.7.refs_3_), channel_id=1, source_target_pairs={{0,64},{64,0},{1,65},{65,1},{2,66},{66,2},{3,67},{67,3},{4,68},{68... | collective-permute-start | bytes 393224 | tf_op jit(solution)/shard_map/ppermute | solution.py:225
  72.6 1.3 %collective-permute-start.9 = (bf16[512,128]{1,0:T(8,128)(2,1)S(1)}, bf16[512,128]{1,0:T(8,128)(2,1)S(1)}, u32[]{:S(2)}, u32[]{:S(2)}) collective-permute-start(bf16[512,128]{1,0:T(8,128)(2,1)S(1)} %collective-permute-done.5.refs_1_), channel_id=1, source_target_pairs={{0,64},{64,0},{1,65},{65,1},{2,66},{66,2},{3,67},{67,3},{4,68},{68... | collective-permute-start | bytes 393224 | tf_op jit(solution)/shard_map/ppermute | solution.py:225
  72.9 5.7 %collective-permute-start.17 = (bf16[512,128]{1,0:T(8,128)(2,1)S(1)}, bf16[512,128]{1,0:T(8,128)(2,1)S(1)}, u32[]{:S(2)}, u32[]{:S(2)}) collective-permute-start(bf16[512,128]{1,0:T(8,128)(2,1)S(1)} %get-tuple-element.67), channel_id=1, source_target_pairs={{0,128},{128,0},{1,129},{129,1},{2,130},{130,2},{3,131},{131,3},{4... | collective-permute-start | bytes 393224 | tf_op jit(solution)/shard_map/ppermute | solution.py:225
  78.7 7.7 %collective-permute-start.18 = (bf16[512,128]{1,0:T(8,128)(2,1)S(1)}, bf16[512,128]{1,0:T(8,128)(2,1)S(1)}, u32[]{:S(2)}, u32[]{:S(2)}) collective-permute-start(bf16[512,128]{1,0:T(8,128)(2,1)S(1)} %get-tuple-element.69.refs_0_), channel_id=1, source_target_pairs={{0,16},{16,32},{32,48},{48,0},{1,17},{17,33},{33,49},{49,1},{2,18}... | collective-permute-start | bytes 393224 | tf_op jit(solution)/shard_map/ppermute | solution.py:221
  79.7 8.6 %collective-permute-start.19 = (bf16[512,128]{1,0:T(8,128)(2,1)S(1)}, bf16[512,128]{1,0:T(8,128)(2,1)S(1)}, u32[]{:S(2)}, u32[]{:S(2)}) collective-permute-start(bf16[512,128]{1,0:T(8,128)(2,1)S(1)} %get-tuple-element.69.refs_0_), channel_id=1, source_target_pairs={{0,32},{16,48},{32,0},{48,16},{1,33},{17,49},{33,1},{49,17},{2,34}... | collective-permute-start | bytes 393224 | tf_op jit(solution)/shard_map/ppermute | solution.py:221
  82.8 5.6 %collective-permute-start.20 = (bf16[512,128]{1,0:T(8,128)(2,1)S(1)}, bf16[512,128]{1,0:T(8,128)(2,1)S(1)}, u32[]{:S(2)}, u32[]{:S(2)}) collective-permute-start(bf16[512,128]{1,0:T(8,128)(2,1)S(1)} %get-tuple-element.69.refs_0_), channel_id=1, source_target_pairs={{0,48},{16,0},{32,16},{48,32},{1,49},{17,1},{33,17},{49,33},{2,50}... | collective-permute-start | bytes 393224 | tf_op jit(solution)/shard_map/ppermute | solution.py:221
  84.4 4.4 %collective-permute-start.21 = (bf16[512,128]{1,0:T(8,128)(2,1)S(1)}, bf16[512,128]{1,0:T(8,128)(2,1)S(1)}, u32[]{:S(2)}, u32[]{:S(2)}) collective-permute-start(bf16[512,128]{1,0:T(8,128)(2,1)S(1)} %get-tuple-element.69.refs_0_), channel_id=1, source_target_pairs={{0,64},{64,0},{1,65},{65,1},{2,66},{66,2},{3,67},{67,3},{4,68},{68... | collective-permute-start | bytes 393224 | tf_op jit(solution)/shard_map/ppermute | solution.py:225
  86.4 2.4 %collective-permute-start.22 = (bf16[512,128]{1,0:T(8,128)(2,1)S(1)}, bf16[512,128]{1,0:T(8,128)(2,1)S(1)}, u32[]{:S(2)}, u32[]{:S(2)}) collective-permute-start(bf16[512,128]{1,0:T(8,128)(2,1)S(1)} %collective-permute-done.18.refs_1_), channel_id=1, source_target_pairs={{0,64},{64,0},{1,65},{65,1},{2,66},{66,2},{3,67},{67,3},{4,68},{68... | collective-permute-start | bytes 393224 | tf_op jit(solution)/shard_map/ppermute | solution.py:225
  88.3 1.3 %collective-permute-start.23 = (bf16[512,128]{1,0:T(8,128)(2,1)S(1)}, bf16[512,128]{1,0:T(8,128)(2,1)S(1)}, u32[]{:S(2)}, u32[]{:S(2)}) collective-permute-start(bf16[512,128]{1,0:T(8,128)(2,1)S(1)} %collective-permute-done.19.refs_2_), channel_id=1, source_target_pairs={{0,64},{64,0},{1,65},{65,1},{2,66},{66,2},{3,67},{67,3},{4,68},{68... | collective-permute-start | bytes 393224 | tf_op jit(solution)/shard_map/ppermute | solution.py:225
  88.4 1.5 %collective-permute-start.24 = (bf16[512,128]{1,0:T(8,128)(2,1)S(1)}, bf16[512,128]{1,0:T(8,128)(2,1)S(1)}, u32[]{:S(2)}, u32[]{:S(2)}) collective-permute-start(bf16[512,128]{1,0:T(8,128)(2,1)S(1)} %collective-permute-done.20.refs_3_), channel_id=1, source_target_pairs={{0,64},{64,0},{1,65},{65,1},{2,66},{66,2},{3,67},{67,3},{4,68},{68... | collective-permute-start | bytes 393224 | tf_op jit(solution)/shard_map/ppermute | solution.py:225
  91.1 8.2 %collective-permute-start.25 = (bf16[128,128]{1,0:T(8,128)(2,1)S(1)}, bf16[128,128]{1,0:T(8,128)(2,1)S(1)}, u32[]{:S(2)}, u32[]{:S(2)}) collective-permute-start(bf16[128,128]{1,0:T(8,128)(2,1)S(1)} %get-tuple-element.71), channel_id=1, source_target_pairs={{0,2},{2,4},{4,6},{6,0},{1,3},{3,5},{5,7},{7,1},{8,10},{10,12},{12... | collective-permute-start | bytes 98312 | tf_op jit(solution)/shard_map/ppermute | solution.py:221
  94.7 8.2 %collective-permute-start.26 = (bf16[128,128]{1,0:T(8,128)(2,1)S(1)}, bf16[128,128]{1,0:T(8,128)(2,1)S(1)}, u32[]{:S(2)}, u32[]{:S(2)}) collective-permute-start(bf16[128,128]{1,0:T(8,128)(2,1)S(1)} %get-tuple-element.72), channel_id=1, source_target_pairs={{0,4},{2,6},{4,0},{6,2},{1,5},{3,7},{5,1},{7,3},{8,12},{10,14},{12... | collective-permute-start | bytes 98312 | tf_op jit(solution)/shard_map/ppermute | solution.py:221
  95.2 7.6 %collective-permute-start.27 = (bf16[128,128]{1,0:T(8,128)(2,1)S(1)}, bf16[128,128]{1,0:T(8,128)(2,1)S(1)}, u32[]{:S(2)}, u32[]{:S(2)}) collective-permute-start(bf16[128,128]{1,0:T(8,128)(2,1)S(1)} %get-tuple-element.73), channel_id=1, source_target_pairs={{0,6},{2,0},{4,2},{6,4},{1,7},{3,1},{5,3},{7,5},{8,14},{10,8},{12,... | collective-permute-start | bytes 98312 | tf_op jit(solution)/shard_map/ppermute | solution.py:221
  102.9 7.7 %collective-permute-start.28 = (bf16[4,128,128]{2,1,0:T(8,128)(2,1)S(1)}, bf16[4,128,128]{2,1,0:T(8,128)(2,1)S(1)}, u32[]{:S(2)}, u32[]{:S(2)}) collective-permute-start(bf16[4,128,128]{2,1,0:T(8,128)(2,1)S(1)} %pad_maximum_fusion), channel_id=1, source_target_pairs={{0,0},{2,2},{4,4},{6,6},{1,64},{3,66},{5,68},{7,70},{8,128},{10,13... | collective-permute-start | bytes 393224 | tf_op jit(solution)/shard_map/ppermute | solution.py:217

commit v3 on v2

--- a/solution.py
+++ b/solution.py
@@ -15,9 +15,10 @@
 VM = pl.BlockSpec(memory_space=pltpu.VMEM)
 SM = pl.BlockSpec(memory_space=pltpu.SMEM)
 ANY = pl.BlockSpec(memory_space=pltpu.HBM)
-
-
-def call(body, outs, operands, specs=None, out_specs=None, vmem=16, flops=0, scratch=()):
+ANYWHERE = pl.BlockSpec(memory_space=pl.ANY)
+
+
+def call(body, outs, operands, specs=None, out_specs=None, vmem=16, flops=0, scratch=(), aliases={}):
     moved = sum(o.size * o.dtype.itemsize for o in [*operands, *outs])
     return pl.pallas_call(
         body,
@@ -25,6 +26,7 @@
         in_specs=specs or [VM] * len(operands),
         out_specs=out_specs or [VM] * len(outs),
         scratch_shapes=list(scratch),
+        input_output_aliases=aliases,
         compiler_params=pltpu.CompilerParams(vmem_limit_bytes=vmem * MIB),
         cost_estimate=pl.CostEstimate(flops=flops, bytes_accessed=moved, transcendentals=0),
     )(*operands)
@@ -89,7 +91,7 @@
         q_ref[pl.ds(pl.multiple_of(first, 64), 64)] = ref[128:192]
 
 
-def unpack_kernel(in_ref, after_ref, kv_ref, q_ref, factor_ref):
+def unpack_kernel(in_ref, after_ref, k_ref, v_ref, q_ref, factor_ref):
     del after_ref
     lane = lax.broadcasted_iota(jnp.int32, (64, 128), 1)
     sub = lax.broadcasted_iota(jnp.int32, (64, 128), 0)
@@ -97,9 +99,8 @@
         yh, zt, zp = place // 8, place // 2 % 4, place % 2
         t = (yh * 2 + zp) * 4 + zt
         rows = slice(t * 64, (t + 1) * 64)
-        first = t // 8 * 1024 + t % 8 * 64
-        kv_ref[first : first + 64] = in_ref[place, 0:64]
-        kv_ref[first + 512 : first + 576] = in_ref[place, 64:128]
+        k_ref[rows] = in_ref[place, 0:64]
+        v_ref[rows] = in_ref[place, 64:128]
         q_ref[rows] = in_ref[place, 128:192]
         code = in_ref[place, 192:208].astype(F32)[0:1]
         code = jnp.broadcast_to(code, (64, 128))
@@ -108,17 +109,21 @@
 
 
 def score_kernel(q_ref, *refs):
-    halves, (p_ref, m_ref, l_ref) = refs[:-3], refs[-3:]
-    keys = [halves[0], halves[-1]]
-    starts = (0, 0 if len(halves) == 2 else 1024)
+    keys, (p_ref, m_ref, l_ref) = refs[:-3], refs[-3:]
     for i in range(4):
         rows = slice(i * 256, (i + 1) * 256)
-        s = jnp.concatenate([dot_nt(q_ref[rows], k[a : a + 512]) for k, a in zip(keys, starts)], axis=1)
+        parts = [dot_nt(q_ref[rows], k[...]) for k in keys]
+        s = jnp.concatenate(parts, axis=1) if len(parts) > 1 else parts[0]
         m = jnp.max(s, axis=1, keepdims=True)
         p = jnp.exp2((s - m) * SCALE2)
         m_ref[rows] = m
         l_ref[rows] = jnp.sum(p, axis=1, keepdims=True)
         p_ref[rows] = p.astype(BF)
+
+
+def own_score_kernel(q_ref, k_ref, v_ref, p_ref, m_ref, l_ref, same_v_ref):
+    del v_ref, same_v_ref
+    score_kernel(q_ref, k_ref, p_ref, m_ref, l_ref)
 
 
 def merge(rows, ms, ls):
@@ -135,10 +140,7 @@
         best, weights, total = merge(rows, ms, ls)
         m_ref[rows] = best
         l_ref[rows] = total
-        acc_ref[rows] = sum(
-            (dot_nn(p[rows, 0:512], v[512:1024]) + dot_nn(p[rows, 512:1024], v[1536:2048])) * w
-            for p, v, w in zip(ps, vs, weights)
-        )
+        acc_ref[rows] = sum(dot_nn(p[rows], v[...]) * w for p, v, w in zip(ps, vs, weights))
 
 
 def finish_kernel(at_ref, factor_ref, *refs):
@@ -147,7 +149,7 @@
     for chunk, out, place in ((1, give_ref, 0), (3, give_ref, 1), (0, keep_ref, 0), (2, keep_ref, 1)):
         rows = pl.ds(pl.multiple_of((b ^ chunk) * 256, 256), 256)
         _, weights, total = merge(rows, ms, ls)
-        far = dot_nn(p_ref[rows, 0:512], va_ref[512:1024]) + dot_nn(p_ref[rows, 512:1024], vb_ref[512:1024])
+        far = dot_nn(p_ref[rows, 0:512], va_ref[...]) + dot_nn(p_ref[rows, 512:1024], vb_ref[...])
         acc = acc_ref[rows] * weights[0] + far * weights[1]
         acc = acc / total * factor_ref[rows]
         out[place * 256 : place * 256 + 256] = acc.astype(out.dtype)
@@ -199,12 +201,13 @@
         out[64:128] = held[rows]
 
 
-def home_kernel(at_ref, in_ref, joined_ref, out_ref):
+def home_kernel(at_ref, *refs):
+    joined_ref, out_ref = refs[4:]
     for step in range(4):
         head = (at_ref[3] + 4 - step) & 3
         cols = pl.ds(pl.multiple_of(head * DIM, DIM), DIM)
-        joined_ref[:, cols] = in_ref[step, 0:64].astype(F32)
-        out_ref[:, cols] = in_ref[step, 64:128]
+        joined_ref[:, cols] = refs[step][0:64].astype(F32)
+        out_ref[:, cols] = refs[step][64:128]
 
 
 def swap(values, step=0):
@@ -258,11 +261,27 @@
     base_kv, base_quer = call(
         base_unpack_kernel, [sds((512, DIM)), sds((256, DIM))], [at, *parts], specs=[SM] + [VM] * 4
     )
-    own, quer, factor = call(
-        unpack_kernel, [sds((2048, DIM)), sds((1024, DIM)), sds((1024, 1), F32)], [sent, base_quer], specs=[VM, pl.BlockSpec(memory_space=pl.ANY)]
-    )
-    after, before = along("x", own, 1), along("x", own, 3)
-    far = [along("x", after[:1024], 1), along("x", before[1024:], 3)]
+    own_k, own_v, quer, factor = call(
+        unpack_kernel,
+        [sds((1024, DIM))] * 3 + [sds((1024, 1), F32)],
+        [sent, base_quer],
+        specs=[VM, ANYWHERE],
+    )
+    outs = [sds((1024, 1024)), sds((1024, 1), F32), sds((1024, 1), F32)]
+    after_k, before_k = along("x", own_k, 1), along("x", own_k, 3)
+    *own_score, own_v = call(
+        own_score_kernel,
+        outs + [sds((1024, DIM))],
+        [quer, own_k, own_v],
+        specs=[VM, VM, ANYWHERE],
+        out_specs=[VM] * 3 + [ANYWHERE],
+        vmem=24,
+        flops=2 * 1024 * 1024 * 128,
+        aliases={2: 3},
+    )
+    after_v, before_v = along("x", own_v, 1), along("x", own_v, 3)
+    far_k = [along("x", after_k[:512], 1), along("x", before_k[512:], 3)]
+    far_v = [along("x", after_v[:512], 1), along("x", before_v[512:], 3)]
 
     more_kv = other(base_kv, "yl")
     (base_pair,) = call(
@@ -279,23 +298,22 @@
         flops=2 * 256 * 4096 * 128,
     )
 
-    outs = [sds((1024, 1024)), sds((1024, 1), F32), sds((1024, 1), F32)]
-    scored = [
-        call(score_kernel, outs, [quer, kv], vmem=24, flops=2 * 1024 * 1024 * 128) for kv in (own, after, before)
+    scored = [own_score] + [
+        call(score_kernel, outs, [quer, k], vmem=24, flops=2 * 1024 * 1024 * 128) for k in (after_k, before_k)
     ]
     ps, ms, ls = zip(*scored)
     m, l, acc = call(
         middle_kernel,
         [sds((1024, 1), F32), sds((1024, 1), F32), sds((1024, DIM), F32)],
-        [*ms, *ls, *ps, own, after, before],
+        [*ms, *ls, *ps, own_v, after_v, before_v],
         vmem=24,
         flops=3 * 2 * 1024 * 1024 * 128,
     )
-    far_p, far_m, far_l = call(score_kernel, outs, [quer, *far], vmem=24, flops=2 * 1024 * 1024 * 128)
+    far_p, far_m, far_l = call(score_kernel, outs, [quer, *far_k], vmem=24, flops=2 * 1024 * 1024 * 128)
     keep, give = call(
         finish_kernel,
         [sds((512, DIM), F32), sds((512, DIM))],
-        [at, factor, m, far_m, l, far_l, acc, far_p, *far],
+        [at, factor, m, far_m, l, far_l, acc, far_p, *far_v],
         specs=[SM] + [VM] * 9,
         vmem=24,
         flops=2 * 1024 * 1024 * 128,
@@ -303,7 +321,7 @@
 
     pair, send = call(pair_kernel, [sds((512, DIM), F32), sds((512, DIM))], [keep, other(give, "co")])
     joined, base_values = call(
-        join_kernel, [sds((256, DIM)), sds((512, DIM))], [pair, other(send, "yl"), base_kv, more_kv, base_l], specs=[VM] * 4 + [pl.BlockSpec(memory_space=pl.ANY)]
+        join_kernel, [sds((256, DIM)), sds((512, DIM))], [pair, other(send, "yl"), base_kv, more_kv, base_l], specs=[VM] * 4 + [ANYWHERE]
     )
 
     outs = call(
@@ -314,11 +332,10 @@
         flops=2 * 256 * 4096 * 128,
         scratch=[pltpu.VMEM((256, DIM), BF)],
     )
-    result = [outs[0]] + [None] * 3
-    for step in (1, 3, 2):
-        result[step] = along("zt", outs[step], step)
-    result = swap(jnp.stack(result))
-    return call(home_kernel, [sds((64, 512), F32), sds((64, 512))], [at, result], specs=[SM, VM])
+    result = [None] * 4
+    for step in (0, 1, 3, 2):
+        result[step] = swap(outs[step], step)
+    return call(home_kernel, [sds((64, 512), F32), sds((64, 512))], [at, *result], specs=[SM] + [VM] * 4)
 
 
 def solution(mesh):

time: 112 us -> 109 us (0.973)
  waiting for transfers between devices: 42.3 us -> 31.6 us
  starting transfers between devices: 52.7 us -> 59.9 us
    ppermute x13 -> x14, waiting for transfers between devices: 17.3 us -> 8.26 us  [along(): return lax.ppermute(values, axis, [(j, (j + step) % 4) for j in range(4)])]
    ppermute x5 -> x8, starting transfers between devices: 16.8 us -> 24.5 us  [swap(): return lax.ppermute(values, ('yl', 'co', 'yh', 'zt', 'zp'), perm)]
    ppermute x5 -> x8, waiting for transfers between devices: 19.8 us -> 18.2 us  [swap(): return lax.ppermute(values, ('yl', 'co', 'yh', 'zt', 'zp'), perm)]
    ppermute x13 -> x14, starting transfers between devices: 23.5 us -> 22.6 us  [along(): return lax.ppermute(values, axis, [(j, (j + step) % 4) for j in range(4)])]
  transfers between devices with their start and end apart: 30 -> 34, of which waited for: 15 -> 14; matrix products, arithmetic and copies ran while one was open for 0% -> 0% of each run, Pallas kernels for 9% -> 10%
where the time goes in v3:
time: 109 us
  starting transfers between devices  59.9 us (55%)
  waiting for transfers between devices  31.6 us (29%)
  Pallas kernels  16.1 us (15%)
    ppermute x8, starting transfers between devices, swap(): return lax.ppermute(values, ('yl', 'co', 'yh', 'zt', 'zp'), perm)  24.5 us
    ppermute x14, starting transfers between devices, along(): return lax.ppermute(values, axis, [(j, (j + step) % 4) for j in range(4)])  22.6 us
    ppermute x8, waiting for transfers between devices, swap(): return lax.ppermute(values, ('yl', 'co', 'yh', 'zt', 'zp'), perm)  18.2 us
    pallas_call x16, Pallas kernels, call(): pl.pallas_call(body, out_shape=outs, in_specs=specs or [VM] * len(operand...  16.1 us
    all_to_all x1, starting transfers between devices, shards(): sent = lax.all_to_all(packed, ('yh', 'zt', 'zp'), 0, 0, tiled=True)  10.3 us
    ppermute x14, waiting for transfers between devices, along(): return lax.ppermute(values, axis, [(j, (j + step) % 4) for j in range(4)])  8.26 us
    ppermute x11, waiting for transfers between devices, other(): return lax.ppermute(values, axis, [(0, 1), (1, 0)])  5.18 us
    ppermute x11, starting transfers between devices, other(): return lax.ppermute(values, axis, [(0, 1), (1, 0)])  2.56 us
  transfers between devices with their start and end apart: 34, of which 14 were waited for; matrix products, arithmetic and copies ran while one was open for 0% of the time, Pallas kernels for 10%

profile of v3, /device:TPU:8, one launch (start us, length us, event | category | flops | bytes accessed | tf_op | source)
XLA Modules:
  0.0 108.6 jit_solution(5270339379667908068)
XLA Ops:
  0.7 2.5 %shard_map.90 = bf16[16,208,128]{2,1,0:T(8,128)(2,1)} custom-call(bf16[1,64,2048]{2,1,0:T(8,128)(2,1)} %k_ref.3, bf16[1,64,2048]{2,1,0:T(8,128)(2,1)} %v_ref.3, bf16[1,64,2048]{2,1,0:T(8,128)(2,1)} %q_ref.3, s32[1,64]{1,0:T(1,128)} %code_ref.1), custom_call_target="tpu_custom_call" | custom-call | bytes 1638656 | tf_op jit(solution)/shard_map/pallas_call | solution.py:23
  3.2 10.3 %all-to-all-start = ((bf16[16,208,128]{2,1,0:T(8,128)(2,1)}), bf16[16,208,128]{2,1,0:T(8,128)(2,1)S(1)}, u32[]{:S(2)}, u32[]{:S(2)}) async-start(bf16[16,208,128]{2,1,0:T(8,128)(2,1)} %shard_map.90), calls=%async_computation | async-start | bytes 1703936 | tf_op jit(solution)/shard_map/all_to_all | solution.py:250
  13.6 0.7 shard_map.86
  14.3 4.6 %collective-permute-start = (bf16[192,128]{1,0:T(8,128)(2,1)S(1)}, bf16[192,128]{1,0:T(8,128)(2,1)S(1)}, u32[]{:S(2)}, u32[]{:S(2)}) collective-permute-start(bf16[192,128]{1,0:T(8,128)(2,1)S(1)} %get-tuple-element.40), channel_id=1, source_target_pairs={{0,0},{2,2},{4,4},{6,6},{1,64},{3,66},{5,68},{7,70},{8,128},{10,13... | collective-permute-start | bytes 147464 | tf_op jit(solution)/shard_map/ppermute | solution.py:220
  18.9 1.9 %collective-permute-start.1 = (bf16[192,128]{1,0:T(8,128)(2,1)S(1)}, bf16[192,128]{1,0:T(8,128)(2,1)S(1)}, u32[]{:S(2)}, u32[]{:S(2)}) collective-permute-start(bf16[192,128]{1,0:T(8,128)(2,1)S(1)} %get-tuple-element.41), channel_id=1, source_target_pairs={{0,2},{2,4},{4,6},{6,0},{1,66},{3,68},{5,70},{7,64},{8,130},{10,13... | collective-permute-start | bytes 147464 | tf_op jit(solution)/shard_map/ppermute | solution.py:220
  20.8 5.0 %collective-permute-start.2 = (bf16[192,128]{1,0:T(8,128)(2,1)S(1)}, bf16[192,128]{1,0:T(8,128)(2,1)S(1)}, u32[]{:S(2)}, u32[]{:S(2)}) collective-permute-start(bf16[192,128]{1,0:T(8,128)(2,1)S(1)} %get-tuple-element.42), channel_id=1, source_target_pairs={{0,4},{2,6},{4,0},{6,2},{1,68},{3,70},{5,64},{7,66},{8,132},{10,13... | collective-permute-start | bytes 147464 | tf_op jit(solution)/shard_map/ppermute | solution.py:220
  25.9 3.0 %collective-permute-start.3 = (bf16[192,128]{1,0:T(8,128)(2,1)S(1)}, bf16[192,128]{1,0:T(8,128)(2,1)S(1)}, u32[]{:S(2)}, u32[]{:S(2)}) collective-permute-start(bf16[192,128]{1,0:T(8,128)(2,1)S(1)} %get-tuple-element.43), channel_id=1, source_target_pairs={{0,6},{2,0},{4,2},{6,4},{1,70},{3,64},{5,66},{7,68},{8,134},{10,12... | collective-permute-start | bytes 147464 | tf_op jit(solution)/shard_map/ppermute | solution.py:220
  28.9 12.4 %collective-permute-done.1.refs_1_ = bf16[192,128]{1,0:T(8,128)(2,1)S(1)} collective-permute-done((bf16[192,128]{1,0:T(8,128)(2,1)S(1)}, bf16[192,128]{1,0:T(8,128)(2,1)S(1)}, u32[]{:S(2)}, u32[]{:S(2)}) %collective-permute-start.1) | collective-permute-done | bytes 49184 | tf_op jit(solution)/shard_map/ppermute | solution.py:220
  41.3 2.0 %collective-permute-done.2.refs_2_ = bf16[192,128]{1,0:T(8,128)(2,1)S(1)} collective-permute-done((bf16[192,128]{1,0:T(8,128)(2,1)S(1)}, bf16[192,128]{1,0:T(8,128)(2,1)S(1)}, u32[]{:S(2)}, u32[]{:S(2)}) %collective-permute-start.2) | collective-permute-done | bytes 49184 | tf_op jit(solution)/shard_map/ppermute | solution.py:220
  43.3 0.6 shard_map.87
  44.1 1.6 %collective-permute-start.12 = (bf16[1024,128]{1,0:T(8,128)(2,1)S(1)}, bf16[1024,128]{1,0:T(8,128)(2,1)S(1)}, u32[]{:S(2)}, u32[]{:S(2)}) collective-permute-start(bf16[1024,128]{1,0:T(8,128)(2,1)S(1)} %get-tuple-element.50.k_ref), channel_id=1, source_target_pairs={{0,16},{16,32},{32,48},{48,0},{1,17},{17,33},{33,49},{49,1},{2,18}... | collective-permute-start | bytes 786440 | tf_op jit(solution)/shard_map/ppermute | solution.py:224
  45.7 1.7 %collective-permute-start.13 = (bf16[1024,128]{1,0:T(8,128)(2,1)S(1)}, bf16[1024,128]{1,0:T(8,128)(2,1)S(1)}, u32[]{:S(2)}, u32[]{:S(2)}) collective-permute-start(bf16[1024,128]{1,0:T(8,128)(2,1)S(1)} %get-tuple-element.50.k_ref), channel_id=1, source_target_pairs={{0,48},{16,0},{32,16},{48,32},{1,49},{17,1},{33,17},{49,33},{2,50}... | collective-permute-start | bytes 786440 | tf_op jit(solution)/shard_map/ppermute | solution.py:224
  47.4 1.2 %shard_map.92 = (bf16[1024,1024]{1,0:T(8,128)(2,1)S(1)}, f32[1024,1]{1,0:T(8,128)S(1)}, f32[1024,1]{1,0:T(8,128)S(1)}, bf16[1024,128]{1,0:T(8,128)(2,1)S(1)}) custom-call(bf16[1024,128]{1,0:T(8,128)(2,1)S(1)} %get-tuple-element.49.q_ref, bf16[1024,128]{1,0:T(8,128)(2,1)S(1)} %get-tuple-element.50.k_ref, ...), custom_call_target="tpu_custom_call", output_to_operand_aliasing={{3}: (2, {})} | custom-call | flops 268435456 | bytes 3153920 | tf_op jit(solution)/shard_map/pallas_call | solution.py:23
  49.0 3.0 %collective-permute-start.15 = (bf16[1024,128]{1,0:T(8,128)(2,1)S(1)}, bf16[1024,128]{1,0:T(8,128)(2,1)S(1)}, u32[]{:S(2)}, u32[]{:S(2)}) collective-permute-start(bf16[1024,128]{1,0:T(8,128)(2,1)S(1)} %get-tuple-element.61.refs_9_), channel_id=1, source_target_pairs={{0,48},{16,0},{32,16},{48,32},{1,49},{17,1},{33,17},{49,33},{2,50}... | collective-permute-start | bytes 786440 | tf_op jit(solution)/shard_map/ppermute | solution.py:224
  52.1 1.4 %collective-permute-done.12.refs_0_ = bf16[1024,128]{1,0:T(8,128)(2,1)S(1)} collective-permute-done((bf16[1024,128]{1,0:T(8,128)(2,1)S(1)}, bf16[1024,128]{1,0:T(8,128)(2,1)S(1)}, u32[]{:S(2)}, u32[]{:S(2)}) %collective-permute-start.12) | collective-permute-done | bytes 262176 | tf_op jit(solution)/shard_map/ppermute | solution.py:224
  53.6 1.5 %collective-permute-start.16 = (bf16[512,128]{1,0:T(8,128)(2,1)S(1)}, bf16[512,128]{1,0:T(8,128)(2,1)S(1)}, u32[]{:S(2)}, u32[]{:S(2)}) collective-permute-start(bf16[512,128]{1,0:T(8,128)(2,1)S(1)} %slice.16), channel_id=1, source_target_pairs={{0,16},{16,32},{32,48},{48,0},{1,17},{17,33},{33,49},{49,1},{2,18}... | collective-permute-start | bytes 393224 | tf_op jit(solution)/shard_map/ppermute | solution.py:224
  55.0 2.2 %collective-permute-start.17 = (bf16[512,128]{1,0:T(8,128)(2,1)S(1)}, bf16[512,128]{1,0:T(8,128)(2,1)S(1)}, u32[]{:S(2)}, u32[]{:S(2)}) collective-permute-start(bf16[512,128]{1,0:T(8,128)(2,1)S(1)} %slice.17), channel_id=1, source_target_pairs={{0,48},{16,0},{32,16},{48,32},{1,49},{17,1},{33,17},{49,33},{2,50}... | collective-permute-start | bytes 393224 | tf_op jit(solution)/shard_map/ppermute | solution.py:224
  57.2 1.6 %collective-permute-start.6 = (bf16[512,128]{1,0:T(8,128)(2,1)S(1)}, bf16[512,128]{1,0:T(8,128)(2,1)S(1)}, u32[]{:S(2)}, u32[]{:S(2)}) collective-permute-start(bf16[512,128]{1,0:T(8,128)(2,1)S(1)} %shard_map.88.refs_0_), channel_id=1, source_target_pairs={{0,32},{16,48},{32,0},{48,16},{1,33},{17,49},{33,1},{49,17},{2,34}... | collective-permute-start | bytes 393224 | tf_op jit(solution)/shard_map/ppermute | solution.py:224
  58.8 0.7 collective-permute-done.14.refs_10_
  59.5 1.5 %collective-permute-start.18 = (bf16[512,128]{1,0:T(8,128)(2,1)S(1)}, bf16[512,128]{1,0:T(8,128)(2,1)S(1)}, u32[]{:S(2)}, u32[]{:S(2)}) collective-permute-start(bf16[512,128]{1,0:T(8,128)(2,1)S(1)} %slice.18), channel_id=1, source_target_pairs={{0,16},{16,32},{32,48},{48,0},{1,17},{17,33},{33,49},{49,1},{2,18}... | collective-permute-start | bytes 393224 | tf_op jit(solution)/shard_map/ppermute | solution.py:224
  60.9 3.3 %collective-permute-start.19 = (bf16[512,128]{1,0:T(8,128)(2,1)S(1)}, bf16[512,128]{1,0:T(8,128)(2,1)S(1)}, u32[]{:S(2)}, u32[]{:S(2)}) collective-permute-start(bf16[512,128]{1,0:T(8,128)(2,1)S(1)} %slice.19), channel_id=1, source_target_pairs={{0,48},{16,0},{32,16},{48,32},{1,49},{17,1},{33,17},{49,33},{2,50}... | collective-permute-start | bytes 393224 | tf_op jit(solution)/shard_map/ppermute | solution.py:224
  64.2 1.2 %shard_map.93 = (bf16[1024,1024]{1,0:T(8,128)(2,1)S(1)}, f32[1024,1]{1,0:T(8,128)S(1)}, f32[1024,1]{1,0:T(8,128)S(1)}) custom-call(bf16[1024,128]{1,0:T(8,128)(2,1)S(1)} %get-tuple-element.49.q_ref, bf16[1024,128]{1,0:T(8,128)(2,1)S(1)} %collective-permute-done.12.refs_0_), custom_call_target="tpu_custom_call" | custom-call | flops 268435456 | bytes 2629632 | tf_op jit(solution)/shard_map/pallas_call | solution.py:23
  65.4 1.2 %shard_map.94 = (bf16[1024,1024]{1,0:T(8,128)(2,1)S(1)}, f32[1024,1]{1,0:T(8,128)S(1)}, f32[1024,1]{1,0:T(8,128)S(1)}) custom-call(bf16[1024,128]{1,0:T(8,128)(2,1)S(1)} %get-tuple-element.49.q_ref, bf16[1024,128]{1,0:T(8,128)(2,1)S(1)} %collective-permute-done.13.refs_0_), custom_call_target="tpu_custom_call" | custom-call | flops 268435456 | bytes 2629632 | tf_op jit(solution)/shard_map/pallas_call | solution.py:23
  66.6 1.9 %shard_map.95 = (f32[1024,1]{1,0:T(8,128)S(1)}, f32[1024,1]{1,0:T(8,128)S(1)}, f32[1024,128]{1,0:T(8,128)S(1)}) custom-call(f32[1024,1]{1,0:T(8,128)S(1)} %get-tuple-element.52.refs_0_, f32[1024,1]{1,0:T(8,128)S(1)} %get-tuple-element.53.refs_1_, f32[1024,1]{1,0:T(8,128)S(1)} %get-tuple-element.54.refs_2_, f32[1024,1]{1,0:T(8,128)S(1)} %get-tuple-element.55.refs_3_, ...), custom_call_target="tpu_custom_call" | custom-call | flops 805306368 | bytes 7634944 | tf_op jit(solution)/shard_map/pallas_call | solution.py:23
  68.7 1.9 %collective-permute-start.5 = (bf16[512,128]{1,0:T(8,128)(2,1)S(1)}, bf16[512,128]{1,0:T(8,128)(2,1)S(1)}, u32[]{:S(2)}, u32[]{:S(2)}) collective-permute-start(bf16[512,128]{1,0:T(8,128)(2,1)S(1)} %shard_map.88.refs_0_), channel_id=1, source_target_pairs={{0,16},{16,32},{32,48},{48,0},{1,17},{17,33},{33,49},{49,1},{2,18}... | collective-permute-start | bytes 393224 | tf_op jit(solution)/shard_map/ppermute | solution.py:224
  70.7 1.2 %shard_map.96 = (bf16[1024,1024]{1,0:T(8,128)(2,1)S(1)}, f32[1024,1]{1,0:T(8,128)S(1)}, f32[1024,1]{1,0:T(8,128)S(1)}) custom-call(bf16[1024,128]{1,0:T(8,128)(2,1)S(1)} %get-tuple-element.49.q_ref, bf16[512,128]{1,0:T(8,128)(2,1)S(1)} %collective-permute-done.16.refs_0_, bf16[512,128]{1,0:T(8,128)(2,1)S(1)} %collective-permute-done.17.refs_1_), custom_call_target="tpu_custom_call" | custom-call | flops 268435456 | bytes 2629632 | tf_op jit(solution)/shard_map/pallas_call | solution.py:23
  71.9 1.4 %shard_map.97 = (f32[512,128]{1,0:T(8,128)S(1)}, bf16[512,128]{1,0:T(8,128)(2,1)S(1)}) custom-call(s32[4]{0:T(128)S(1)} %pad_add_fusion.at_ref, f32[1024,1]{1,0:T(8,128)S(1)} %get-tuple-element.48.factor_ref, f32[1024,1]{1,0:T(8,128)S(1)} %get-tuple-element.62.refs_0_, f32[1024,1]{1,0:T(8,128)S(1)} %get-tuple-element.63.refs_1_, ...), custom_call_target="tpu_custom_call" | custom-call | flops 268435456 | bytes 3297296 | tf_op jit(solution)/shard_map/pallas_call | solution.py:23
  73.4 0.5 collective-permute-start.8
  74.0 0.4 collective-permute-start.11
  74.4 0.5 collective-permute-done.5.refs_1_
  75.0 0.8 collective-permute-start.21
  75.7 0.5 collective-permute-done.9.refs_5_
  76.3 1.4 %shard_map.89 = (bf16[8,256,512]{2,1,0:T(8,128)(2,1)S(1)}, f32[256,1]{1,0:T(8,128)S(1)}) custom-call(bf16[256,128]{1,0:T(8,128)(2,1)S(1)} %get-tuple-element.44.q_ref.after_ref, bf16[512,128]{1,0:T(8,128)(2,1)S(1)} %shard_map.88.refs_0_, bf16[512,128]{1,0:T(8,128)(2,1)S(1)} %collective-permute-done.5.refs_1_, ...), custom_call_target="tpu_custom_call" | custom-call | flops 268435456 | bytes 3212288 | tf_op jit(solution)/shard_map/pallas_call | solution.py:23
  77.7 3.3 %collective-permute-done.21.got_ref = bf16[512,128]{1,0:T(8,128)(2,1)S(1)} collective-permute-done((bf16[512,128]{1,0:T(8,128)(2,1)S(1)}, bf16[512,128]{1,0:T(8,128)(2,1)S(1)}, u32[]{:S(2)}, u32[]{:S(2)}) %collective-permute-start.21) | collective-permute-done | bytes 131104 | tf_op jit(solution)/shard_map/ppermute | solution.py:228
  81.0 1.0 collective-permute-start.22
  82.0 1.5 %collective-permute-start.23 = (bf16[512,128]{1,0:T(8,128)(2,1)S(1)}, bf16[512,128]{1,0:T(8,128)(2,1)S(1)}, u32[]{:S(2)}, u32[]{:S(2)}) collective-permute-start(bf16[512,128]{1,0:T(8,128)(2,1)S(1)} %get-tuple-element.73.refs_0_), channel_id=1, source_target_pairs={{0,32},{16,48},{32,0},{48,16},{1,33},{17,49},{33,1},{49,17},{2,34}... | collective-permute-start | bytes 393224 | tf_op jit(solution)/shard_map/ppermute | solution.py:224
  83.6 1.4 %collective-permute-start.24 = (bf16[512,128]{1,0:T(8,128)(2,1)S(1)}, bf16[512,128]{1,0:T(8,128)(2,1)S(1)}, u32[]{:S(2)}, u32[]{:S(2)}) collective-permute-start(bf16[512,128]{1,0:T(8,128)(2,1)S(1)} %get-tuple-element.73.refs_0_), channel_id=1, source_target_pairs={{0,48},{16,0},{32,16},{48,32},{1,49},{17,1},{33,17},{49,33},{2,50}... | collective-permute-start | bytes 393224 | tf_op jit(solution)/shard_map/ppermute | solution.py:224
  84.9 5.5 %collective-permute-done.22.refs_1_ = bf16[512,128]{1,0:T(8,128)(2,1)S(1)} collective-permute-done((bf16[512,128]{1,0:T(8,128)(2,1)S(1)}, bf16[512,128]{1,0:T(8,128)(2,1)S(1)}, u32[]{:S(2)}, u32[]{:S(2)}) %collective-permute-start.22) | collective-permute-done | bytes 131104 | tf_op jit(solution)/shard_map/ppermute | solution.py:224
  90.5 0.5 collective-permute-start.27
  91.1 0.7 collective-permute-done.26.refs_5_
  92.0 0.4 collective-permute-done.28.refs_7_
  92.4 1.2 %shard_map.100 = (bf16[128,128]{1,0:T(8,128)(2,1)S(1)}, bf16[128,128]{1,0:T(8,128)(2,1)S(1)}, bf16[128,128]{1,0:T(8,128)(2,1)S(1)}, bf16[128,128]{1,0:T(8,128)(2,1)S(1)}) custom-call(s32[4]{0:T(128)S(1)} %pad_add_fusion.at_ref, bf16[8,256,512]{2,1,0:T(8,128)(2,1)S(1)} %get-tuple-element.46.p_ref, f32[256,1]{1,0:T(8,128)S(1)} %get-tuple-element.47.after_ref.l_ref, ...), custom_call_target="tpu_custom_call" | custom-call | flops 268435456 | bytes 3343376 | tf_op jit(solution)/shard_map/pallas_call | solution.py:23
  93.7 2.9 %collective-permute-start.29 = (bf16[128,128]{1,0:T(8,128)(2,1)S(1)}, bf16[128,128]{1,0:T(8,128)(2,1)S(1)}, u32[]{:S(2)}, u32[]{:S(2)}) collective-permute-start(bf16[128,128]{1,0:T(8,128)(2,1)S(1)} %get-tuple-element.74), channel_id=1, source_target_pairs={{0,0},{2,2},{4,4},{6,6},{1,64},{3,66},{5,68},{7,70},{8,128},{10,13... | collective-permute-start | bytes 98312 | tf_op jit(solution)/shard_map/ppermute | solution.py:220
  96.6 1.5 %collective-permute-start.30 = (bf16[128,128]{1,0:T(8,128)(2,1)S(1)}, bf16[128,128]{1,0:T(8,128)(2,1)S(1)}, u32[]{:S(2)}, u32[]{:S(2)}) collective-permute-start(bf16[128,128]{1,0:T(8,128)(2,1)S(1)} %get-tuple-element.75), channel_id=1, source_target_pairs={{0,2},{2,4},{4,6},{6,0},{1,66},{3,68},{5,70},{7,64},{8,130},{10,13... | collective-permute-start | bytes 98312 | tf_op jit(solution)/shard_map/ppermute | solution.py:220
  98.1 2.4 %collective-permute-start.31 = (bf16[128,128]{1,0:T(8,128)(2,1)S(1)}, bf16[128,128]{1,0:T(8,128)(2,1)S(1)}, u32[]{:S(2)}, u32[]{:S(2)}) collective-permute-start(bf16[128,128]{1,0:T(8,128)(2,1)S(1)} %get-tuple-element.76), channel_id=1, source_target_pairs={{0,4},{2,6},{4,0},{6,2},{1,68},{3,70},{5,64},{7,66},{8,132},{10,13... | collective-permute-start | bytes 98312 | tf_op jit(solution)/shard_map/ppermute | solution.py:220
  100.6 3.0 %collective-permute-start.32 = (bf16[128,128]{1,0:T(8,128)(2,1)S(1)}, bf16[128,128]{1,0:T(8,128)(2,1)S(1)}, u32[]{:S(2)}, u32[]{:S(2)}) collective-permute-start(bf16[128,128]{1,0:T(8,128)(2,1)S(1)} %get-tuple-element.77), channel_id=1, source_target_pairs={{0,6},{2,0},{4,2},{6,4},{1,70},{3,64},{5,66},{7,68},{8,134},{10,12... | collective-permute-start | bytes 98312 | tf_op jit(solution)/shard_map/ppermute | solution.py:220
  103.9 3.5 %collective-permute-done.31.refs_2_ = bf16[128,128]{1,0:T(8,128)(2,1)S(1)} collective-permute-done((bf16[128,128]{1,0:T(8,128)(2,1)S(1)}, bf16[128,128]{1,0:T(8,128)(2,1)S(1)}, u32[]{:S(2)}, u32[]{:S(2)}) %collective-permute-start.31) | collective-permute-done | bytes 32800 | tf_op jit(solution)/shard_map/ppermute | solution.py:220
  107.4 1.2 %shard_map.101 = (f32[64,512]{1,0:T(8,128)}, bf16[64,512]{1,0:T(8,128)(2,1)}) custom-call(s32[4]{0:T(128)S(1)} %pad_add_fusion.at_ref, bf16[128,128]{1,0:T(8,128)(2,1)S(1)} %collective-permute-done.29.refs_0_, bf16[128,128]{1,0:T(8,128)(2,1)S(1)} %collective-permute-done.30.refs_1_, bf16[128,128]{1,0:T(8,128)(2,1)S(1)} %collective-permute-done.31.refs_2_, ...), custom_call_target="tpu_custom_call" | custom-call | bytes 327696 | tf_op jit(solution)/shard_map/pallas_call | solution.py:23
  (47 shorter events, 1.9 us)
Async XLA Ops:
  0.6 12.9 %copy-start.2 = (bf16[64,512]{1,0:T(8,128)(2,1)S(1)}, bf16[64,512]{1,0:T(8,128)(2,1)}, u32[]{:S(2)}) copy-start(bf16[64,512]{1,0:T(8,128)(2,1)} %q_ref.2) | copy-start | bytes 196612
  0.6 12.9 %copy-start = (bf16[64,512]{1,0:T(8,128)(2,1)S(1)}, bf16[64,512]{1,0:T(8,128)(2,1)}, u32[]{:S(2)}) copy-start(bf16[64,512]{1,0:T(8,128)(2,1)} %k_ref.2) | copy-start | bytes 196612
  0.7 12.9 %copy-start.1 = (bf16[64,512]{1,0:T(8,128)(2,1)S(1)}, bf16[64,512]{1,0:T(8,128)(2,1)}, u32[]{:S(2)}) copy-start(bf16[64,512]{1,0:T(8,128)(2,1)} %v_ref.2) | copy-start | bytes 196612
  3.2 40.7 %all-to-all-start = ((bf16[16,208,128]{2,1,0:T(8,128)(2,1)}), bf16[16,208,128]{2,1,0:T(8,128)(2,1)S(1)}, u32[]{:S(2)}, u32[]{:S(2)}) async-start(bf16[16,208,128]{2,1,0:T(8,128)(2,1)} %shard_map.90), calls=%async_computation | async-start | bytes 1703936 | tf_op jit(solution)/shard_map/all_to_all | solution.py:250
  14.3 14.6 %collective-permute-start = (bf16[192,128]{1,0:T(8,128)(2,1)S(1)}, bf16[192,128]{1,0:T(8,128)(2,1)S(1)}, u32[]{:S(2)}, u32[]{:S(2)}) collective-permute-start(bf16[192,128]{1,0:T(8,128)(2,1)S(1)} %get-tuple-element.40), channel_id=1, source_target_pairs={{0,0},{2,2},{4,4},{6,6},{1,64},{3,66},{5,68},{7,70},{8,128},{10,13... | collective-permute-start | bytes 147464 | tf_op jit(solution)/shard_map/ppermute | solution.py:220
  18.9 22.4 %collective-permute-start.1 = (bf16[192,128]{1,0:T(8,128)(2,1)S(1)}, bf16[192,128]{1,0:T(8,128)(2,1)S(1)}, u32[]{:S(2)}, u32[]{:S(2)}) collective-permute-start(bf16[192,128]{1,0:T(8,128)(2,1)S(1)} %get-tuple-element.41), channel_id=1, source_target_pairs={{0,2},{2,4},{4,6},{6,0},{1,66},{3,68},{5,70},{7,64},{8,130},{10,13... | collective-permute-start | bytes 147464 | tf_op jit(solution)/shard_map/ppermute | solution.py:220
  20.8 22.5 %collective-permute-start.2 = (bf16[192,128]{1,0:T(8,128)(2,1)S(1)}, bf16[192,128]{1,0:T(8,128)(2,1)S(1)}, u32[]{:S(2)}, u32[]{:S(2)}) collective-permute-start(bf16[192,128]{1,0:T(8,128)(2,1)S(1)} %get-tuple-element.42), channel_id=1, source_target_pairs={{0,4},{2,6},{4,0},{6,2},{1,68},{3,70},{5,64},{7,66},{8,132},{10,13... | collective-permute-start | bytes 147464 | tf_op jit(solution)/shard_map/ppermute | solution.py:220
  25.9 17.4 %collective-permute-start.3 = (bf16[192,128]{1,0:T(8,128)(2,1)S(1)}, bf16[192,128]{1,0:T(8,128)(2,1)S(1)}, u32[]{:S(2)}, u32[]{:S(2)}) collective-permute-start(bf16[192,128]{1,0:T(8,128)(2,1)S(1)} %get-tuple-element.43), channel_id=1, source_target_pairs={{0,6},{2,0},{4,2},{6,4},{1,70},{3,64},{5,66},{7,68},{8,134},{10,12... | collective-permute-start | bytes 147464 | tf_op jit(solution)/shard_map/ppermute | solution.py:220
  44.1 9.4 %collective-permute-start.12 = (bf16[1024,128]{1,0:T(8,128)(2,1)S(1)}, bf16[1024,128]{1,0:T(8,128)(2,1)S(1)}, u32[]{:S(2)}, u32[]{:S(2)}) collective-permute-start(bf16[1024,128]{1,0:T(8,128)(2,1)S(1)} %get-tuple-element.50.k_ref), channel_id=1, source_target_pairs={{0,16},{16,32},{32,48},{48,0},{1,17},{17,33},{33,49},{49,1},{2,18}... | collective-permute-start | bytes 786440 | tf_op jit(solution)/shard_map/ppermute | solution.py:224
  45.7 9.3 %collective-permute-start.13 = (bf16[1024,128]{1,0:T(8,128)(2,1)S(1)}, bf16[1024,128]{1,0:T(8,128)(2,1)S(1)}, u32[]{:S(2)}, u32[]{:S(2)}) collective-permute-start(bf16[1024,128]{1,0:T(8,128)(2,1)S(1)} %get-tuple-element.50.k_ref), channel_id=1, source_target_pairs={{0,48},{16,0},{32,16},{48,32},{1,49},{17,1},{33,17},{49,33},{2,50}... | collective-permute-start | bytes 786440 | tf_op jit(solution)/shard_map/ppermute | solution.py:224
  48.6 10.8 %collective-permute-start.14 = (bf16[1024,128]{1,0:T(8,128)(2,1)S(1)}, bf16[1024,128]{1,0:T(8,128)(2,1)S(1)}, u32[]{:S(2)}, u32[]{:S(2)}) collective-permute-start(bf16[1024,128]{1,0:T(8,128)(2,1)S(1)} %get-tuple-element.61.refs_9_), channel_id=1, source_target_pairs={{0,16},{16,32},{32,48},{48,0},{1,17},{17,33},{33,49},{49,1},{2,18}... | collective-permute-start | bytes 786440 | tf_op jit(solution)/shard_map/ppermute | solution.py:224
  49.0 11.9 %collective-permute-start.15 = (bf16[1024,128]{1,0:T(8,128)(2,1)S(1)}, bf16[1024,128]{1,0:T(8,128)(2,1)S(1)}, u32[]{:S(2)}, u32[]{:S(2)}) collective-permute-start(bf16[1024,128]{1,0:T(8,128)(2,1)S(1)} %get-tuple-element.61.refs_9_), channel_id=1, source_target_pairs={{0,48},{16,0},{32,16},{48,32},{1,49},{17,1},{33,17},{49,33},{2,50}... | collective-permute-start | bytes 786440 | tf_op jit(solution)/shard_map/ppermute | solution.py:224
  51.9 5.3 %collective-permute-start.4 = (bf16[512,128]{1,0:T(8,128)(2,1)S(1)}, bf16[512,128]{1,0:T(8,128)(2,1)S(1)}, u32[]{:S(2)}, u32[]{:S(2)}) collective-permute-start(bf16[512,128]{1,0:T(8,128)(2,1)S(1)} %get-tuple-element.45.kv_ref.bv_ref), channel_id=1, source_target_pairs={{0,128},{128,0},{1,129},{129,1},{2,130},{130,2},{3,131},{131,3},{4... | collective-permute-start | bytes 393224 | tf_op jit(solution)/shard_map/ppermute | solution.py:228
  53.6 15.0 %collective-permute-start.16 = (bf16[512,128]{1,0:T(8,128)(2,1)S(1)}, bf16[512,128]{1,0:T(8,128)(2,1)S(1)}, u32[]{:S(2)}, u32[]{:S(2)}) collective-permute-start(bf16[512,128]{1,0:T(8,128)(2,1)S(1)} %slice.16), channel_id=1, source_target_pairs={{0,16},{16,32},{32,48},{48,0},{1,17},{17,33},{33,49},{49,1},{2,18}... | collective-permute-start | bytes 393224 | tf_op jit(solution)/shard_map/ppermute | solution.py:224
  55.0 13.7 %collective-permute-start.17 = (bf16[512,128]{1,0:T(8,128)(2,1)S(1)}, bf16[512,128]{1,0:T(8,128)(2,1)S(1)}, u32[]{:S(2)}, u32[]{:S(2)}) collective-permute-start(bf16[512,128]{1,0:T(8,128)(2,1)S(1)} %slice.17), channel_id=1, source_target_pairs={{0,48},{16,0},{32,16},{48,32},{1,49},{17,1},{33,17},{49,33},{2,50}... | collective-permute-start | bytes 393224 | tf_op jit(solution)/shard_map/ppermute | solution.py:224
  57.2 16.7 %collective-permute-start.6 = (bf16[512,128]{1,0:T(8,128)(2,1)S(1)}, bf16[512,128]{1,0:T(8,128)(2,1)S(1)}, u32[]{:S(2)}, u32[]{:S(2)}) collective-permute-start(bf16[512,128]{1,0:T(8,128)(2,1)S(1)} %shard_map.88.refs_0_), channel_id=1, source_target_pairs={{0,32},{16,48},{32,0},{48,16},{1,33},{17,49},{33,1},{49,17},{2,34}... | collective-permute-start | bytes 393224 | tf_op jit(solution)/shard_map/ppermute | solution.py:224
  59.5 12.4 %collective-permute-start.18 = (bf16[512,128]{1,0:T(8,128)(2,1)S(1)}, bf16[512,128]{1,0:T(8,128)(2,1)S(1)}, u32[]{:S(2)}, u32[]{:S(2)}) collective-permute-start(bf16[512,128]{1,0:T(8,128)(2,1)S(1)} %slice.18), channel_id=1, source_target_pairs={{0,16},{16,32},{32,48},{48,0},{1,17},{17,33},{33,49},{49,1},{2,18}... | collective-permute-start | bytes 393224 | tf_op jit(solution)/shard_map/ppermute | solution.py:224
  60.9 10.9 %collective-permute-start.19 = (bf16[512,128]{1,0:T(8,128)(2,1)S(1)}, bf16[512,128]{1,0:T(8,128)(2,1)S(1)}, u32[]{:S(2)}, u32[]{:S(2)}) collective-permute-start(bf16[512,128]{1,0:T(8,128)(2,1)S(1)} %slice.19), channel_id=1, source_target_pairs={{0,48},{16,0},{32,16},{48,32},{1,49},{17,1},{33,17},{49,33},{2,50}... | collective-permute-start | bytes 393224 | tf_op jit(solution)/shard_map/ppermute | solution.py:224
  68.6 5.4 %collective-permute-start.7 = (bf16[512,128]{1,0:T(8,128)(2,1)S(1)}, bf16[512,128]{1,0:T(8,128)(2,1)S(1)}, u32[]{:S(2)}, u32[]{:S(2)}) collective-permute-start(bf16[512,128]{1,0:T(8,128)(2,1)S(1)} %shard_map.88.refs_0_), channel_id=1, source_target_pairs={{0,48},{16,0},{32,16},{48,32},{1,49},{17,1},{33,17},{49,33},{2,50}... | collective-permute-start | bytes 393224 | tf_op jit(solution)/shard_map/ppermute | solution.py:224
  68.7 6.2 %collective-permute-start.5 = (bf16[512,128]{1,0:T(8,128)(2,1)S(1)}, bf16[512,128]{1,0:T(8,128)(2,1)S(1)}, u32[]{:S(2)}, u32[]{:S(2)}) collective-permute-start(bf16[512,128]{1,0:T(8,128)(2,1)S(1)} %shard_map.88.refs_0_), channel_id=1, source_target_pairs={{0,16},{16,32},{32,48},{48,0},{1,17},{17,33},{33,49},{49,1},{2,18}... | collective-permute-start | bytes 393224 | tf_op jit(solution)/shard_map/ppermute | solution.py:224
  73.3 1.6 %collective-permute-start.20 = (bf16[512,128]{1,0:T(8,128)(2,1)S(1)}, bf16[512,128]{1,0:T(8,128)(2,1)S(1)}, u32[]{:S(2)}, u32[]{:S(2)}) collective-permute-start(bf16[512,128]{1,0:T(8,128)(2,1)S(1)} %get-tuple-element.69), channel_id=1, source_target_pairs={{0,64},{64,0},{1,65},{65,1},{2,66},{66,2},{3,67},{67,3},{4,68},{68... | collective-permute-start | bytes 393224 | tf_op jit(solution)/shard_map/ppermute | solution.py:228
  73.4 2.3 %collective-permute-start.8 = (bf16[512,128]{1,0:T(8,128)(2,1)S(1)}, bf16[512,128]{1,0:T(8,128)(2,1)S(1)}, u32[]{:S(2)}, u32[]{:S(2)}) collective-permute-start(bf16[512,128]{1,0:T(8,128)(2,1)S(1)} %shard_map.88.refs_0_), channel_id=1, source_target_pairs={{0,64},{64,0},{1,65},{65,1},{2,66},{66,2},{3,67},{67,3},{4,68},{68... | collective-permute-start | bytes 393224 | tf_op jit(solution)/shard_map/ppermute | solution.py:228
  73.9 1.8 %collective-permute-start.10 = (bf16[512,128]{1,0:T(8,128)(2,1)S(1)}, bf16[512,128]{1,0:T(8,128)(2,1)S(1)}, u32[]{:S(2)}, u32[]{:S(2)}) collective-permute-start(bf16[512,128]{1,0:T(8,128)(2,1)S(1)} %collective-permute-done.6.refs_2_), channel_id=1, source_target_pairs={{0,64},{64,0},{1,65},{65,1},{2,66},{66,2},{3,67},{67,3},{4,68},{68... | collective-permute-start | bytes 393224 | tf_op jit(solution)/shard_map/ppermute | solution.py:228
  74.0 1.7 %collective-permute-start.11 = (bf16[512,128]{1,0:T(8,128)(2,1)S(1)}, bf16[512,128]{1,0:T(8,128)(2,1)S(1)}, u32[]{:S(2)}, u32[]{:S(2)}) collective-permute-start(bf16[512,128]{1,0:T(8,128)(2,1)S(1)} %collective-permute-done.7.refs_3_), channel_id=1, source_target_pairs={{0,64},{64,0},{1,65},{65,1},{2,66},{66,2},{3,67},{67,3},{4,68},{68... | collective-permute-start | bytes 393224 | tf_op jit(solution)/shard_map/ppermute | solution.py:228
  74.9 1.3 %collective-permute-start.9 = (bf16[512,128]{1,0:T(8,128)(2,1)S(1)}, bf16[512,128]{1,0:T(8,128)(2,1)S(1)}, u32[]{:S(2)}, u32[]{:S(2)}) collective-permute-start(bf16[512,128]{1,0:T(8,128)(2,1)S(1)} %collective-permute-done.5.refs_1_), channel_id=1, source_target_pairs={{0,64},{64,0},{1,65},{65,1},{2,66},{66,2},{3,67},{67,3},{4,68},{68... | collective-permute-start | bytes 393224 | tf_op jit(solution)/shard_map/ppermute | solution.py:228
  75.0 6.0 %collective-permute-start.21 = (bf16[512,128]{1,0:T(8,128)(2,1)S(1)}, bf16[512,128]{1,0:T(8,128)(2,1)S(1)}, u32[]{:S(2)}, u32[]{:S(2)}) collective-permute-start(bf16[512,128]{1,0:T(8,128)(2,1)S(1)} %get-tuple-element.71), channel_id=1, source_target_pairs={{0,128},{128,0},{1,129},{129,1},{2,130},{130,2},{3,131},{131,3},{4... | collective-permute-start | bytes 393224 | tf_op jit(solution)/shard_map/ppermute | solution.py:228
  81.0 9.4 %collective-permute-start.22 = (bf16[512,128]{1,0:T(8,128)(2,1)S(1)}, bf16[512,128]{1,0:T(8,128)(2,1)S(1)}, u32[]{:S(2)}, u32[]{:S(2)}) collective-permute-start(bf16[512,128]{1,0:T(8,128)(2,1)S(1)} %get-tuple-element.73.refs_0_), channel_id=1, source_target_pairs={{0,16},{16,32},{32,48},{48,0},{1,17},{17,33},{33,49},{49,1},{2,18}... | collective-permute-start | bytes 393224 | tf_op jit(solution)/shard_map/ppermute | solution.py:224
  82.0 8.4 %collective-permute-start.23 = (bf16[512,128]{1,0:T(8,128)(2,1)S(1)}, bf16[512,128]{1,0:T(8,128)(2,1)S(1)}, u32[]{:S(2)}, u32[]{:S(2)}) collective-permute-start(bf16[512,128]{1,0:T(8,128)(2,1)S(1)} %get-tuple-element.73.refs_0_), channel_id=1, source_target_pairs={{0,32},{16,48},{32,0},{48,16},{1,33},{17,49},{33,1},{49,17},{2,34}... | collective-permute-start | bytes 393224 | tf_op jit(solution)/shard_map/ppermute | solution.py:224
  83.6 7.5 %collective-permute-start.24 = (bf16[512,128]{1,0:T(8,128)(2,1)S(1)}, bf16[512,128]{1,0:T(8,128)(2,1)S(1)}, u32[]{:S(2)}, u32[]{:S(2)}) collective-permute-start(bf16[512,128]{1,0:T(8,128)(2,1)S(1)} %get-tuple-element.73.refs_0_), channel_id=1, source_target_pairs={{0,48},{16,0},{32,16},{48,32},{1,49},{17,1},{33,17},{49,33},{2,50}... | collective-permute-start | bytes 393224 | tf_op jit(solution)/shard_map/ppermute | solution.py:224
  84.9 6.1 %collective-permute-start.25 = (bf16[512,128]{1,0:T(8,128)(2,1)S(1)}, bf16[512,128]{1,0:T(8,128)(2,1)S(1)}, u32[]{:S(2)}, u32[]{:S(2)}) collective-permute-start(bf16[512,128]{1,0:T(8,128)(2,1)S(1)} %get-tuple-element.73.refs_0_), channel_id=1, source_target_pairs={{0,64},{64,0},{1,65},{65,1},{2,66},{66,2},{3,67},{67,3},{4,68},{68... | collective-permute-start | bytes 393224 | tf_op jit(solution)/shard_map/ppermute | solution.py:228
  90.5 1.3 %collective-permute-start.26 = (bf16[512,128]{1,0:T(8,128)(2,1)S(1)}, bf16[512,128]{1,0:T(8,128)(2,1)S(1)}, u32[]{:S(2)}, u32[]{:S(2)}) collective-permute-start(bf16[512,128]{1,0:T(8,128)(2,1)S(1)} %collective-permute-done.22.refs_1_), channel_id=1, source_target_pairs={{0,64},{64,0},{1,65},{65,1},{2,66},{66,2},{3,67},{67,3},{4,68},{68... | collective-permute-start | bytes 393224 | tf_op jit(solution)/shard_map/ppermute | solution.py:228
  90.5 1.5 %collective-permute-start.27 = (bf16[512,128]{1,0:T(8,128)(2,1)S(1)}, bf16[512,128]{1,0:T(8,128)(2,1)S(1)}, u32[]{:S(2)}, u32[]{:S(2)}) collective-permute-start(bf16[512,128]{1,0:T(8,128)(2,1)S(1)} %collective-permute-done.23.refs_2_), channel_id=1, source_target_pairs={{0,64},{64,0},{1,65},{65,1},{2,66},{66,2},{3,67},{67,3},{4,68},{68... | collective-permute-start | bytes 393224 | tf_op jit(solution)/shard_map/ppermute | solution.py:228
  91.1 1.3 %collective-permute-start.28 = (bf16[512,128]{1,0:T(8,128)(2,1)S(1)}, bf16[512,128]{1,0:T(8,128)(2,1)S(1)}, u32[]{:S(2)}, u32[]{:S(2)}) collective-permute-start(bf16[512,128]{1,0:T(8,128)(2,1)S(1)} %collective-permute-done.24.refs_3_), channel_id=1, source_target_pairs={{0,64},{64,0},{1,65},{65,1},{2,66},{66,2},{3,67},{67,3},{4,68},{68... | collective-permute-start | bytes 393224 | tf_op jit(solution)/shard_map/ppermute | solution.py:228
  93.7 10.0 %collective-permute-start.29 = (bf16[128,128]{1,0:T(8,128)(2,1)S(1)}, bf16[128,128]{1,0:T(8,128)(2,1)S(1)}, u32[]{:S(2)}, u32[]{:S(2)}) collective-permute-start(bf16[128,128]{1,0:T(8,128)(2,1)S(1)} %get-tuple-element.74), channel_id=1, source_target_pairs={{0,0},{2,2},{4,4},{6,6},{1,64},{3,66},{5,68},{7,70},{8,128},{10,13... | collective-permute-start | bytes 98312 | tf_op jit(solution)/shard_map/ppermute | solution.py:220
  96.6 7.3 %collective-permute-start.30 = (bf16[128,128]{1,0:T(8,128)(2,1)S(1)}, bf16[128,128]{1,0:T(8,128)(2,1)S(1)}, u32[]{:S(2)}, u32[]{:S(2)}) collective-permute-start(bf16[128,128]{1,0:T(8,128)(2,1)S(1)} %get-tuple-element.75), channel_id=1, source_target_pairs={{0,2},{2,4},{4,6},{6,0},{1,66},{3,68},{5,70},{7,64},{8,130},{10,13... | collective-permute-start | bytes 98312 | tf_op jit(solution)/shard_map/ppermute | solution.py:220
  98.1 9.2 %collective-permute-start.31 = (bf16[128,128]{1,0:T(8,128)(2,1)S(1)}, bf16[128,128]{1,0:T(8,128)(2,1)S(1)}, u32[]{:S(2)}, u32[]{:S(2)}) collective-permute-start(bf16[128,128]{1,0:T(8,128)(2,1)S(1)} %get-tuple-element.76), channel_id=1, source_target_pairs={{0,4},{2,6},{4,0},{6,2},{1,68},{3,70},{5,64},{7,66},{8,132},{10,13... | collective-permute-start | bytes 98312 | tf_op jit(solution)/shard_map/ppermute | solution.py:220
  100.6 6.8 %collective-permute-start.32 = (bf16[128,128]{1,0:T(8,128)(2,1)S(1)}, bf16[128,128]{1,0:T(8,128)(2,1)S(1)}, u32[]{:S(2)}, u32[]{:S(2)}) collective-permute-start(bf16[128,128]{1,0:T(8,128)(2,1)S(1)} %get-tuple-element.77), channel_id=1, source_target_pairs={{0,6},{2,0},{4,2},{6,4},{1,70},{3,64},{5,66},{7,68},{8,134},{10,12... | collective-permute-start | bytes 98312 | tf_op jit(solution)/shard_map/ppermute | solution.py:220

commit v4 on v3

--- a/solution.py
+++ b/solution.py
@@ -144,7 +144,7 @@
 
 
 def finish_kernel(at_ref, factor_ref, *refs):
-    ms, ls, acc_ref, p_ref, va_ref, vb_ref, keep_ref, give_ref = refs[0:2], refs[2:4], *refs[4:]
+    ms, ls, acc_ref, p_ref, va_ref, vb_ref, keep_ref, share_ref, give_ref = refs[0:2], refs[2:4], *refs[4:]
     b = at_ref[0] * 2 + at_ref[1]
     for chunk, out, place in ((1, give_ref, 0), (3, give_ref, 1), (0, keep_ref, 0), (2, keep_ref, 1)):
         rows = pl.ds(pl.multiple_of((b ^ chunk) * 256, 256), 256)
@@ -153,25 +153,22 @@
         acc = acc_ref[rows] * weights[0] + far * weights[1]
         acc = acc / total * factor_ref[rows]
         out[place * 256 : place * 256 + 256] = acc.astype(out.dtype)
-
-
-def pair_kernel(keep_ref, got_ref, pair_ref, send_ref):
-    pair = keep_ref[...] + got_ref[...].astype(F32)
-    pair_ref[...] = pair
-    send_ref[...] = pair.astype(BF)
-
-
-def join_kernel(pair_ref, got_ref, bv_ref, more_ref, after_ref, joined_ref, values_ref):
-    del after_ref
+        if out is keep_ref:
+            share_ref[place * 256 : place * 256 + 256] = acc.astype(BF)
+
+
+def join_kernel(keep_ref, core_ref, y_ref, both_ref, bv_ref, more_ref, joined_ref, values_ref):
     for n, base in enumerate((bv_ref, more_ref)):
-        rows = slice(n * 256, n * 256 + 256)
-        joined = pair_ref[rows] + got_ref[256 - n * 256 : 512 - n * 256].astype(F32)
+        rows, crossed = slice(n * 256, n * 256 + 256), slice(256 - n * 256, 512 - n * 256)
+        joined = keep_ref[rows] + core_ref[rows].astype(F32)
+        joined = joined + (y_ref[crossed].astype(F32) + both_ref[crossed].astype(F32))
         if n == 0:
             joined_ref[...] = joined.astype(BF)
         values_ref[rows] = (base[256:512].astype(F32) + joined).astype(BF)
 
 
-def base_pair_kernel(kv_ref, more_ref, out_ref):
+def base_pair_kernel(kv_ref, more_ref, after_ref, out_ref):
+    del after_ref
     out_ref[0:256] = kv_ref[0:256]
     out_ref[256:512] = more_ref[0:256]
 
@@ -228,10 +225,14 @@
     return lax.ppermute(values, axis, [(0, 1), (1, 0)])
 
 
-def gather_pair(pair):
+def gather_x(pair):
     mine = [pair] + [None] * 3
     for step in (1, 3, 2):
         mine[step] = along("x", pair, step)
+    return mine
+
+
+def gather_core(mine):
     return mine + [other(v, "co") for v in mine]
 
 
@@ -257,7 +258,8 @@
         out_specs=[ANY] * 4,
         scratch=[pltpu.SemaphoreType.DMA((12,))],
     )
-    parts = [swap(part, step) for step, part in enumerate(parts)]
+    swapped = {step: swap(parts[step], step) for step in (2, 1, 3, 0)}
+    parts = [swapped[step] for step in range(4)]
     base_kv, base_quer = call(
         base_unpack_kernel, [sds((512, DIM)), sds((256, DIM))], [at, *parts], specs=[SM] + [VM] * 4
     )
@@ -284,19 +286,6 @@
     far_v = [along("x", after_v[:512], 1), along("x", before_v[512:], 3)]
 
     more_kv = other(base_kv, "yl")
-    (base_pair,) = call(
-        base_pair_kernel,
-        [sds((512, DIM))],
-        [base_kv, more_kv],
-    )
-    base_keys = gather_pair(base_pair)
-    base_p, base_l = call(
-        base_score_kernel,
-        [sds((8, 256, 512)), sds((256, 1), F32)],
-        [base_quer, *base_keys],
-        vmem=24,
-        flops=2 * 256 * 4096 * 128,
-    )
 
     scored = [own_score] + [
         call(score_kernel, outs, [quer, k], vmem=24, flops=2 * 1024 * 1024 * 128) for k in (after_k, before_k)
@@ -310,30 +299,45 @@
         flops=3 * 2 * 1024 * 1024 * 128,
     )
     far_p, far_m, far_l = call(score_kernel, outs, [quer, *far_k], vmem=24, flops=2 * 1024 * 1024 * 128)
-    keep, give = call(
+    keep, share, give = call(
         finish_kernel,
-        [sds((512, DIM), F32), sds((512, DIM))],
+        [sds((512, DIM), F32), sds((512, DIM)), sds((512, DIM))],
         [at, factor, m, far_m, l, far_l, acc, far_p, *far_v],
         specs=[SM] + [VM] * 9,
         vmem=24,
         flops=2 * 1024 * 1024 * 128,
     )
 
-    pair, send = call(pair_kernel, [sds((512, DIM), F32), sds((512, DIM))], [keep, other(give, "co")])
+    got_core = other(give, "co")
+    got_both = lax.ppermute(give, ("yl", "co"), [(j, j ^ 3) for j in range(4)])
+    got_y = other(share, "yl")
+    (base_pair,) = call(
+        base_pair_kernel, [sds((512, DIM))], [base_kv, more_kv, give], specs=[VM, VM, ANYWHERE]
+    )
+    base_mine = gather_x(base_pair)
     joined, base_values = call(
-        join_kernel, [sds((256, DIM)), sds((512, DIM))], [pair, other(send, "yl"), base_kv, more_kv, base_l], specs=[VM] * 4 + [ANYWHERE]
-    )
-
+        join_kernel,
+        [sds((256, DIM)), sds((512, DIM))],
+        [keep, got_core, got_y, got_both, base_kv, more_kv],
+    )
+
+    base_p, base_l = call(
+        base_score_kernel,
+        [sds((8, 256, 512)), sds((256, 1), F32)],
+        [base_quer, *gather_core(base_mine)],
+        vmem=24,
+        flops=2 * 256 * 4096 * 128,
+    )
     outs = call(
         base_value_kernel,
         [sds((128, DIM))] * 4,
-        [at, base_p, base_l, joined, *gather_pair(base_values)],
+        [at, base_p, base_l, joined, *gather_core(gather_x(base_values))],
         specs=[SM] + [VM] * 11,
         flops=2 * 256 * 4096 * 128,
         scratch=[pltpu.VMEM((256, DIM), BF)],
     )
     result = [None] * 4
-    for step in (0, 1, 3, 2):
+    for step in (2, 1, 3, 0):
         result[step] = swap(outs[step], step)
     return call(home_kernel, [sds((64, 512), F32), sds((64, 512))], [at, *result], specs=[SM] + [VM] * 4)
 

time: 109 us -> 108 us (level)
  starting transfers between devices: 59.9 us -> 58.7 us
    ppermute x11, waiting for transfers between devices: 5.18 us -> 0.18 us  [other(): return lax.ppermute(values, axis, [(0, 1), (1, 0)])]
    ppermute x14, starting transfers between devices: 22.6 us -> 18.6 us  [along(): return lax.ppermute(values, axis, [(j, (j + step) % 4) for j in range(4)])]
    ppermute x14, waiting for transfers between devices: 8.26 us -> 11.9 us  [along(): return lax.ppermute(values, axis, [(j, (j + step) % 4) for j in range(4)])]
    ppermute x0 -> x1, waiting for transfers between devices: none -> 1.71 us  [shards(): got_both = lax.ppermute(give, ('yl', 'co'), [(j, j ^ 3) for j in range(4)])]
    ppermute x0 -> x1, starting transfers between devices: none -> 1.17 us  [shards(): got_both = lax.ppermute(give, ('yl', 'co'), [(j, j ^ 3) for j in range(4)])]
    pallas_call x16 -> x15, Pallas kernels: 16.1 us -> 16.1 us  [call(): pl.pallas_call(body, out_shape=outs, in_specs=specs or [VM] * len(operand...]
  transfers between devices with their start and end apart: 34 -> 35, of which waited for: 14 -> 10; matrix products, arithmetic and copies ran while one was open for 0% -> 0% of each run, Pallas kernels for 10% -> 10%
where the time goes in v4:
time: 108 us; the launch traced here: 107 us
  starting transfers between devices  58.7 us (54%)
  waiting for transfers between devices  31.5 us (29%)
  Pallas kernels  16.1 us (15%)
    ppermute x8, starting transfers between devices, swap(): return lax.ppermute(values, ('yl', 'co', 'yh', 'zt', 'zp'), perm)  25.4 us
    ppermute x14, starting transfers between devices, along(): return lax.ppermute(values, axis, [(j, (j + step) % 4) for j in range(4)])  18.6 us
    ppermute x8, waiting for transfers between devices, swap(): return lax.ppermute(values, ('yl', 'co', 'yh', 'zt', 'zp'), perm)  17.7 us
    pallas_call x15, Pallas kernels, call(): pl.pallas_call(body, out_shape=outs, in_specs=specs or [VM] * len(operand...  16.1 us
    ppermute x14, waiting for transfers between devices, along(): return lax.ppermute(values, axis, [(j, (j + step) % 4) for j in range(4)])  11.9 us
    all_to_all x1, starting transfers between devices, shards(): sent = lax.all_to_all(packed, ('yh', 'zt', 'zp'), 0, 0, tiled=True)  10.3 us
    ppermute x11, starting transfers between devices, other(): return lax.ppermute(values, axis, [(0, 1), (1, 0)])  3.32 us
  transfers between devices with their start and end apart: 35, of which 10 were waited for; matrix products, arithmetic and copies ran while one was open for 0% of the time, Pallas kernels for 10%

profile of v4, /device:TPU:8, one launch (start us, length us, event | category | flops | bytes accessed | tf_op | source)
XLA Modules:
  0.0 107.3 jit_solution(8986375179947820705)
XLA Ops:
  0.7 2.5 %shard_map.88 = bf16[16,208,128]{2,1,0:T(8,128)(2,1)} custom-call(bf16[1,64,2048]{2,1,0:T(8,128)(2,1)} %k_ref.3, bf16[1,64,2048]{2,1,0:T(8,128)(2,1)} %v_ref.3, bf16[1,64,2048]{2,1,0:T(8,128)(2,1)} %q_ref.3, s32[1,64]{1,0:T(1,128)} %code_ref.1), custom_call_target="tpu_custom_call" | custom-call | bytes 1638656 | tf_op jit(solution)/shard_map/pallas_call | solution.py:23
  3.2 10.3 %all-to-all-start = ((bf16[16,208,128]{2,1,0:T(8,128)(2,1)}), bf16[16,208,128]{2,1,0:T(8,128)(2,1)S(1)}, u32[]{:S(2)}, u32[]{:S(2)}) async-start(bf16[16,208,128]{2,1,0:T(8,128)(2,1)} %shard_map.88), calls=%async_computation | async-start | bytes 1703936 | tf_op jit(solution)/shard_map/all_to_all | solution.py:251
  13.6 0.7 shard_map.86
  14.3 4.6 %collective-permute-start = (bf16[192,128]{1,0:T(8,128)(2,1)S(1)}, bf16[192,128]{1,0:T(8,128)(2,1)S(1)}, u32[]{:S(2)}, u32[]{:S(2)}) collective-permute-start(bf16[192,128]{1,0:T(8,128)(2,1)S(1)} %get-tuple-element.39), channel_id=1, source_target_pairs={{0,0},{2,2},{4,4},{6,6},{1,64},{3,66},{5,68},{7,70},{8,128},{10,13... | collective-permute-start | bytes 147464 | tf_op jit(solution)/shard_map/ppermute | solution.py:217
  18.9 1.9 %collective-permute-start.1 = (bf16[192,128]{1,0:T(8,128)(2,1)S(1)}, bf16[192,128]{1,0:T(8,128)(2,1)S(1)}, u32[]{:S(2)}, u32[]{:S(2)}) collective-permute-start(bf16[192,128]{1,0:T(8,128)(2,1)S(1)} %get-tuple-element.40), channel_id=1, source_target_pairs={{0,2},{2,4},{4,6},{6,0},{1,66},{3,68},{5,70},{7,64},{8,130},{10,13... | collective-permute-start | bytes 147464 | tf_op jit(solution)/shard_map/ppermute | solution.py:217
  20.8 5.0 %collective-permute-start.2 = (bf16[192,128]{1,0:T(8,128)(2,1)S(1)}, bf16[192,128]{1,0:T(8,128)(2,1)S(1)}, u32[]{:S(2)}, u32[]{:S(2)}) collective-permute-start(bf16[192,128]{1,0:T(8,128)(2,1)S(1)} %get-tuple-element.41), channel_id=1, source_target_pairs={{0,4},{2,6},{4,0},{6,2},{1,68},{3,70},{5,64},{7,66},{8,132},{10,13... | collective-permute-start | bytes 147464 | tf_op jit(solution)/shard_map/ppermute | solution.py:217
  25.9 3.0 %collective-permute-start.3 = (bf16[192,128]{1,0:T(8,128)(2,1)S(1)}, bf16[192,128]{1,0:T(8,128)(2,1)S(1)}, u32[]{:S(2)}, u32[]{:S(2)}) collective-permute-start(bf16[192,128]{1,0:T(8,128)(2,1)S(1)} %get-tuple-element.42), channel_id=1, source_target_pairs={{0,6},{2,0},{4,2},{6,4},{1,70},{3,64},{5,66},{7,68},{8,134},{10,12... | collective-permute-start | bytes 147464 | tf_op jit(solution)/shard_map/ppermute | solution.py:217
  28.9 12.4 %collective-permute-done.1.refs_1_ = bf16[192,128]{1,0:T(8,128)(2,1)S(1)} collective-permute-done((bf16[192,128]{1,0:T(8,128)(2,1)S(1)}, bf16[192,128]{1,0:T(8,128)(2,1)S(1)}, u32[]{:S(2)}, u32[]{:S(2)}) %collective-permute-start.1) | collective-permute-done | bytes 49184 | tf_op jit(solution)/shard_map/ppermute | solution.py:217
  41.3 2.0 %collective-permute-done.2.refs_2_ = bf16[192,128]{1,0:T(8,128)(2,1)S(1)} collective-permute-done((bf16[192,128]{1,0:T(8,128)(2,1)S(1)}, bf16[192,128]{1,0:T(8,128)(2,1)S(1)}, u32[]{:S(2)}, u32[]{:S(2)}) %collective-permute-start.2) | collective-permute-done | bytes 49184 | tf_op jit(solution)/shard_map/ppermute | solution.py:217
  43.3 0.6 shard_map.87
  43.9 0.2 shard_map.89
  44.1 1.6 %collective-permute-start.5 = (bf16[1024,128]{1,0:T(8,128)(2,1)S(1)}, bf16[1024,128]{1,0:T(8,128)(2,1)S(1)}, u32[]{:S(2)}, u32[]{:S(2)}) collective-permute-start(bf16[1024,128]{1,0:T(8,128)(2,1)S(1)} %get-tuple-element.47.k_ref), channel_id=1, source_target_pairs={{0,16},{16,32},{32,48},{48,0},{1,17},{17,33},{33,49},{49,1},{2,18}... | collective-permute-start | bytes 786440 | tf_op jit(solution)/shard_map/ppermute | solution.py:221
  45.7 1.7 %collective-permute-start.6 = (bf16[1024,128]{1,0:T(8,128)(2,1)S(1)}, bf16[1024,128]{1,0:T(8,128)(2,1)S(1)}, u32[]{:S(2)}, u32[]{:S(2)}) collective-permute-start(bf16[1024,128]{1,0:T(8,128)(2,1)S(1)} %get-tuple-element.47.k_ref), channel_id=1, source_target_pairs={{0,48},{16,0},{32,16},{48,32},{1,49},{17,1},{33,17},{49,33},{2,50}... | collective-permute-start | bytes 786440 | tf_op jit(solution)/shard_map/ppermute | solution.py:221
  47.4 1.2 %shard_map.90 = (bf16[1024,1024]{1,0:T(8,128)(2,1)S(1)}, f32[1024,1]{1,0:T(8,128)S(1)}, f32[1024,1]{1,0:T(8,128)S(1)}, bf16[1024,128]{1,0:T(8,128)(2,1)S(1)}) custom-call(bf16[1024,128]{1,0:T(8,128)(2,1)S(1)} %get-tuple-element.46.q_ref, bf16[1024,128]{1,0:T(8,128)(2,1)S(1)} %get-tuple-element.47.k_ref, ...), custom_call_target="tpu_custom_call", output_to_operand_aliasing={{3}: (2, {})} | custom-call | flops 268435456 | bytes 3153920 | tf_op jit(solution)/shard_map/pallas_call | solution.py:23
  48.6 0.3 collective-permute-start.7
  49.0 3.0 %collective-permute-start.8 = (bf16[1024,128]{1,0:T(8,128)(2,1)S(1)}, bf16[1024,128]{1,0:T(8,128)(2,1)S(1)}, u32[]{:S(2)}, u32[]{:S(2)}) collective-permute-start(bf16[1024,128]{1,0:T(8,128)(2,1)S(1)} %get-tuple-element.58.refs_9_), channel_id=1, source_target_pairs={{0,48},{16,0},{32,16},{48,32},{1,49},{17,1},{33,17},{49,33},{2,50}... | collective-permute-start | bytes 786440 | tf_op jit(solution)/shard_map/ppermute | solution.py:221
  51.9 3.0 %collective-permute-done.6.refs_0_ = bf16[1024,128]{1,0:T(8,128)(2,1)S(1)} collective-permute-done((bf16[1024,128]{1,0:T(8,128)(2,1)S(1)}, bf16[1024,128]{1,0:T(8,128)(2,1)S(1)}, u32[]{:S(2)}, u32[]{:S(2)}) %collective-permute-start.6) | collective-permute-done | bytes 262176 | tf_op jit(solution)/shard_map/ppermute | solution.py:221
  54.9 2.2 %collective-permute-start.10 = (bf16[512,128]{1,0:T(8,128)(2,1)S(1)}, bf16[512,128]{1,0:T(8,128)(2,1)S(1)}, u32[]{:S(2)}, u32[]{:S(2)}) collective-permute-start(bf16[512,128]{1,0:T(8,128)(2,1)S(1)} %slice.17), channel_id=1, source_target_pairs={{0,48},{16,0},{32,16},{48,32},{1,49},{17,1},{33,17},{49,33},{2,50}... | collective-permute-start | bytes 393224 | tf_op jit(solution)/shard_map/ppermute | solution.py:221
  57.3 0.9 collective-permute-start.4
  58.2 0.6 collective-permute-done.7.refs_10_
  58.8 0.7 collective-permute-start.11
  59.5 2.9 %collective-permute-start.12 = (bf16[512,128]{1,0:T(8,128)(2,1)S(1)}, bf16[512,128]{1,0:T(8,128)(2,1)S(1)}, u32[]{:S(2)}, u32[]{:S(2)}) collective-permute-start(bf16[512,128]{1,0:T(8,128)(2,1)S(1)} %slice.19), channel_id=1, source_target_pairs={{0,48},{16,0},{32,16},{48,32},{1,49},{17,1},{33,17},{49,33},{2,50}... | collective-permute-start | bytes 393224 | tf_op jit(solution)/shard_map/ppermute | solution.py:221
  62.4 1.2 %shard_map.91 = (bf16[1024,1024]{1,0:T(8,128)(2,1)S(1)}, f32[1024,1]{1,0:T(8,128)S(1)}, f32[1024,1]{1,0:T(8,128)S(1)}) custom-call(bf16[1024,128]{1,0:T(8,128)(2,1)S(1)} %get-tuple-element.46.q_ref, bf16[1024,128]{1,0:T(8,128)(2,1)S(1)} %collective-permute-done.5.refs_0_), custom_call_target="tpu_custom_call" | custom-call | flops 268435456 | bytes 2629632 | tf_op jit(solution)/shard_map/pallas_call | solution.py:23
  63.6 1.2 %shard_map.92 = (bf16[1024,1024]{1,0:T(8,128)(2,1)S(1)}, f32[1024,1]{1,0:T(8,128)S(1)}, f32[1024,1]{1,0:T(8,128)S(1)}) custom-call(bf16[1024,128]{1,0:T(8,128)(2,1)S(1)} %get-tuple-element.46.q_ref, bf16[1024,128]{1,0:T(8,128)(2,1)S(1)} %collective-permute-done.6.refs_0_), custom_call_target="tpu_custom_call" | custom-call | flops 268435456 | bytes 2629632 | tf_op jit(solution)/shard_map/pallas_call | solution.py:23
  64.8 1.9 %shard_map.93 = (f32[1024,1]{1,0:T(8,128)S(1)}, f32[1024,1]{1,0:T(8,128)S(1)}, f32[1024,128]{1,0:T(8,128)S(1)}) custom-call(f32[1024,1]{1,0:T(8,128)S(1)} %get-tuple-element.49.refs_0_, f32[1024,1]{1,0:T(8,128)S(1)} %get-tuple-element.50.refs_1_, f32[1024,1]{1,0:T(8,128)S(1)} %get-tuple-element.51.refs_2_, f32[1024,1]{1,0:T(8,128)S(1)} %get-tuple-element.52.refs_3_, ...), custom_call_target="tpu_custom_call" | custom-call | flops 805306368 | bytes 7634944 | tf_op jit(solution)/shard_map/pallas_call | solution.py:23
  66.8 1.2 %shard_map.94 = (bf16[1024,1024]{1,0:T(8,128)(2,1)S(1)}, f32[1024,1]{1,0:T(8,128)S(1)}, f32[1024,1]{1,0:T(8,128)S(1)}) custom-call(bf16[1024,128]{1,0:T(8,128)(2,1)S(1)} %get-tuple-element.46.q_ref, bf16[512,128]{1,0:T(8,128)(2,1)S(1)} %collective-permute-done.9.refs_0_, bf16[512,128]{1,0:T(8,128)(2,1)S(1)} %collective-permute-done.10.refs_1_), custom_call_target="tpu_custom_call" | custom-call | flops 268435456 | bytes 2629632 | tf_op jit(solution)/shard_map/pallas_call | solution.py:23
  68.0 1.4 %shard_map.95 = (f32[512,128]{1,0:T(8,128)S(1)}, bf16[512,128]{1,0:T(8,128)(2,1)S(1)}, bf16[512,128]{1,0:T(8,128)(2,1)S(1)}) custom-call(s32[4]{0:T(128)S(1)} %pad_add_fusion.at_ref, f32[1024,1]{1,0:T(8,128)S(1)} %get-tuple-element.45.factor_ref, f32[1024,1]{1,0:T(8,128)S(1)} %get-tuple-element.59.refs_0_, f32[1024,1]{1,0:T(8,128)S(1)} %get-tuple-element.60.refs_1_, ...), custom_call_target="tpu_custom_call" | custom-call | flops 268435456 | bytes 3428368 | tf_op jit(solution)/shard_map/pallas_call | solution.py:23
  69.5 0.7 collective-permute-start.21
  70.2 1.2 %collective-permute-start.22 = (bf16[512,128]{1,0:T(8,128)(2,1)S(1)}, bf16[512,128]{1,0:T(8,128)(2,1)S(1)}, u32[]{:S(2)}, u32[]{:S(2)}) collective-permute-start(bf16[512,128]{1,0:T(8,128)(2,1)S(1)} %get-tuple-element.65.after_ref), channel_id=1, source_target_pairs={{0,192},{64,128},{128,64},{192,0},{1,193},{65,129},{129,65},{193,1... | collective-permute-start | bytes 393224 | tf_op jit(solution)/shard_map/ppermute | solution.py:312
  71.5 3.1 %collective-permute-start.14 = (bf16[512,128]{1,0:T(8,128)(2,1)S(1)}, bf16[512,128]{1,0:T(8,128)(2,1)S(1)}, u32[]{:S(2)}, u32[]{:S(2)}) collective-permute-start(bf16[512,128]{1,0:T(8,128)(2,1)S(1)} %shard_map.96.refs_0_), channel_id=1, source_target_pairs={{0,32},{16,48},{32,0},{48,16},{1,33},{17,49},{33,1},{49,17},{2,34}... | collective-permute-start | bytes 393224 | tf_op jit(solution)/shard_map/ppermute | solution.py:221
  74.6 1.4 %collective-permute-start.15 = (bf16[512,128]{1,0:T(8,128)(2,1)S(1)}, bf16[512,128]{1,0:T(8,128)(2,1)S(1)}, u32[]{:S(2)}, u32[]{:S(2)}) collective-permute-start(bf16[512,128]{1,0:T(8,128)(2,1)S(1)} %shard_map.96.refs_0_), channel_id=1, source_target_pairs={{0,48},{16,0},{32,16},{48,32},{1,49},{17,1},{33,17},{49,33},{2,50}... | collective-permute-start | bytes 393224 | tf_op jit(solution)/shard_map/ppermute | solution.py:221
  76.0 1.7 %collective-permute-done.22.both_ref = bf16[512,128]{1,0:T(8,128)(2,1)S(1)} collective-permute-done((bf16[512,128]{1,0:T(8,128)(2,1)S(1)}, bf16[512,128]{1,0:T(8,128)(2,1)S(1)}, u32[]{:S(2)}, u32[]{:S(2)}) %collective-permute-start.22) | collective-permute-done | bytes 131104 | tf_op jit(solution)/shard_map/ppermute | solution.py:312
  77.9 3.3 %collective-permute-done.13.refs_1_ = bf16[512,128]{1,0:T(8,128)(2,1)S(1)} collective-permute-done((bf16[512,128]{1,0:T(8,128)(2,1)S(1)}, bf16[512,128]{1,0:T(8,128)(2,1)S(1)}, u32[]{:S(2)}, u32[]{:S(2)}) %collective-permute-start.13) | collective-permute-done | bytes 131104 | tf_op jit(solution)/shard_map/ppermute | solution.py:221
  81.2 0.7 collective-permute-start.24
  81.9 0.6 collective-permute-start.25
  82.6 0.5 collective-permute-start.18
  83.1 4.8 %collective-permute-done.23.refs_1_ = bf16[512,128]{1,0:T(8,128)(2,1)S(1)} collective-permute-done((bf16[512,128]{1,0:T(8,128)(2,1)S(1)}, bf16[512,128]{1,0:T(8,128)(2,1)S(1)}, u32[]{:S(2)}, u32[]{:S(2)}) %collective-permute-start.23) | collective-permute-done | bytes 131104 | tf_op jit(solution)/shard_map/ppermute | solution.py:221
  87.9 0.5 collective-permute-start.26
  88.5 0.5 collective-permute-start.28
  89.1 0.2 collective-permute-done.19.refs_7_
  89.3 1.4 %shard_map.97 = (bf16[8,256,512]{2,1,0:T(8,128)(2,1)S(1)}, f32[256,1]{1,0:T(8,128)S(1)}) custom-call(bf16[256,128]{1,0:T(8,128)(2,1)S(1)} %get-tuple-element.43.after_ref.q_ref, bf16[512,128]{1,0:T(8,128)(2,1)S(1)} %shard_map.96.refs_0_, bf16[512,128]{1,0:T(8,128)(2,1)S(1)} %collective-permute-done.13.refs_1_, ...), custom_call_target="tpu_custom_call" | custom-call | flops 268435456 | bytes 3212288 | tf_op jit(solution)/shard_map/pallas_call | solution.py:23
  90.7 1.2 %shard_map.99 = (bf16[128,128]{1,0:T(8,128)(2,1)S(1)}, bf16[128,128]{1,0:T(8,128)(2,1)S(1)}, bf16[128,128]{1,0:T(8,128)(2,1)S(1)}, bf16[128,128]{1,0:T(8,128)(2,1)S(1)}) custom-call(s32[4]{0:T(128)S(1)} %pad_add_fusion.at_ref, bf16[8,256,512]{2,1,0:T(8,128)(2,1)S(1)} %get-tuple-element.66.p_ref, f32[256,1]{1,0:T(8,128)S(1)} %get-tuple-element.67.l_ref, ...), custom_call_target="tpu_custom_call" | custom-call | flops 268435456 | bytes 3343376 | tf_op jit(solution)/shard_map/pallas_call | solution.py:23
  91.9 3.0 %collective-permute-start.30 = (bf16[128,128]{1,0:T(8,128)(2,1)S(1)}, bf16[128,128]{1,0:T(8,128)(2,1)S(1)}, u32[]{:S(2)}, u32[]{:S(2)}) collective-permute-start(bf16[128,128]{1,0:T(8,128)(2,1)S(1)} %get-tuple-element.72), channel_id=1, source_target_pairs={{0,0},{2,2},{4,4},{6,6},{1,64},{3,66},{5,68},{7,70},{8,128},{10,13... | collective-permute-start | bytes 98312 | tf_op jit(solution)/shard_map/ppermute | solution.py:217
  94.9 2.4 %collective-permute-start.31 = (bf16[128,128]{1,0:T(8,128)(2,1)S(1)}, bf16[128,128]{1,0:T(8,128)(2,1)S(1)}, u32[]{:S(2)}, u32[]{:S(2)}) collective-permute-start(bf16[128,128]{1,0:T(8,128)(2,1)S(1)} %get-tuple-element.73), channel_id=1, source_target_pairs={{0,2},{2,4},{4,6},{6,0},{1,66},{3,68},{5,70},{7,64},{8,130},{10,13... | collective-permute-start | bytes 98312 | tf_op jit(solution)/shard_map/ppermute | solution.py:217
  97.3 1.6 %collective-permute-start.32 = (bf16[128,128]{1,0:T(8,128)(2,1)S(1)}, bf16[128,128]{1,0:T(8,128)(2,1)S(1)}, u32[]{:S(2)}, u32[]{:S(2)}) collective-permute-start(bf16[128,128]{1,0:T(8,128)(2,1)S(1)} %get-tuple-element.74), channel_id=1, source_target_pairs={{0,4},{2,6},{4,0},{6,2},{1,68},{3,70},{5,64},{7,66},{8,132},{10,13... | collective-permute-start | bytes 98312 | tf_op jit(solution)/shard_map/ppermute | solution.py:217
  98.8 3.9 %collective-permute-start.33 = (bf16[128,128]{1,0:T(8,128)(2,1)S(1)}, bf16[128,128]{1,0:T(8,128)(2,1)S(1)}, u32[]{:S(2)}, u32[]{:S(2)}) collective-permute-start(bf16[128,128]{1,0:T(8,128)(2,1)S(1)} %get-tuple-element.75), channel_id=1, source_target_pairs={{0,6},{2,0},{4,2},{6,4},{1,70},{3,64},{5,66},{7,68},{8,134},{10,12... | collective-permute-start | bytes 98312 | tf_op jit(solution)/shard_map/ppermute | solution.py:217
  102.8 3.3 %collective-permute-done.32.refs_2_ = bf16[128,128]{1,0:T(8,128)(2,1)S(1)} collective-permute-done((bf16[128,128]{1,0:T(8,128)(2,1)S(1)}, bf16[128,128]{1,0:T(8,128)(2,1)S(1)}, u32[]{:S(2)}, u32[]{:S(2)}) %collective-permute-start.32) | collective-permute-done | bytes 32800 | tf_op jit(solution)/shard_map/ppermute | solution.py:217
  106.1 1.2 %shard_map.100 = (f32[64,512]{1,0:T(8,128)}, bf16[64,512]{1,0:T(8,128)(2,1)}) custom-call(s32[4]{0:T(128)S(1)} %pad_add_fusion.at_ref, bf16[128,128]{1,0:T(8,128)(2,1)S(1)} %collective-permute-done.30.refs_0_, bf16[128,128]{1,0:T(8,128)(2,1)S(1)} %collective-permute-done.31.refs_1_, bf16[128,128]{1,0:T(8,128)(2,1)S(1)} %collective-permute-done.32.refs_2_, ...), custom_call_target="tpu_custom_call" | custom-call | bytes 327696 | tf_op jit(solution)/shard_map/pallas_call | solution.py:23
  (48 shorter events, 0.8 us)
Async XLA Ops:
  0.6 12.9 %copy-start.2 = (bf16[64,512]{1,0:T(8,128)(2,1)S(1)}, bf16[64,512]{1,0:T(8,128)(2,1)}, u32[]{:S(2)}) copy-start(bf16[64,512]{1,0:T(8,128)(2,1)} %q_ref.2) | copy-start | bytes 196612
  0.6 12.9 %copy-start = (bf16[64,512]{1,0:T(8,128)(2,1)S(1)}, bf16[64,512]{1,0:T(8,128)(2,1)}, u32[]{:S(2)}) copy-start(bf16[64,512]{1,0:T(8,128)(2,1)} %k_ref.2) | copy-start | bytes 196612
  0.7 12.9 %copy-start.1 = (bf16[64,512]{1,0:T(8,128)(2,1)S(1)}, bf16[64,512]{1,0:T(8,128)(2,1)}, u32[]{:S(2)}) copy-start(bf16[64,512]{1,0:T(8,128)(2,1)} %v_ref.2) | copy-start | bytes 196612
  3.2 40.7 %all-to-all-start = ((bf16[16,208,128]{2,1,0:T(8,128)(2,1)}), bf16[16,208,128]{2,1,0:T(8,128)(2,1)S(1)}, u32[]{:S(2)}, u32[]{:S(2)}) async-start(bf16[16,208,128]{2,1,0:T(8,128)(2,1)} %shard_map.88), calls=%async_computation | async-start | bytes 1703936 | tf_op jit(solution)/shard_map/all_to_all | solution.py:251
  14.3 14.6 %collective-permute-start = (bf16[192,128]{1,0:T(8,128)(2,1)S(1)}, bf16[192,128]{1,0:T(8,128)(2,1)S(1)}, u32[]{:S(2)}, u32[]{:S(2)}) collective-permute-start(bf16[192,128]{1,0:T(8,128)(2,1)S(1)} %get-tuple-element.39), channel_id=1, source_target_pairs={{0,0},{2,2},{4,4},{6,6},{1,64},{3,66},{5,68},{7,70},{8,128},{10,13... | collective-permute-start | bytes 147464 | tf_op jit(solution)/shard_map/ppermute | solution.py:217
  18.9 22.4 %collective-permute-start.1 = (bf16[192,128]{1,0:T(8,128)(2,1)S(1)}, bf16[192,128]{1,0:T(8,128)(2,1)S(1)}, u32[]{:S(2)}, u32[]{:S(2)}) collective-permute-start(bf16[192,128]{1,0:T(8,128)(2,1)S(1)} %get-tuple-element.40), channel_id=1, source_target_pairs={{0,2},{2,4},{4,6},{6,0},{1,66},{3,68},{5,70},{7,64},{8,130},{10,13... | collective-permute-start | bytes 147464 | tf_op jit(solution)/shard_map/ppermute | solution.py:217
  20.8 22.5 %collective-permute-start.2 = (bf16[192,128]{1,0:T(8,128)(2,1)S(1)}, bf16[192,128]{1,0:T(8,128)(2,1)S(1)}, u32[]{:S(2)}, u32[]{:S(2)}) collective-permute-start(bf16[192,128]{1,0:T(8,128)(2,1)S(1)} %get-tuple-element.41), channel_id=1, source_target_pairs={{0,4},{2,6},{4,0},{6,2},{1,68},{3,70},{5,64},{7,66},{8,132},{10,13... | collective-permute-start | bytes 147464 | tf_op jit(solution)/shard_map/ppermute | solution.py:217
  25.9 17.4 %collective-permute-start.3 = (bf16[192,128]{1,0:T(8,128)(2,1)S(1)}, bf16[192,128]{1,0:T(8,128)(2,1)S(1)}, u32[]{:S(2)}, u32[]{:S(2)}) collective-permute-start(bf16[192,128]{1,0:T(8,128)(2,1)S(1)} %get-tuple-element.42), channel_id=1, source_target_pairs={{0,6},{2,0},{4,2},{6,4},{1,70},{3,64},{5,66},{7,68},{8,134},{10,12... | collective-permute-start | bytes 147464 | tf_op jit(solution)/shard_map/ppermute | solution.py:217
  44.1 13.1 %collective-permute-start.5 = (bf16[1024,128]{1,0:T(8,128)(2,1)S(1)}, bf16[1024,128]{1,0:T(8,128)(2,1)S(1)}, u32[]{:S(2)}, u32[]{:S(2)}) collective-permute-start(bf16[1024,128]{1,0:T(8,128)(2,1)S(1)} %get-tuple-element.47.k_ref), channel_id=1, source_target_pairs={{0,16},{16,32},{32,48},{48,0},{1,17},{17,33},{33,49},{49,1},{2,18}... | collective-permute-start | bytes 786440 | tf_op jit(solution)/shard_map/ppermute | solution.py:221
  45.7 9.2 %collective-permute-start.6 = (bf16[1024,128]{1,0:T(8,128)(2,1)S(1)}, bf16[1024,128]{1,0:T(8,128)(2,1)S(1)}, u32[]{:S(2)}, u32[]{:S(2)}) collective-permute-start(bf16[1024,128]{1,0:T(8,128)(2,1)S(1)} %get-tuple-element.47.k_ref), channel_id=1, source_target_pairs={{0,48},{16,0},{32,16},{48,32},{1,49},{17,1},{33,17},{49,33},{2,50}... | collective-permute-start | bytes 786440 | tf_op jit(solution)/shard_map/ppermute | solution.py:221
  48.6 10.2 %collective-permute-start.7 = (bf16[1024,128]{1,0:T(8,128)(2,1)S(1)}, bf16[1024,128]{1,0:T(8,128)(2,1)S(1)}, u32[]{:S(2)}, u32[]{:S(2)}) collective-permute-start(bf16[1024,128]{1,0:T(8,128)(2,1)S(1)} %get-tuple-element.58.refs_9_), channel_id=1, source_target_pairs={{0,16},{16,32},{32,48},{48,0},{1,17},{17,33},{33,49},{49,1},{2,18}... | collective-permute-start | bytes 786440 | tf_op jit(solution)/shard_map/ppermute | solution.py:221
  49.0 10.5 %collective-permute-start.8 = (bf16[1024,128]{1,0:T(8,128)(2,1)S(1)}, bf16[1024,128]{1,0:T(8,128)(2,1)S(1)}, u32[]{:S(2)}, u32[]{:S(2)}) collective-permute-start(bf16[1024,128]{1,0:T(8,128)(2,1)S(1)} %get-tuple-element.58.refs_9_), channel_id=1, source_target_pairs={{0,48},{16,0},{32,16},{48,32},{1,49},{17,1},{33,17},{49,33},{2,50}... | collective-permute-start | bytes 786440 | tf_op jit(solution)/shard_map/ppermute | solution.py:221
  54.9 11.8 %collective-permute-start.10 = (bf16[512,128]{1,0:T(8,128)(2,1)S(1)}, bf16[512,128]{1,0:T(8,128)(2,1)S(1)}, u32[]{:S(2)}, u32[]{:S(2)}) collective-permute-start(bf16[512,128]{1,0:T(8,128)(2,1)S(1)} %slice.17), channel_id=1, source_target_pairs={{0,48},{16,0},{32,16},{48,32},{1,49},{17,1},{33,17},{49,33},{2,50}... | collective-permute-start | bytes 393224 | tf_op jit(solution)/shard_map/ppermute | solution.py:221
  57.2 9.5 %collective-permute-start.9 = (bf16[512,128]{1,0:T(8,128)(2,1)S(1)}, bf16[512,128]{1,0:T(8,128)(2,1)S(1)}, u32[]{:S(2)}, u32[]{:S(2)}) collective-permute-start(bf16[512,128]{1,0:T(8,128)(2,1)S(1)} %slice.16), channel_id=1, source_target_pairs={{0,16},{16,32},{32,48},{48,0},{1,17},{17,33},{33,49},{49,1},{2,18}... | collective-permute-start | bytes 393224 | tf_op jit(solution)/shard_map/ppermute | solution.py:221
  57.3 14.1 %collective-permute-start.4 = (bf16[512,128]{1,0:T(8,128)(2,1)S(1)}, bf16[512,128]{1,0:T(8,128)(2,1)S(1)}, u32[]{:S(2)}, u32[]{:S(2)}) collective-permute-start(bf16[512,128]{1,0:T(8,128)(2,1)S(1)} %get-tuple-element.44.kv_ref.bv_ref), channel_id=1, source_target_pairs={{0,128},{128,0},{1,129},{129,1},{2,130},{130,2},{3,131},{131,3},{4... | collective-permute-start | bytes 393224 | tf_op jit(solution)/shard_map/ppermute | solution.py:225
  58.8 9.1 %collective-permute-start.11 = (bf16[512,128]{1,0:T(8,128)(2,1)S(1)}, bf16[512,128]{1,0:T(8,128)(2,1)S(1)}, u32[]{:S(2)}, u32[]{:S(2)}) collective-permute-start(bf16[512,128]{1,0:T(8,128)(2,1)S(1)} %slice.18), channel_id=1, source_target_pairs={{0,16},{16,32},{32,48},{48,0},{1,17},{17,33},{33,49},{49,1},{2,18}... | collective-permute-start | bytes 393224 | tf_op jit(solution)/shard_map/ppermute | solution.py:221
  59.5 8.4 %collective-permute-start.12 = (bf16[512,128]{1,0:T(8,128)(2,1)S(1)}, bf16[512,128]{1,0:T(8,128)(2,1)S(1)}, u32[]{:S(2)}, u32[]{:S(2)}) collective-permute-start(bf16[512,128]{1,0:T(8,128)(2,1)S(1)} %slice.19), channel_id=1, source_target_pairs={{0,48},{16,0},{32,16},{48,32},{1,49},{17,1},{33,17},{49,33},{2,50}... | collective-permute-start | bytes 393224 | tf_op jit(solution)/shard_map/ppermute | solution.py:221
  69.4 5.2 %collective-permute-start.20 = (bf16[512,128]{1,0:T(8,128)(2,1)S(1)}, bf16[512,128]{1,0:T(8,128)(2,1)S(1)}, u32[]{:S(2)}, u32[]{:S(2)}) collective-permute-start(bf16[512,128]{1,0:T(8,128)(2,1)S(1)} %get-tuple-element.65.after_ref), channel_id=1, source_target_pairs={{0,64},{64,0},{1,65},{65,1},{2,66},{66,2},{3,67},{67,3},{4,68},{68... | collective-permute-start | bytes 393224 | tf_op jit(solution)/shard_map/ppermute | solution.py:225
  69.5 6.5 %collective-permute-start.21 = (bf16[512,128]{1,0:T(8,128)(2,1)S(1)}, bf16[512,128]{1,0:T(8,128)(2,1)S(1)}, u32[]{:S(2)}, u32[]{:S(2)}) collective-permute-start(bf16[512,128]{1,0:T(8,128)(2,1)S(1)} %get-tuple-element.69), channel_id=1, source_target_pairs={{0,128},{128,0},{1,129},{129,1},{2,130},{130,2},{3,131},{131,3},{4... | collective-permute-start | bytes 393224 | tf_op jit(solution)/shard_map/ppermute | solution.py:225
  70.2 7.6 %collective-permute-start.22 = (bf16[512,128]{1,0:T(8,128)(2,1)S(1)}, bf16[512,128]{1,0:T(8,128)(2,1)S(1)}, u32[]{:S(2)}, u32[]{:S(2)}) collective-permute-start(bf16[512,128]{1,0:T(8,128)(2,1)S(1)} %get-tuple-element.65.after_ref), channel_id=1, source_target_pairs={{0,192},{64,128},{128,64},{192,0},{1,193},{65,129},{129,65},{193,1... | collective-permute-start | bytes 393224 | tf_op jit(solution)/shard_map/ppermute | solution.py:312
  71.4 9.9 %collective-permute-start.13 = (bf16[512,128]{1,0:T(8,128)(2,1)S(1)}, bf16[512,128]{1,0:T(8,128)(2,1)S(1)}, u32[]{:S(2)}, u32[]{:S(2)}) collective-permute-start(bf16[512,128]{1,0:T(8,128)(2,1)S(1)} %shard_map.96.refs_0_), channel_id=1, source_target_pairs={{0,16},{16,32},{32,48},{48,0},{1,17},{17,33},{33,49},{49,1},{2,18}... | collective-permute-start | bytes 393224 | tf_op jit(solution)/shard_map/ppermute | solution.py:221
  71.5 10.5 %collective-permute-start.14 = (bf16[512,128]{1,0:T(8,128)(2,1)S(1)}, bf16[512,128]{1,0:T(8,128)(2,1)S(1)}, u32[]{:S(2)}, u32[]{:S(2)}) collective-permute-start(bf16[512,128]{1,0:T(8,128)(2,1)S(1)} %shard_map.96.refs_0_), channel_id=1, source_target_pairs={{0,32},{16,48},{32,0},{48,16},{1,33},{17,49},{33,1},{49,17},{2,34}... | collective-permute-start | bytes 393224 | tf_op jit(solution)/shard_map/ppermute | solution.py:221
  74.6 8.0 %collective-permute-start.15 = (bf16[512,128]{1,0:T(8,128)(2,1)S(1)}, bf16[512,128]{1,0:T(8,128)(2,1)S(1)}, u32[]{:S(2)}, u32[]{:S(2)}) collective-permute-start(bf16[512,128]{1,0:T(8,128)(2,1)S(1)} %shard_map.96.refs_0_), channel_id=1, source_target_pairs={{0,48},{16,0},{32,16},{48,32},{1,49},{17,1},{33,17},{49,33},{2,50}... | collective-permute-start | bytes 393224 | tf_op jit(solution)/shard_map/ppermute | solution.py:221
  76.0 6.5 %collective-permute-start.16 = (bf16[512,128]{1,0:T(8,128)(2,1)S(1)}, bf16[512,128]{1,0:T(8,128)(2,1)S(1)}, u32[]{:S(2)}, u32[]{:S(2)}) collective-permute-start(bf16[512,128]{1,0:T(8,128)(2,1)S(1)} %shard_map.96.refs_0_), channel_id=1, source_target_pairs={{0,64},{64,0},{1,65},{65,1},{2,66},{66,2},{3,67},{67,3},{4,68},{68... | collective-permute-start | bytes 393224 | tf_op jit(solution)/shard_map/ppermute | solution.py:225
  77.8 10.1 %collective-permute-start.23 = (bf16[512,128]{1,0:T(8,128)(2,1)S(1)}, bf16[512,128]{1,0:T(8,128)(2,1)S(1)}, u32[]{:S(2)}, u32[]{:S(2)}) collective-permute-start(bf16[512,128]{1,0:T(8,128)(2,1)S(1)} %get-tuple-element.71.refs_0_), channel_id=1, source_target_pairs={{0,16},{16,32},{32,48},{48,0},{1,17},{17,33},{33,49},{49,1},{2,18}... | collective-permute-start | bytes 393224 | tf_op jit(solution)/shard_map/ppermute | solution.py:221
  81.2 6.7 %collective-permute-start.24 = (bf16[512,128]{1,0:T(8,128)(2,1)S(1)}, bf16[512,128]{1,0:T(8,128)(2,1)S(1)}, u32[]{:S(2)}, u32[]{:S(2)}) collective-permute-start(bf16[512,128]{1,0:T(8,128)(2,1)S(1)} %get-tuple-element.71.refs_0_), channel_id=1, source_target_pairs={{0,32},{16,48},{32,0},{48,16},{1,33},{17,49},{33,1},{49,17},{2,34}... | collective-permute-start | bytes 393224 | tf_op jit(solution)/shard_map/ppermute | solution.py:221
  81.9 6.5 %collective-permute-start.25 = (bf16[512,128]{1,0:T(8,128)(2,1)S(1)}, bf16[512,128]{1,0:T(8,128)(2,1)S(1)}, u32[]{:S(2)}, u32[]{:S(2)}) collective-permute-start(bf16[512,128]{1,0:T(8,128)(2,1)S(1)} %get-tuple-element.71.refs_0_), channel_id=1, source_target_pairs={{0,48},{16,0},{32,16},{48,32},{1,49},{17,1},{33,17},{49,33},{2,50}... | collective-permute-start | bytes 393224 | tf_op jit(solution)/shard_map/ppermute | solution.py:221
  82.6 6.0 %collective-permute-start.17 = (bf16[512,128]{1,0:T(8,128)(2,1)S(1)}, bf16[512,128]{1,0:T(8,128)(2,1)S(1)}, u32[]{:S(2)}, u32[]{:S(2)}) collective-permute-start(bf16[512,128]{1,0:T(8,128)(2,1)S(1)} %collective-permute-done.13.refs_1_), channel_id=1, source_target_pairs={{0,64},{64,0},{1,65},{65,1},{2,66},{66,2},{3,67},{67,3},{4,68},{68... | collective-permute-start | bytes 393224 | tf_op jit(solution)/shard_map/ppermute | solution.py:225
  82.6 6.4 %collective-permute-start.18 = (bf16[512,128]{1,0:T(8,128)(2,1)S(1)}, bf16[512,128]{1,0:T(8,128)(2,1)S(1)}, u32[]{:S(2)}, u32[]{:S(2)}) collective-permute-start(bf16[512,128]{1,0:T(8,128)(2,1)S(1)} %collective-permute-done.14.refs_2_), channel_id=1, source_target_pairs={{0,64},{64,0},{1,65},{65,1},{2,66},{66,2},{3,67},{67,3},{4,68},{68... | collective-permute-start | bytes 393224 | tf_op jit(solution)/shard_map/ppermute | solution.py:225
  87.9 1.3 %collective-permute-start.19 = (bf16[512,128]{1,0:T(8,128)(2,1)S(1)}, bf16[512,128]{1,0:T(8,128)(2,1)S(1)}, u32[]{:S(2)}, u32[]{:S(2)}) collective-permute-start(bf16[512,128]{1,0:T(8,128)(2,1)S(1)} %collective-permute-done.15.refs_3_), channel_id=1, source_target_pairs={{0,64},{64,0},{1,65},{65,1},{2,66},{66,2},{3,67},{67,3},{4,68},{68... | collective-permute-start | bytes 393224 | tf_op jit(solution)/shard_map/ppermute | solution.py:225
  87.9 2.7 %collective-permute-start.26 = (bf16[512,128]{1,0:T(8,128)(2,1)S(1)}, bf16[512,128]{1,0:T(8,128)(2,1)S(1)}, u32[]{:S(2)}, u32[]{:S(2)}) collective-permute-start(bf16[512,128]{1,0:T(8,128)(2,1)S(1)} %get-tuple-element.71.refs_0_), channel_id=1, source_target_pairs={{0,64},{64,0},{1,65},{65,1},{2,66},{66,2},{3,67},{67,3},{4,68},{68... | collective-permute-start | bytes 393224 | tf_op jit(solution)/shard_map/ppermute | solution.py:225
  88.5 2.2 %collective-permute-start.27 = (bf16[512,128]{1,0:T(8,128)(2,1)S(1)}, bf16[512,128]{1,0:T(8,128)(2,1)S(1)}, u32[]{:S(2)}, u32[]{:S(2)}) collective-permute-start(bf16[512,128]{1,0:T(8,128)(2,1)S(1)} %collective-permute-done.23.refs_1_), channel_id=1, source_target_pairs={{0,64},{64,0},{1,65},{65,1},{2,66},{66,2},{3,67},{67,3},{4,68},{68... | collective-permute-start | bytes 393224 | tf_op jit(solution)/shard_map/ppermute | solution.py:225
  88.5 2.1 %collective-permute-start.28 = (bf16[512,128]{1,0:T(8,128)(2,1)S(1)}, bf16[512,128]{1,0:T(8,128)(2,1)S(1)}, u32[]{:S(2)}, u32[]{:S(2)}) collective-permute-start(bf16[512,128]{1,0:T(8,128)(2,1)S(1)} %collective-permute-done.24.refs_2_), channel_id=1, source_target_pairs={{0,64},{64,0},{1,65},{65,1},{2,66},{66,2},{3,67},{67,3},{4,68},{68... | collective-permute-start | bytes 393224 | tf_op jit(solution)/shard_map/ppermute | solution.py:225
  89.0 1.7 %collective-permute-start.29 = (bf16[512,128]{1,0:T(8,128)(2,1)S(1)}, bf16[512,128]{1,0:T(8,128)(2,1)S(1)}, u32[]{:S(2)}, u32[]{:S(2)}) collective-permute-start(bf16[512,128]{1,0:T(8,128)(2,1)S(1)} %collective-permute-done.25.refs_3_), channel_id=1, source_target_pairs={{0,64},{64,0},{1,65},{65,1},{2,66},{66,2},{3,67},{67,3},{4,68},{68... | collective-permute-start | bytes 393224 | tf_op jit(solution)/shard_map/ppermute | solution.py:225
  91.9 10.8 %collective-permute-start.30 = (bf16[128,128]{1,0:T(8,128)(2,1)S(1)}, bf16[128,128]{1,0:T(8,128)(2,1)S(1)}, u32[]{:S(2)}, u32[]{:S(2)}) collective-permute-start(bf16[128,128]{1,0:T(8,128)(2,1)S(1)} %get-tuple-element.72), channel_id=1, source_target_pairs={{0,0},{2,2},{4,4},{6,6},{1,64},{3,66},{5,68},{7,70},{8,128},{10,13... | collective-permute-start | bytes 98312 | tf_op jit(solution)/shard_map/ppermute | solution.py:217
  94.9 7.9 %collective-permute-start.31 = (bf16[128,128]{1,0:T(8,128)(2,1)S(1)}, bf16[128,128]{1,0:T(8,128)(2,1)S(1)}, u32[]{:S(2)}, u32[]{:S(2)}) collective-permute-start(bf16[128,128]{1,0:T(8,128)(2,1)S(1)} %get-tuple-element.73), channel_id=1, source_target_pairs={{0,2},{2,4},{4,6},{6,0},{1,66},{3,68},{5,70},{7,64},{8,130},{10,13... | collective-permute-start | bytes 98312 | tf_op jit(solution)/shard_map/ppermute | solution.py:217
  97.3 8.8 %collective-permute-start.32 = (bf16[128,128]{1,0:T(8,128)(2,1)S(1)}, bf16[128,128]{1,0:T(8,128)(2,1)S(1)}, u32[]{:S(2)}, u32[]{:S(2)}) collective-permute-start(bf16[128,128]{1,0:T(8,128)(2,1)S(1)} %get-tuple-element.74), channel_id=1, source_target_pairs={{0,4},{2,6},{4,0},{6,2},{1,68},{3,70},{5,64},{7,66},{8,132},{10,13... | collective-permute-start | bytes 98312 | tf_op jit(solution)/shard_map/ppermute | solution.py:217
  98.8 7.2 %collective-permute-start.33 = (bf16[128,128]{1,0:T(8,128)(2,1)S(1)}, bf16[128,128]{1,0:T(8,128)(2,1)S(1)}, u32[]{:S(2)}, u32[]{:S(2)}) collective-permute-start(bf16[128,128]{1,0:T(8,128)(2,1)S(1)} %get-tuple-element.75), channel_id=1, source_target_pairs={{0,6},{2,0},{4,2},{6,4},{1,70},{3,64},{5,66},{7,68},{8,134},{10,12... | collective-permute-start | bytes 98312 | tf_op jit(solution)/shard_map/ppermute | solution.py:217

commit v5 on v4

--- a/solution.py
+++ b/solution.py
@@ -60,11 +60,14 @@
     code.wait()
     row = jnp.concatenate([code_row[...].astype(F32), jnp.zeros((1, 64), F32)], axis=1)
     held[:, 192:208] = jnp.broadcast_to(row.reshape(1, 1, 128), (HEADS, 16, DIM)).astype(BF)
-    for copy in copies:
+    outs = []
+    for place in range(HEADS):
+        for copy in copies[place * 3 : place * 3 + 3]:
+            copy.wait()
+        outs.append(pltpu.make_async_copy(held.at[place], out_ref.at[place], sem.at[49 + place]))
+        outs[-1].start()
+    for copy in outs:
         copy.wait()
-    last = pltpu.make_async_copy(held, out_ref, sem.at[49])
-    last.start()
-    last.wait()
 
 
 def base_pack_kernel(at_ref, k_ref, v_ref, q_ref, *refs):
@@ -110,8 +113,8 @@
 
 def score_kernel(q_ref, *refs):
     keys, (p_ref, m_ref, l_ref) = refs[:-3], refs[-3:]
-    for i in range(4):
-        rows = slice(i * 256, (i + 1) * 256)
+    for i in range(8):
+        rows = slice(i * 128, (i + 1) * 128)
         parts = [dot_nt(q_ref[rows], k[...]) for k in keys]
         s = jnp.concatenate(parts, axis=1) if len(parts) > 1 else parts[0]
         m = jnp.max(s, axis=1, keepdims=True)
@@ -135,8 +138,8 @@
 
 def middle_kernel(*refs):
     ms, ls, ps, vs, (m_ref, l_ref, acc_ref) = refs[0:3], refs[3:6], refs[6:9], refs[9:12], refs[12:]
-    for i in range(4):
-        rows = slice(i * 256, (i + 1) * 256)
+    for i in range(8):
+        rows = slice(i * 128, (i + 1) * 128)
         best, weights, total = merge(rows, ms, ls)
         m_ref[rows] = best
         l_ref[rows] = total
@@ -246,7 +249,7 @@
         specs=[ANY] * 4,
         out_specs=[ANY],
         vmem=60,
-        scratch=[pltpu.VMEM((1, 64), jnp.int32), pltpu.VMEM((HEADS, 208, DIM), BF), pltpu.SemaphoreType.DMA((50,))],
+        scratch=[pltpu.VMEM((1, 64), jnp.int32), pltpu.VMEM((HEADS, 208, DIM), BF), pltpu.SemaphoreType.DMA((65,))],
     )
     sent = lax.all_to_all(packed, ("yh", "zt", "zp"), 0, 0, tiled=True)
 

time: 108 us -> 107 us (level)
  no operation moved by 1% of the time
where the time goes in v5:
time: 107 us
  starting transfers between devices  58.9 us (55%)
  waiting for transfers between devices  31.3 us (29%)
  Pallas kernels  16 us (15%)
    ppermute x8, starting transfers between devices, swap(): return lax.ppermute(values, ('yl', 'co', 'yh', 'zt', 'zp'), perm)  25.4 us
    ppermute x14, starting transfers between devices, along(): return lax.ppermute(values, axis, [(j, (j + step) % 4) for j in range(4)])  18.7 us
    ppermute x8, waiting for transfers between devices, swap(): return lax.ppermute(values, ('yl', 'co', 'yh', 'zt', 'zp'), perm)  17.7 us
    pallas_call x15, Pallas kernels, call(): pl.pallas_call(body, out_shape=outs, in_specs=specs or [VM] * len(operand...  16 us
    ppermute x14, waiting for transfers between devices, along(): return lax.ppermute(values, axis, [(j, (j + step) % 4) for j in range(4)])  11.7 us
    all_to_all x1, starting transfers between devices, shards(): sent = lax.all_to_all(packed, ('yh', 'zt', 'zp'), 0, 0, tiled=True)  10.3 us
    ppermute x11, starting transfers between devices, other(): return lax.ppermute(values, axis, [(0, 1), (1, 0)])  3.32 us
  transfers between devices with their start and end apart: 35, of which 10 were waited for; matrix products, arithmetic and copies ran while one was open for 0% of the time, Pallas kernels for 10%

profile of v5, /device:TPU:8, one launch (start us, length us, event | category | flops | bytes accessed | tf_op | source)
XLA Modules:
  0.0 107.1 jit_solution(15129239135702067097)
XLA Ops:
  0.7 2.4 %shard_map.88 = bf16[16,208,128]{2,1,0:T(8,128)(2,1)} custom-call(bf16[1,64,2048]{2,1,0:T(8,128)(2,1)} %k_ref.3, bf16[1,64,2048]{2,1,0:T(8,128)(2,1)} %v_ref.3, bf16[1,64,2048]{2,1,0:T(8,128)(2,1)} %q_ref.3, s32[1,64]{1,0:T(1,128)} %code_ref.1), custom_call_target="tpu_custom_call" | custom-call | bytes 1638656 | tf_op jit(solution)/shard_map/pallas_call | solution.py:23
  3.0 10.3 %all-to-all-start = ((bf16[16,208,128]{2,1,0:T(8,128)(2,1)}), bf16[16,208,128]{2,1,0:T(8,128)(2,1)S(1)}, u32[]{:S(2)}, u32[]{:S(2)}) async-start(bf16[16,208,128]{2,1,0:T(8,128)(2,1)} %shard_map.88), calls=%async_computation | async-start | bytes 1703936 | tf_op jit(solution)/shard_map/all_to_all | solution.py:254
  13.4 0.7 shard_map.86
  14.2 4.6 %collective-permute-start = (bf16[192,128]{1,0:T(8,128)(2,1)S(1)}, bf16[192,128]{1,0:T(8,128)(2,1)S(1)}, u32[]{:S(2)}, u32[]{:S(2)}) collective-permute-start(bf16[192,128]{1,0:T(8,128)(2,1)S(1)} %get-tuple-element.39), channel_id=1, source_target_pairs={{0,0},{2,2},{4,4},{6,6},{1,64},{3,66},{5,68},{7,70},{8,128},{10,13... | collective-permute-start | bytes 147464 | tf_op jit(solution)/shard_map/ppermute | solution.py:220
  18.8 1.9 %collective-permute-start.1 = (bf16[192,128]{1,0:T(8,128)(2,1)S(1)}, bf16[192,128]{1,0:T(8,128)(2,1)S(1)}, u32[]{:S(2)}, u32[]{:S(2)}) collective-permute-start(bf16[192,128]{1,0:T(8,128)(2,1)S(1)} %get-tuple-element.40), channel_id=1, source_target_pairs={{0,2},{2,4},{4,6},{6,0},{1,66},{3,68},{5,70},{7,64},{8,130},{10,13... | collective-permute-start | bytes 147464 | tf_op jit(solution)/shard_map/ppermute | solution.py:220
  20.7 5.0 %collective-permute-start.2 = (bf16[192,128]{1,0:T(8,128)(2,1)S(1)}, bf16[192,128]{1,0:T(8,128)(2,1)S(1)}, u32[]{:S(2)}, u32[]{:S(2)}) collective-permute-start(bf16[192,128]{1,0:T(8,128)(2,1)S(1)} %get-tuple-element.41), channel_id=1, source_target_pairs={{0,4},{2,6},{4,0},{6,2},{1,68},{3,70},{5,64},{7,66},{8,132},{10,13... | collective-permute-start | bytes 147464 | tf_op jit(solution)/shard_map/ppermute | solution.py:220
  25.7 3.0 %collective-permute-start.3 = (bf16[192,128]{1,0:T(8,128)(2,1)S(1)}, bf16[192,128]{1,0:T(8,128)(2,1)S(1)}, u32[]{:S(2)}, u32[]{:S(2)}) collective-permute-start(bf16[192,128]{1,0:T(8,128)(2,1)S(1)} %get-tuple-element.42), channel_id=1, source_target_pairs={{0,6},{2,0},{4,2},{6,4},{1,70},{3,64},{5,66},{7,68},{8,134},{10,12... | collective-permute-start | bytes 147464 | tf_op jit(solution)/shard_map/ppermute | solution.py:220
  28.7 12.4 %collective-permute-done.1.refs_1_ = bf16[192,128]{1,0:T(8,128)(2,1)S(1)} collective-permute-done((bf16[192,128]{1,0:T(8,128)(2,1)S(1)}, bf16[192,128]{1,0:T(8,128)(2,1)S(1)}, u32[]{:S(2)}, u32[]{:S(2)}) %collective-permute-start.1) | collective-permute-done | bytes 49184 | tf_op jit(solution)/shard_map/ppermute | solution.py:220
  41.2 2.0 %collective-permute-done.2.refs_2_ = bf16[192,128]{1,0:T(8,128)(2,1)S(1)} collective-permute-done((bf16[192,128]{1,0:T(8,128)(2,1)S(1)}, bf16[192,128]{1,0:T(8,128)(2,1)S(1)}, u32[]{:S(2)}, u32[]{:S(2)}) %collective-permute-start.2) | collective-permute-done | bytes 49184 | tf_op jit(solution)/shard_map/ppermute | solution.py:220
  43.1 0.6 shard_map.87
  43.7 0.2 shard_map.89
  44.0 1.6 %collective-permute-start.5 = (bf16[1024,128]{1,0:T(8,128)(2,1)S(1)}, bf16[1024,128]{1,0:T(8,128)(2,1)S(1)}, u32[]{:S(2)}, u32[]{:S(2)}) collective-permute-start(bf16[1024,128]{1,0:T(8,128)(2,1)S(1)} %get-tuple-element.47.k_ref), channel_id=1, source_target_pairs={{0,16},{16,32},{32,48},{48,0},{1,17},{17,33},{33,49},{49,1},{2,18}... | collective-permute-start | bytes 786440 | tf_op jit(solution)/shard_map/ppermute | solution.py:224
  45.5 1.7 %collective-permute-start.6 = (bf16[1024,128]{1,0:T(8,128)(2,1)S(1)}, bf16[1024,128]{1,0:T(8,128)(2,1)S(1)}, u32[]{:S(2)}, u32[]{:S(2)}) collective-permute-start(bf16[1024,128]{1,0:T(8,128)(2,1)S(1)} %get-tuple-element.47.k_ref), channel_id=1, source_target_pairs={{0,48},{16,0},{32,16},{48,32},{1,49},{17,1},{33,17},{49,33},{2,50}... | collective-permute-start | bytes 786440 | tf_op jit(solution)/shard_map/ppermute | solution.py:224
  47.3 1.2 %shard_map.90 = (bf16[1024,1024]{1,0:T(8,128)(2,1)S(1)}, f32[1024,1]{1,0:T(8,128)S(1)}, f32[1024,1]{1,0:T(8,128)S(1)}, bf16[1024,128]{1,0:T(8,128)(2,1)S(1)}) custom-call(bf16[1024,128]{1,0:T(8,128)(2,1)S(1)} %get-tuple-element.46.q_ref, bf16[1024,128]{1,0:T(8,128)(2,1)S(1)} %get-tuple-element.47.k_ref, ...), custom_call_target="tpu_custom_call", output_to_operand_aliasing={{3}: (2, {})} | custom-call | flops 268435456 | bytes 3153920 | tf_op jit(solution)/shard_map/pallas_call | solution.py:23
  48.5 0.3 collective-permute-start.7
  48.8 3.0 %collective-permute-start.8 = (bf16[1024,128]{1,0:T(8,128)(2,1)S(1)}, bf16[1024,128]{1,0:T(8,128)(2,1)S(1)}, u32[]{:S(2)}, u32[]{:S(2)}) collective-permute-start(bf16[1024,128]{1,0:T(8,128)(2,1)S(1)} %get-tuple-element.58.refs_9_), channel_id=1, source_target_pairs={{0,48},{16,0},{32,16},{48,32},{1,49},{17,1},{33,17},{49,33},{2,50}... | collective-permute-start | bytes 786440 | tf_op jit(solution)/shard_map/ppermute | solution.py:224
  51.8 2.8 %collective-permute-done.6.refs_0_ = bf16[1024,128]{1,0:T(8,128)(2,1)S(1)} collective-permute-done((bf16[1024,128]{1,0:T(8,128)(2,1)S(1)}, bf16[1024,128]{1,0:T(8,128)(2,1)S(1)}, u32[]{:S(2)}, u32[]{:S(2)}) %collective-permute-start.6) | collective-permute-done | bytes 262176 | tf_op jit(solution)/shard_map/ppermute | solution.py:224
  54.6 2.4 %collective-permute-start.10 = (bf16[512,128]{1,0:T(8,128)(2,1)S(1)}, bf16[512,128]{1,0:T(8,128)(2,1)S(1)}, u32[]{:S(2)}, u32[]{:S(2)}) collective-permute-start(bf16[512,128]{1,0:T(8,128)(2,1)S(1)} %slice.17), channel_id=1, source_target_pairs={{0,48},{16,0},{32,16},{48,32},{1,49},{17,1},{33,17},{49,33},{2,50}... | collective-permute-start | bytes 393224 | tf_op jit(solution)/shard_map/ppermute | solution.py:224
  57.1 0.9 collective-permute-start.4
  58.1 0.6 collective-permute-done.7.refs_10_
  58.7 0.7 collective-permute-start.11
  59.4 2.9 %collective-permute-start.12 = (bf16[512,128]{1,0:T(8,128)(2,1)S(1)}, bf16[512,128]{1,0:T(8,128)(2,1)S(1)}, u32[]{:S(2)}, u32[]{:S(2)}) collective-permute-start(bf16[512,128]{1,0:T(8,128)(2,1)S(1)} %slice.19), channel_id=1, source_target_pairs={{0,48},{16,0},{32,16},{48,32},{1,49},{17,1},{33,17},{49,33},{2,50}... | collective-permute-start | bytes 393224 | tf_op jit(solution)/shard_map/ppermute | solution.py:224
  62.3 1.2 %shard_map.91 = (bf16[1024,1024]{1,0:T(8,128)(2,1)S(1)}, f32[1024,1]{1,0:T(8,128)S(1)}, f32[1024,1]{1,0:T(8,128)S(1)}) custom-call(bf16[1024,128]{1,0:T(8,128)(2,1)S(1)} %get-tuple-element.46.q_ref, bf16[1024,128]{1,0:T(8,128)(2,1)S(1)} %collective-permute-done.5.refs_0_), custom_call_target="tpu_custom_call" | custom-call | flops 268435456 | bytes 2629632 | tf_op jit(solution)/shard_map/pallas_call | solution.py:23
  63.5 1.2 %shard_map.92 = (bf16[1024,1024]{1,0:T(8,128)(2,1)S(1)}, f32[1024,1]{1,0:T(8,128)S(1)}, f32[1024,1]{1,0:T(8,128)S(1)}) custom-call(bf16[1024,128]{1,0:T(8,128)(2,1)S(1)} %get-tuple-element.46.q_ref, bf16[1024,128]{1,0:T(8,128)(2,1)S(1)} %collective-permute-done.6.refs_0_), custom_call_target="tpu_custom_call" | custom-call | flops 268435456 | bytes 2629632 | tf_op jit(solution)/shard_map/pallas_call | solution.py:23
  64.7 1.9 %shard_map.93 = (f32[1024,1]{1,0:T(8,128)S(1)}, f32[1024,1]{1,0:T(8,128)S(1)}, f32[1024,128]{1,0:T(8,128)S(1)}) custom-call(f32[1024,1]{1,0:T(8,128)S(1)} %get-tuple-element.49.refs_0_, f32[1024,1]{1,0:T(8,128)S(1)} %get-tuple-element.50.refs_1_, f32[1024,1]{1,0:T(8,128)S(1)} %get-tuple-element.51.refs_2_, f32[1024,1]{1,0:T(8,128)S(1)} %get-tuple-element.52.refs_3_, ...), custom_call_target="tpu_custom_call" | custom-call | flops 805306368 | bytes 7634944 | tf_op jit(solution)/shard_map/pallas_call | solution.py:23
  66.6 1.2 %shard_map.94 = (bf16[1024,1024]{1,0:T(8,128)(2,1)S(1)}, f32[1024,1]{1,0:T(8,128)S(1)}, f32[1024,1]{1,0:T(8,128)S(1)}) custom-call(bf16[1024,128]{1,0:T(8,128)(2,1)S(1)} %get-tuple-element.46.q_ref, bf16[512,128]{1,0:T(8,128)(2,1)S(1)} %collective-permute-done.9.refs_0_, bf16[512,128]{1,0:T(8,128)(2,1)S(1)} %collective-permute-done.10.refs_1_), custom_call_target="tpu_custom_call" | custom-call | flops 268435456 | bytes 2629632 | tf_op jit(solution)/shard_map/pallas_call | solution.py:23
  67.8 1.4 %shard_map.95 = (f32[512,128]{1,0:T(8,128)S(1)}, bf16[512,128]{1,0:T(8,128)(2,1)S(1)}, bf16[512,128]{1,0:T(8,128)(2,1)S(1)}) custom-call(s32[4]{0:T(128)S(1)} %pad_add_fusion.at_ref, f32[1024,1]{1,0:T(8,128)S(1)} %get-tuple-element.45.factor_ref, f32[1024,1]{1,0:T(8,128)S(1)} %get-tuple-element.59.refs_0_, f32[1024,1]{1,0:T(8,128)S(1)} %get-tuple-element.60.refs_1_, ...), custom_call_target="tpu_custom_call" | custom-call | flops 268435456 | bytes 3428368 | tf_op jit(solution)/shard_map/pallas_call | solution.py:23
  69.3 0.7 collective-permute-start.21
  70.0 1.2 %collective-permute-start.22 = (bf16[512,128]{1,0:T(8,128)(2,1)S(1)}, bf16[512,128]{1,0:T(8,128)(2,1)S(1)}, u32[]{:S(2)}, u32[]{:S(2)}) collective-permute-start(bf16[512,128]{1,0:T(8,128)(2,1)S(1)} %get-tuple-element.65.after_ref), channel_id=1, source_target_pairs={{0,192},{64,128},{128,64},{192,0},{1,193},{65,129},{129,65},{193,1... | collective-permute-start | bytes 393224 | tf_op jit(solution)/shard_map/ppermute | solution.py:315
  71.3 3.1 %collective-permute-start.14 = (bf16[512,128]{1,0:T(8,128)(2,1)S(1)}, bf16[512,128]{1,0:T(8,128)(2,1)S(1)}, u32[]{:S(2)}, u32[]{:S(2)}) collective-permute-start(bf16[512,128]{1,0:T(8,128)(2,1)S(1)} %shard_map.96.refs_0_), channel_id=1, source_target_pairs={{0,32},{16,48},{32,0},{48,16},{1,33},{17,49},{33,1},{49,17},{2,34}... | collective-permute-start | bytes 393224 | tf_op jit(solution)/shard_map/ppermute | solution.py:224
  74.4 1.4 %collective-permute-start.15 = (bf16[512,128]{1,0:T(8,128)(2,1)S(1)}, bf16[512,128]{1,0:T(8,128)(2,1)S(1)}, u32[]{:S(2)}, u32[]{:S(2)}) collective-permute-start(bf16[512,128]{1,0:T(8,128)(2,1)S(1)} %shard_map.96.refs_0_), channel_id=1, source_target_pairs={{0,48},{16,0},{32,16},{48,32},{1,49},{17,1},{33,17},{49,33},{2,50}... | collective-permute-start | bytes 393224 | tf_op jit(solution)/shard_map/ppermute | solution.py:224
  75.8 1.7 %collective-permute-done.22.both_ref = bf16[512,128]{1,0:T(8,128)(2,1)S(1)} collective-permute-done((bf16[512,128]{1,0:T(8,128)(2,1)S(1)}, bf16[512,128]{1,0:T(8,128)(2,1)S(1)}, u32[]{:S(2)}, u32[]{:S(2)}) %collective-permute-start.22) | collective-permute-done | bytes 131104 | tf_op jit(solution)/shard_map/ppermute | solution.py:315
  77.7 3.3 %collective-permute-done.13.refs_1_ = bf16[512,128]{1,0:T(8,128)(2,1)S(1)} collective-permute-done((bf16[512,128]{1,0:T(8,128)(2,1)S(1)}, bf16[512,128]{1,0:T(8,128)(2,1)S(1)}, u32[]{:S(2)}, u32[]{:S(2)}) %collective-permute-start.13) | collective-permute-done | bytes 131104 | tf_op jit(solution)/shard_map/ppermute | solution.py:224
  81.1 0.7 collective-permute-start.24
  81.8 0.6 collective-permute-start.25
  82.4 0.5 collective-permute-start.18
  82.9 4.8 %collective-permute-done.23.refs_1_ = bf16[512,128]{1,0:T(8,128)(2,1)S(1)} collective-permute-done((bf16[512,128]{1,0:T(8,128)(2,1)S(1)}, bf16[512,128]{1,0:T(8,128)(2,1)S(1)}, u32[]{:S(2)}, u32[]{:S(2)}) %collective-permute-start.23) | collective-permute-done | bytes 131104 | tf_op jit(solution)/shard_map/ppermute | solution.py:224
  87.7 0.5 collective-permute-start.26
  88.3 0.5 collective-permute-start.28
  88.9 0.2 collective-permute-done.19.refs_7_
  89.1 1.4 %shard_map.97 = (bf16[8,256,512]{2,1,0:T(8,128)(2,1)S(1)}, f32[256,1]{1,0:T(8,128)S(1)}) custom-call(bf16[256,128]{1,0:T(8,128)(2,1)S(1)} %get-tuple-element.43.after_ref.q_ref, bf16[512,128]{1,0:T(8,128)(2,1)S(1)} %shard_map.96.refs_0_, bf16[512,128]{1,0:T(8,128)(2,1)S(1)} %collective-permute-done.13.refs_1_, ...), custom_call_target="tpu_custom_call" | custom-call | flops 268435456 | bytes 3212288 | tf_op jit(solution)/shard_map/pallas_call | solution.py:23
  90.5 1.3 %shard_map.99 = (bf16[128,128]{1,0:T(8,128)(2,1)S(1)}, bf16[128,128]{1,0:T(8,128)(2,1)S(1)}, bf16[128,128]{1,0:T(8,128)(2,1)S(1)}, bf16[128,128]{1,0:T(8,128)(2,1)S(1)}) custom-call(s32[4]{0:T(128)S(1)} %pad_add_fusion.at_ref, bf16[8,256,512]{2,1,0:T(8,128)(2,1)S(1)} %get-tuple-element.66.p_ref, f32[256,1]{1,0:T(8,128)S(1)} %get-tuple-element.67.l_ref, ...), custom_call_target="tpu_custom_call" | custom-call | flops 268435456 | bytes 3343376 | tf_op jit(solution)/shard_map/pallas_call | solution.py:23
  91.8 3.0 %collective-permute-start.30 = (bf16[128,128]{1,0:T(8,128)(2,1)S(1)}, bf16[128,128]{1,0:T(8,128)(2,1)S(1)}, u32[]{:S(2)}, u32[]{:S(2)}) collective-permute-start(bf16[128,128]{1,0:T(8,128)(2,1)S(1)} %get-tuple-element.72), channel_id=1, source_target_pairs={{0,0},{2,2},{4,4},{6,6},{1,64},{3,66},{5,68},{7,70},{8,128},{10,13... | collective-permute-start | bytes 98312 | tf_op jit(solution)/shard_map/ppermute | solution.py:220
  94.7 2.4 %collective-permute-start.31 = (bf16[128,128]{1,0:T(8,128)(2,1)S(1)}, bf16[128,128]{1,0:T(8,128)(2,1)S(1)}, u32[]{:S(2)}, u32[]{:S(2)}) collective-permute-start(bf16[128,128]{1,0:T(8,128)(2,1)S(1)} %get-tuple-element.73), channel_id=1, source_target_pairs={{0,2},{2,4},{4,6},{6,0},{1,66},{3,68},{5,70},{7,64},{8,130},{10,13... | collective-permute-start | bytes 98312 | tf_op jit(solution)/shard_map/ppermute | solution.py:220
  97.1 1.6 %collective-permute-start.32 = (bf16[128,128]{1,0:T(8,128)(2,1)S(1)}, bf16[128,128]{1,0:T(8,128)(2,1)S(1)}, u32[]{:S(2)}, u32[]{:S(2)}) collective-permute-start(bf16[128,128]{1,0:T(8,128)(2,1)S(1)} %get-tuple-element.74), channel_id=1, source_target_pairs={{0,4},{2,6},{4,0},{6,2},{1,68},{3,70},{5,64},{7,66},{8,132},{10,13... | collective-permute-start | bytes 98312 | tf_op jit(solution)/shard_map/ppermute | solution.py:220
  98.7 3.9 %collective-permute-start.33 = (bf16[128,128]{1,0:T(8,128)(2,1)S(1)}, bf16[128,128]{1,0:T(8,128)(2,1)S(1)}, u32[]{:S(2)}, u32[]{:S(2)}) collective-permute-start(bf16[128,128]{1,0:T(8,128)(2,1)S(1)} %get-tuple-element.75), channel_id=1, source_target_pairs={{0,6},{2,0},{4,2},{6,4},{1,70},{3,64},{5,66},{7,68},{8,134},{10,12... | collective-permute-start | bytes 98312 | tf_op jit(solution)/shard_map/ppermute | solution.py:220
  102.6 3.3 %collective-permute-done.32.refs_2_ = bf16[128,128]{1,0:T(8,128)(2,1)S(1)} collective-permute-done((bf16[128,128]{1,0:T(8,128)(2,1)S(1)}, bf16[128,128]{1,0:T(8,128)(2,1)S(1)}, u32[]{:S(2)}, u32[]{:S(2)}) %collective-permute-start.32) | collective-permute-done | bytes 32800 | tf_op jit(solution)/shard_map/ppermute | solution.py:220
  105.9 1.2 %shard_map.100 = (f32[64,512]{1,0:T(8,128)}, bf16[64,512]{1,0:T(8,128)(2,1)}) custom-call(s32[4]{0:T(128)S(1)} %pad_add_fusion.at_ref, bf16[128,128]{1,0:T(8,128)(2,1)S(1)} %collective-permute-done.30.refs_0_, bf16[128,128]{1,0:T(8,128)(2,1)S(1)} %collective-permute-done.31.refs_1_, bf16[128,128]{1,0:T(8,128)(2,1)S(1)} %collective-permute-done.32.refs_2_, ...), custom_call_target="tpu_custom_call" | custom-call | bytes 327696 | tf_op jit(solution)/shard_map/pallas_call | solution.py:23
  (48 shorter events, 0.8 us)
Async XLA Ops:
  0.6 12.8 %copy-start.2 = (bf16[64,512]{1,0:T(8,128)(2,1)S(1)}, bf16[64,512]{1,0:T(8,128)(2,1)}, u32[]{:S(2)}) copy-start(bf16[64,512]{1,0:T(8,128)(2,1)} %q_ref.2) | copy-start | bytes 196612
  0.6 12.8 %copy-start = (bf16[64,512]{1,0:T(8,128)(2,1)S(1)}, bf16[64,512]{1,0:T(8,128)(2,1)}, u32[]{:S(2)}) copy-start(bf16[64,512]{1,0:T(8,128)(2,1)} %k_ref.2) | copy-start | bytes 196612
  0.7 12.8 %copy-start.1 = (bf16[64,512]{1,0:T(8,128)(2,1)S(1)}, bf16[64,512]{1,0:T(8,128)(2,1)}, u32[]{:S(2)}) copy-start(bf16[64,512]{1,0:T(8,128)(2,1)} %v_ref.2) | copy-start | bytes 196612
  3.0 40.7 %all-to-all-start = ((bf16[16,208,128]{2,1,0:T(8,128)(2,1)}), bf16[16,208,128]{2,1,0:T(8,128)(2,1)S(1)}, u32[]{:S(2)}, u32[]{:S(2)}) async-start(bf16[16,208,128]{2,1,0:T(8,128)(2,1)} %shard_map.88), calls=%async_computation | async-start | bytes 1703936 | tf_op jit(solution)/shard_map/all_to_all | solution.py:254
  14.2 14.6 %collective-permute-start = (bf16[192,128]{1,0:T(8,128)(2,1)S(1)}, bf16[192,128]{1,0:T(8,128)(2,1)S(1)}, u32[]{:S(2)}, u32[]{:S(2)}) collective-permute-start(bf16[192,128]{1,0:T(8,128)(2,1)S(1)} %get-tuple-element.39), channel_id=1, source_target_pairs={{0,0},{2,2},{4,4},{6,6},{1,64},{3,66},{5,68},{7,70},{8,128},{10,13... | collective-permute-start | bytes 147464 | tf_op jit(solution)/shard_map/ppermute | solution.py:220
  18.8 22.4 %collective-permute-start.1 = (bf16[192,128]{1,0:T(8,128)(2,1)S(1)}, bf16[192,128]{1,0:T(8,128)(2,1)S(1)}, u32[]{:S(2)}, u32[]{:S(2)}) collective-permute-start(bf16[192,128]{1,0:T(8,128)(2,1)S(1)} %get-tuple-element.40), channel_id=1, source_target_pairs={{0,2},{2,4},{4,6},{6,0},{1,66},{3,68},{5,70},{7,64},{8,130},{10,13... | collective-permute-start | bytes 147464 | tf_op jit(solution)/shard_map/ppermute | solution.py:220
  20.7 22.5 %collective-permute-start.2 = (bf16[192,128]{1,0:T(8,128)(2,1)S(1)}, bf16[192,128]{1,0:T(8,128)(2,1)S(1)}, u32[]{:S(2)}, u32[]{:S(2)}) collective-permute-start(bf16[192,128]{1,0:T(8,128)(2,1)S(1)} %get-tuple-element.41), channel_id=1, source_target_pairs={{0,4},{2,6},{4,0},{6,2},{1,68},{3,70},{5,64},{7,66},{8,132},{10,13... | collective-permute-start | bytes 147464 | tf_op jit(solution)/shard_map/ppermute | solution.py:220
  25.7 17.4 %collective-permute-start.3 = (bf16[192,128]{1,0:T(8,128)(2,1)S(1)}, bf16[192,128]{1,0:T(8,128)(2,1)S(1)}, u32[]{:S(2)}, u32[]{:S(2)}) collective-permute-start(bf16[192,128]{1,0:T(8,128)(2,1)S(1)} %get-tuple-element.42), channel_id=1, source_target_pairs={{0,6},{2,0},{4,2},{6,4},{1,70},{3,64},{5,66},{7,68},{8,134},{10,12... | collective-permute-start | bytes 147464 | tf_op jit(solution)/shard_map/ppermute | solution.py:220
  44.0 13.1 %collective-permute-start.5 = (bf16[1024,128]{1,0:T(8,128)(2,1)S(1)}, bf16[1024,128]{1,0:T(8,128)(2,1)S(1)}, u32[]{:S(2)}, u32[]{:S(2)}) collective-permute-start(bf16[1024,128]{1,0:T(8,128)(2,1)S(1)} %get-tuple-element.47.k_ref), channel_id=1, source_target_pairs={{0,16},{16,32},{32,48},{48,0},{1,17},{17,33},{33,49},{49,1},{2,18}... | collective-permute-start | bytes 786440 | tf_op jit(solution)/shard_map/ppermute | solution.py:224
  45.5 9.1 %collective-permute-start.6 = (bf16[1024,128]{1,0:T(8,128)(2,1)S(1)}, bf16[1024,128]{1,0:T(8,128)(2,1)S(1)}, u32[]{:S(2)}, u32[]{:S(2)}) collective-permute-start(bf16[1024,128]{1,0:T(8,128)(2,1)S(1)} %get-tuple-element.47.k_ref), channel_id=1, source_target_pairs={{0,48},{16,0},{32,16},{48,32},{1,49},{17,1},{33,17},{49,33},{2,50}... | collective-permute-start | bytes 786440 | tf_op jit(solution)/shard_map/ppermute | solution.py:224
  48.5 10.2 %collective-permute-start.7 = (bf16[1024,128]{1,0:T(8,128)(2,1)S(1)}, bf16[1024,128]{1,0:T(8,128)(2,1)S(1)}, u32[]{:S(2)}, u32[]{:S(2)}) collective-permute-start(bf16[1024,128]{1,0:T(8,128)(2,1)S(1)} %get-tuple-element.58.refs_9_), channel_id=1, source_target_pairs={{0,16},{16,32},{32,48},{48,0},{1,17},{17,33},{33,49},{49,1},{2,18}... | collective-permute-start | bytes 786440 | tf_op jit(solution)/shard_map/ppermute | solution.py:224
  48.8 10.5 %collective-permute-start.8 = (bf16[1024,128]{1,0:T(8,128)(2,1)S(1)}, bf16[1024,128]{1,0:T(8,128)(2,1)S(1)}, u32[]{:S(2)}, u32[]{:S(2)}) collective-permute-start(bf16[1024,128]{1,0:T(8,128)(2,1)S(1)} %get-tuple-element.58.refs_9_), channel_id=1, source_target_pairs={{0,48},{16,0},{32,16},{48,32},{1,49},{17,1},{33,17},{49,33},{2,50}... | collective-permute-start | bytes 786440 | tf_op jit(solution)/shard_map/ppermute | solution.py:224
  54.6 11.9 %collective-permute-start.10 = (bf16[512,128]{1,0:T(8,128)(2,1)S(1)}, bf16[512,128]{1,0:T(8,128)(2,1)S(1)}, u32[]{:S(2)}, u32[]{:S(2)}) collective-permute-start(bf16[512,128]{1,0:T(8,128)(2,1)S(1)} %slice.17), channel_id=1, source_target_pairs={{0,48},{16,0},{32,16},{48,32},{1,49},{17,1},{33,17},{49,33},{2,50}... | collective-permute-start | bytes 393224 | tf_op jit(solution)/shard_map/ppermute | solution.py:224
  57.1 9.5 %collective-permute-start.9 = (bf16[512,128]{1,0:T(8,128)(2,1)S(1)}, bf16[512,128]{1,0:T(8,128)(2,1)S(1)}, u32[]{:S(2)}, u32[]{:S(2)}) collective-permute-start(bf16[512,128]{1,0:T(8,128)(2,1)S(1)} %slice.16), channel_id=1, source_target_pairs={{0,16},{16,32},{32,48},{48,0},{1,17},{17,33},{33,49},{49,1},{2,18}... | collective-permute-start | bytes 393224 | tf_op jit(solution)/shard_map/ppermute | solution.py:224
  57.1 14.0 %collective-permute-start.4 = (bf16[512,128]{1,0:T(8,128)(2,1)S(1)}, bf16[512,128]{1,0:T(8,128)(2,1)S(1)}, u32[]{:S(2)}, u32[]{:S(2)}) collective-permute-start(bf16[512,128]{1,0:T(8,128)(2,1)S(1)} %get-tuple-element.44.kv_ref.bv_ref), channel_id=1, source_target_pairs={{0,128},{128,0},{1,129},{129,1},{2,130},{130,2},{3,131},{131,3},{4... | collective-permute-start | bytes 393224 | tf_op jit(solution)/shard_map/ppermute | solution.py:228
  58.7 9.1 %collective-permute-start.11 = (bf16[512,128]{1,0:T(8,128)(2,1)S(1)}, bf16[512,128]{1,0:T(8,128)(2,1)S(1)}, u32[]{:S(2)}, u32[]{:S(2)}) collective-permute-start(bf16[512,128]{1,0:T(8,128)(2,1)S(1)} %slice.18), channel_id=1, source_target_pairs={{0,16},{16,32},{32,48},{48,0},{1,17},{17,33},{33,49},{49,1},{2,18}... | collective-permute-start | bytes 393224 | tf_op jit(solution)/shard_map/ppermute | solution.py:224
  59.4 8.4 %collective-permute-start.12 = (bf16[512,128]{1,0:T(8,128)(2,1)S(1)}, bf16[512,128]{1,0:T(8,128)(2,1)S(1)}, u32[]{:S(2)}, u32[]{:S(2)}) collective-permute-start(bf16[512,128]{1,0:T(8,128)(2,1)S(1)} %slice.19), channel_id=1, source_target_pairs={{0,48},{16,0},{32,16},{48,32},{1,49},{17,1},{33,17},{49,33},{2,50}... | collective-permute-start | bytes 393224 | tf_op jit(solution)/shard_map/ppermute | solution.py:224
  69.2 5.2 %collective-permute-start.20 = (bf16[512,128]{1,0:T(8,128)(2,1)S(1)}, bf16[512,128]{1,0:T(8,128)(2,1)S(1)}, u32[]{:S(2)}, u32[]{:S(2)}) collective-permute-start(bf16[512,128]{1,0:T(8,128)(2,1)S(1)} %get-tuple-element.65.after_ref), channel_id=1, source_target_pairs={{0,64},{64,0},{1,65},{65,1},{2,66},{66,2},{3,67},{67,3},{4,68},{68... | collective-permute-start | bytes 393224 | tf_op jit(solution)/shard_map/ppermute | solution.py:228
  69.3 6.5 %collective-permute-start.21 = (bf16[512,128]{1,0:T(8,128)(2,1)S(1)}, bf16[512,128]{1,0:T(8,128)(2,1)S(1)}, u32[]{:S(2)}, u32[]{:S(2)}) collective-permute-start(bf16[512,128]{1,0:T(8,128)(2,1)S(1)} %get-tuple-element.69), channel_id=1, source_target_pairs={{0,128},{128,0},{1,129},{129,1},{2,130},{130,2},{3,131},{131,3},{4... | collective-permute-start | bytes 393224 | tf_op jit(solution)/shard_map/ppermute | solution.py:228
  70.0 7.6 %collective-permute-start.22 = (bf16[512,128]{1,0:T(8,128)(2,1)S(1)}, bf16[512,128]{1,0:T(8,128)(2,1)S(1)}, u32[]{:S(2)}, u32[]{:S(2)}) collective-permute-start(bf16[512,128]{1,0:T(8,128)(2,1)S(1)} %get-tuple-element.65.after_ref), channel_id=1, source_target_pairs={{0,192},{64,128},{128,64},{192,0},{1,193},{65,129},{129,65},{193,1... | collective-permute-start | bytes 393224 | tf_op jit(solution)/shard_map/ppermute | solution.py:315
  71.2 9.9 %collective-permute-start.13 = (bf16[512,128]{1,0:T(8,128)(2,1)S(1)}, bf16[512,128]{1,0:T(8,128)(2,1)S(1)}, u32[]{:S(2)}, u32[]{:S(2)}) collective-permute-start(bf16[512,128]{1,0:T(8,128)(2,1)S(1)} %shard_map.96.refs_0_), channel_id=1, source_target_pairs={{0,16},{16,32},{32,48},{48,0},{1,17},{17,33},{33,49},{49,1},{2,18}... | collective-permute-start | bytes 393224 | tf_op jit(solution)/shard_map/ppermute | solution.py:224
  71.3 10.5 %collective-permute-start.14 = (bf16[512,128]{1,0:T(8,128)(2,1)S(1)}, bf16[512,128]{1,0:T(8,128)(2,1)S(1)}, u32[]{:S(2)}, u32[]{:S(2)}) collective-permute-start(bf16[512,128]{1,0:T(8,128)(2,1)S(1)} %shard_map.96.refs_0_), channel_id=1, source_target_pairs={{0,32},{16,48},{32,0},{48,16},{1,33},{17,49},{33,1},{49,17},{2,34}... | collective-permute-start | bytes 393224 | tf_op jit(solution)/shard_map/ppermute | solution.py:224
  74.4 8.0 %collective-permute-start.15 = (bf16[512,128]{1,0:T(8,128)(2,1)S(1)}, bf16[512,128]{1,0:T(8,128)(2,1)S(1)}, u32[]{:S(2)}, u32[]{:S(2)}) collective-permute-start(bf16[512,128]{1,0:T(8,128)(2,1)S(1)} %shard_map.96.refs_0_), channel_id=1, source_target_pairs={{0,48},{16,0},{32,16},{48,32},{1,49},{17,1},{33,17},{49,33},{2,50}... | collective-permute-start | bytes 393224 | tf_op jit(solution)/shard_map/ppermute | solution.py:224
  75.8 6.5 %collective-permute-start.16 = (bf16[512,128]{1,0:T(8,128)(2,1)S(1)}, bf16[512,128]{1,0:T(8,128)(2,1)S(1)}, u32[]{:S(2)}, u32[]{:S(2)}) collective-permute-start(bf16[512,128]{1,0:T(8,128)(2,1)S(1)} %shard_map.96.refs_0_), channel_id=1, source_target_pairs={{0,64},{64,0},{1,65},{65,1},{2,66},{66,2},{3,67},{67,3},{4,68},{68... | collective-permute-start | bytes 393224 | tf_op jit(solution)/shard_map/ppermute | solution.py:228
  77.6 10.1 %collective-permute-start.23 = (bf16[512,128]{1,0:T(8,128)(2,1)S(1)}, bf16[512,128]{1,0:T(8,128)(2,1)S(1)}, u32[]{:S(2)}, u32[]{:S(2)}) collective-permute-start(bf16[512,128]{1,0:T(8,128)(2,1)S(1)} %get-tuple-element.71.refs_0_), channel_id=1, source_target_pairs={{0,16},{16,32},{32,48},{48,0},{1,17},{17,33},{33,49},{49,1},{2,18}... | collective-permute-start | bytes 393224 | tf_op jit(solution)/shard_map/ppermute | solution.py:224
  81.1 6.7 %collective-permute-start.24 = (bf16[512,128]{1,0:T(8,128)(2,1)S(1)}, bf16[512,128]{1,0:T(8,128)(2,1)S(1)}, u32[]{:S(2)}, u32[]{:S(2)}) collective-permute-start(bf16[512,128]{1,0:T(8,128)(2,1)S(1)} %get-tuple-element.71.refs_0_), channel_id=1, source_target_pairs={{0,32},{16,48},{32,0},{48,16},{1,33},{17,49},{33,1},{49,17},{2,34}... | collective-permute-start | bytes 393224 | tf_op jit(solution)/shard_map/ppermute | solution.py:224
  81.8 6.5 %collective-permute-start.25 = (bf16[512,128]{1,0:T(8,128)(2,1)S(1)}, bf16[512,128]{1,0:T(8,128)(2,1)S(1)}, u32[]{:S(2)}, u32[]{:S(2)}) collective-permute-start(bf16[512,128]{1,0:T(8,128)(2,1)S(1)} %get-tuple-element.71.refs_0_), channel_id=1, source_target_pairs={{0,48},{16,0},{32,16},{48,32},{1,49},{17,1},{33,17},{49,33},{2,50}... | collective-permute-start | bytes 393224 | tf_op jit(solution)/shard_map/ppermute | solution.py:224
  82.4 6.0 %collective-permute-start.17 = (bf16[512,128]{1,0:T(8,128)(2,1)S(1)}, bf16[512,128]{1,0:T(8,128)(2,1)S(1)}, u32[]{:S(2)}, u32[]{:S(2)}) collective-permute-start(bf16[512,128]{1,0:T(8,128)(2,1)S(1)} %collective-permute-done.13.refs_1_), channel_id=1, source_target_pairs={{0,64},{64,0},{1,65},{65,1},{2,66},{66,2},{3,67},{67,3},{4,68},{68... | collective-permute-start | bytes 393224 | tf_op jit(solution)/shard_map/ppermute | solution.py:228
  82.4 6.4 %collective-permute-start.18 = (bf16[512,128]{1,0:T(8,128)(2,1)S(1)}, bf16[512,128]{1,0:T(8,128)(2,1)S(1)}, u32[]{:S(2)}, u32[]{:S(2)}) collective-permute-start(bf16[512,128]{1,0:T(8,128)(2,1)S(1)} %collective-permute-done.14.refs_2_), channel_id=1, source_target_pairs={{0,64},{64,0},{1,65},{65,1},{2,66},{66,2},{3,67},{67,3},{4,68},{68... | collective-permute-start | bytes 393224 | tf_op jit(solution)/shard_map/ppermute | solution.py:228
  87.7 1.3 %collective-permute-start.19 = (bf16[512,128]{1,0:T(8,128)(2,1)S(1)}, bf16[512,128]{1,0:T(8,128)(2,1)S(1)}, u32[]{:S(2)}, u32[]{:S(2)}) collective-permute-start(bf16[512,128]{1,0:T(8,128)(2,1)S(1)} %collective-permute-done.15.refs_3_), channel_id=1, source_target_pairs={{0,64},{64,0},{1,65},{65,1},{2,66},{66,2},{3,67},{67,3},{4,68},{68... | collective-permute-start | bytes 393224 | tf_op jit(solution)/shard_map/ppermute | solution.py:228
  87.7 2.7 %collective-permute-start.26 = (bf16[512,128]{1,0:T(8,128)(2,1)S(1)}, bf16[512,128]{1,0:T(8,128)(2,1)S(1)}, u32[]{:S(2)}, u32[]{:S(2)}) collective-permute-start(bf16[512,128]{1,0:T(8,128)(2,1)S(1)} %get-tuple-element.71.refs_0_), channel_id=1, source_target_pairs={{0,64},{64,0},{1,65},{65,1},{2,66},{66,2},{3,67},{67,3},{4,68},{68... | collective-permute-start | bytes 393224 | tf_op jit(solution)/shard_map/ppermute | solution.py:228
  88.3 2.2 %collective-permute-start.27 = (bf16[512,128]{1,0:T(8,128)(2,1)S(1)}, bf16[512,128]{1,0:T(8,128)(2,1)S(1)}, u32[]{:S(2)}, u32[]{:S(2)}) collective-permute-start(bf16[512,128]{1,0:T(8,128)(2,1)S(1)} %collective-permute-done.23.refs_1_), channel_id=1, source_target_pairs={{0,64},{64,0},{1,65},{65,1},{2,66},{66,2},{3,67},{67,3},{4,68},{68... | collective-permute-start | bytes 393224 | tf_op jit(solution)/shard_map/ppermute | solution.py:228
  88.3 2.1 %collective-permute-start.28 = (bf16[512,128]{1,0:T(8,128)(2,1)S(1)}, bf16[512,128]{1,0:T(8,128)(2,1)S(1)}, u32[]{:S(2)}, u32[]{:S(2)}) collective-permute-start(bf16[512,128]{1,0:T(8,128)(2,1)S(1)} %collective-permute-done.24.refs_2_), channel_id=1, source_target_pairs={{0,64},{64,0},{1,65},{65,1},{2,66},{66,2},{3,67},{67,3},{4,68},{68... | collective-permute-start | bytes 393224 | tf_op jit(solution)/shard_map/ppermute | solution.py:228
  88.8 1.7 %collective-permute-start.29 = (bf16[512,128]{1,0:T(8,128)(2,1)S(1)}, bf16[512,128]{1,0:T(8,128)(2,1)S(1)}, u32[]{:S(2)}, u32[]{:S(2)}) collective-permute-start(bf16[512,128]{1,0:T(8,128)(2,1)S(1)} %collective-permute-done.25.refs_3_), channel_id=1, source_target_pairs={{0,64},{64,0},{1,65},{65,1},{2,66},{66,2},{3,67},{67,3},{4,68},{68... | collective-permute-start | bytes 393224 | tf_op jit(solution)/shard_map/ppermute | solution.py:228
  91.8 10.8 %collective-permute-start.30 = (bf16[128,128]{1,0:T(8,128)(2,1)S(1)}, bf16[128,128]{1,0:T(8,128)(2,1)S(1)}, u32[]{:S(2)}, u32[]{:S(2)}) collective-permute-start(bf16[128,128]{1,0:T(8,128)(2,1)S(1)} %get-tuple-element.72), channel_id=1, source_target_pairs={{0,0},{2,2},{4,4},{6,6},{1,64},{3,66},{5,68},{7,70},{8,128},{10,13... | collective-permute-start | bytes 98312 | tf_op jit(solution)/shard_map/ppermute | solution.py:220
  94.7 7.9 %collective-permute-start.31 = (bf16[128,128]{1,0:T(8,128)(2,1)S(1)}, bf16[128,128]{1,0:T(8,128)(2,1)S(1)}, u32[]{:S(2)}, u32[]{:S(2)}) collective-permute-start(bf16[128,128]{1,0:T(8,128)(2,1)S(1)} %get-tuple-element.73), channel_id=1, source_target_pairs={{0,2},{2,4},{4,6},{6,0},{1,66},{3,68},{5,70},{7,64},{8,130},{10,13... | collective-permute-start | bytes 98312 | tf_op jit(solution)/shard_map/ppermute | solution.py:220
  97.1 8.8 %collective-permute-start.32 = (bf16[128,128]{1,0:T(8,128)(2,1)S(1)}, bf16[128,128]{1,0:T(8,128)(2,1)S(1)}, u32[]{:S(2)}, u32[]{:S(2)}) collective-permute-start(bf16[128,128]{1,0:T(8,128)(2,1)S(1)} %get-tuple-element.74), channel_id=1, source_target_pairs={{0,4},{2,6},{4,0},{6,2},{1,68},{3,70},{5,64},{7,66},{8,132},{10,13... | collective-permute-start | bytes 98312 | tf_op jit(solution)/shard_map/ppermute | solution.py:220
  98.7 7.2 %collective-permute-start.33 = (bf16[128,128]{1,0:T(8,128)(2,1)S(1)}, bf16[128,128]{1,0:T(8,128)(2,1)S(1)}, u32[]{:S(2)}, u32[]{:S(2)}) collective-permute-start(bf16[128,128]{1,0:T(8,128)(2,1)S(1)} %get-tuple-element.75), channel_id=1, source_target_pairs={{0,6},{2,0},{4,2},{6,4},{1,70},{3,64},{5,66},{7,68},{8,134},{10,12... | collective-permute-start | bytes 98312 | tf_op jit(solution)/shard_map/ppermute | solution.py:220
